TPU v7x, 1024 devices: a whole 4x4x32 slice. The times are simulated.
1024 devices in a mesh: space: 128 (over y, z), chan: 8 (over x, core).
Axes of the slice: x: 4, y: 4, z: 32, core: 2. Of those that a mesh axis runs over, the one named last changes fastest.
Arguments:
- volume: bfloat16 [256, 128, 8, 128], P('chan', 'space'), may hold values from -6 to 6
- kernel: bfloat16 [3, 3, 3, 256, 256], replicated, may hold values from -0.078125 to 0.078125
- cotangent: bfloat16 [256, 128, 8, 128], P('chan', 'space'), may hold values from -6 to 6
Outputs:
- output: bfloat16 [256, 128, 8, 128], P('chan', 'space')
- input_grad: bfloat16 [256, 128, 8, 128], P('chan', 'space')
- weight_grad: float32 [3, 3, 3, 256, 256], P(None, None, None, 'chan')
All inputs are finite; a program needn't handle non-finite values.
Results may differ from a plain program's by a relative error of at most 0.001.
Values may be sent and summed in bfloat16 or wider, within the bound.
No kernel may reach another device: no remote copies, remote signals or barrier semaphores. Data moves between devices by JAX's collectives and lax.ppermute only.
A program may use at most 64 MiB of HBM per device.

v0:
```python
import math

import jax
import jax.numpy as jnp
from jax import lax
from jax.sharding import PartitionSpec as P


def extended(block, sides, width):
    for axis, dim in sides:
        count = lax.axis_size(axis)
        forward = [(i, i + 1) for i in range(count - 1)]
        backward = [(target, source) for source, target in forward]
        low = lax.ppermute(
            lax.slice_in_dim(block, block.shape[dim] - width, None, axis=dim), axis, forward
        )
        high = lax.ppermute(lax.slice_in_dim(block, 0, width, axis=dim), axis, backward)
        block = jnp.concatenate([low, block, high], axis=dim)
    return block


def pad_sides(slab):
    return jnp.pad(slab, ((0, 0), (0, 0), (1, 1), (1, 1)))


def window(padded, along_x, along_y, along_z, extent):
    planes, height, breadth = extent
    portion = padded[
        :, along_x : along_x + planes, along_y : along_y + height, along_z : along_z + breadth
    ]
    return portion.reshape(portion.shape[0], -1)


def tap_offsets():
    return [
        (along_x, along_y, along_z)
        for along_x in range(3)
        for along_y in range(3)
        for along_z in range(3)
    ]


def stacked_windows(widened, extent, mirror):
    pieces = []
    for along_x, along_y, along_z in tap_offsets():
        if mirror:
            pieces.append(window(widened, 2 - along_x, 2 - along_y, 2 - along_z, extent))
        else:
            pieces.append(window(widened, along_x, along_y, along_z, extent))
    return jnp.concatenate(pieces, axis=0)


def local(volume, kernel, cotangent):
    own_count = volume.shape[0]
    extent = volume.shape[1:]
    cell_count = extent[0] * extent[1] * extent[2]
    channels = kernel.shape[3]
    member = lax.axis_index("chan")
    factor = 1.0 / math.sqrt(lax.axis_size("space") * cell_count)
    vol_halo = extended(volume, (("space", 1),), 1)
    vol_stack = stacked_windows(pad_sides(vol_halo), extent, False)
    own_inputs = lax.dynamic_slice_in_dim(kernel, member * own_count, own_count, 3)
    own_rows = own_inputs.reshape(27 * own_count, channels)
    columns = own_rows
    forward = lax.psum_scatter(
        lax.dot_general(
            columns, vol_stack, (((0,), (0,)), ((), ())), preferred_element_type=jnp.float32
        ),
        "chan",
        scatter_dimension=0,
        tiled=True,
    )
    output = forward.astype(jnp.bfloat16).reshape(volume.shape)
    cot_halo = extended(cotangent, (("space", 1),), 1)
    portion = lax.all_gather(cot_halo, "chan", axis=0, tiled=True)
    amount = portion.shape[0]
    widened_piece = pad_sides(portion)
    centre = window(widened_piece, 1, 1, 1, extent)
    mirrored = stacked_windows(widened_piece, extent, True).reshape(27, amount, cell_count)
    columns = own_inputs.reshape(27, own_count, amount)
    back_sum = lax.dot_general(
        columns, mirrored, (((0, 2), (0, 1)), ((), ())), preferred_element_type=jnp.float32
    )
    update = lax.dot_general(
        vol_stack, centre, (((1,), (1,)), ((), ())), preferred_element_type=jnp.float32
    )
    update = update.reshape(3, 3, 3, own_count, amount)
    grad_sum = update
    back_sum, grad_sum = (back_sum, grad_sum)
    input_grad = back_sum.astype(jnp.bfloat16).reshape(volume.shape)
    weight_grad = lax.psum(grad_sum, "space") * factor
    return (output, input_grad, weight_grad)


def solution(mesh):
    return jax.shard_map(
        local,
        mesh=mesh,
        in_specs=(P("chan", "space", None, None), P(), P("chan", "space", None, None)),
        out_specs=(
            P("chan", "space", None, None),
            P("chan", "space", None, None),
            P(None, None, None, "chan", None),
        ),
        check_vma=False,
    )
```

profile of v0, /device:TPU:4, one launch (start us, length us, event | category | flops | bytes accessed | tf_op | source)
XLA Modules:
  0.0 653.1 jit_solution(2444731907815945008)
XLA Ops:
  7.2 4.7 collective-permute-start
  11.9 1.3 collective-permute-start.1
  13.5 4.9 collective-permute-done.1
  18.4 1.5 select_maximum_fusion
  22.6 1.2 copy-done.1
  23.8 1.7 fusion.12
  25.6 3.2 collective-permute-start.2
  28.9 1.3 collective-permute-start.3
  30.2 0.9 collective-permute-done.2
  31.1 5.2 collective-permute-done.3
  36.3 1.6 pad_maximum_fusion
  37.9 39.0 %reduce-scatter.2.cloned.1.call-done = f32[32,1024]{1,0:T(8,128)} async-done(((f32[256,1024]{1,0:T(8,128)}), f32[32,1024]{1,0:T(8,128)}) %reduce-scatter.2.cloned.1.call-update) | async-done | bytes 131088 | tf_op jit(solution)/shard_map/reduce_scatter | solution.py:65
  76.9 0.9 convert_bitcast_fusion
  78.5 47.2 %all-gather.2.cloned.1.call-done = bf16[256,3,8,128]{3,2,1,0:T(8,128)(2,1)} async-done(((bf16[32,3,8,128]{3,2,1,0:T(8,128)(2,1)}), bf16[256,3,8,128]{3,2,1,0:T(8,128)(2,1)}) %all-gather.2.cloned.1.call-update) | async-done | bytes 1572880 | tf_op jit(solution)/shard_map/all_gather | solution.py:75
  125.7 4.9 pad_slice_fusion.1
  130.6 0.9 bitcast_dynamic-update-slice_fusion.26
  131.5 2.1 reshape.246
  133.6 3.1 fusion.8
  136.8 6.6 %pad_slice_fusion = (bf16[256,1,8,128]{3,2,1,0:T(8,128)(2,1)S(1)}, bf16[256,1,8,128]{3,2,1,0:T(8,128)(2,1)S(1)}, bf16[256,1,8,128]{3,2,1,0:T(8,128)(2,1)S(1)}, b...) fusion(bf16[256,3,8,128]{3,2,1,0:T(8,128)(2,1)} %all-gather.2.c, ...), kind=kLoop, calls=%fused_computation | loop fusion | bytes 11534336 | tf_op jit(solution)/shard_map/slice | solution.py:28
  143.4 0.9 bitcast_dynamic-update-slice_fusion.25
  144.3 0.9 bitcast_dynamic-update-slice_fusion.24
  145.2 0.9 bitcast_dynamic-update-slice_fusion.23
  146.1 0.9 bitcast_dynamic-update-slice_fusion.22
  146.9 0.9 bitcast_dynamic-update-slice_fusion.21
  147.8 0.9 bitcast_dynamic-update-slice_fusion.20
  148.7 0.9 bitcast_dynamic-update-slice_fusion.19
  149.5 0.9 bitcast_dynamic-update-slice_fusion.18
  150.4 0.9 bitcast_dynamic-update-slice_fusion.17
  151.3 0.9 bitcast_dynamic-update-slice_fusion.16
  152.2 0.9 bitcast_dynamic-update-slice_fusion.15
  153.1 0.9 bitcast_dynamic-update-slice_fusion.14
  153.9 0.9 bitcast_dynamic-update-slice_fusion.13
  154.8 0.9 bitcast_dynamic-update-slice_fusion.12
  155.7 0.9 bitcast_dynamic-update-slice_fusion.11
  156.6 0.9 bitcast_dynamic-update-slice_fusion.10
  157.5 0.9 bitcast_dynamic-update-slice_fusion.9
  158.4 0.9 bitcast_dynamic-update-slice_fusion.8
  159.3 0.9 bitcast_dynamic-update-slice_fusion.7
  160.2 0.9 bitcast_dynamic-update-slice_fusion.6
  161.1 0.9 bitcast_dynamic-update-slice_fusion.5
  161.9 0.9 bitcast_dynamic-update-slice_fusion.4
  162.8 0.9 bitcast_dynamic-update-slice_fusion.3
  163.7 0.9 bitcast_dynamic-update-slice_fusion.2
  164.6 0.9 bitcast_dynamic-update-slice_fusion.1
  165.5 0.9 bitcast_dynamic-update-slice_fusion
  166.4 7.6 %fusion.4 = bf16[4,8,8,128]{3,1,2,0:T(8,128)(2,1)S(1)} fusion(bf16[27,32,256]{2,1,0:T(8,128)(2,1)S(1)} %bitcast.253, bf16[27,256,1024]{2,1,0:T(8,128)(2,1)} %bitcast.250), kind=kOutput, calls=%fused_computation.33 | convolution fusion | flops 453017600 | bytes 14663680 | tf_op jit(solution)/shard_map/dot_general | solution.py:81
  174.6 469.7 %all-reduce.4.cloned.1.call-done = f32[3,3,3,32,256]{4,3,2,1,0:T(8,128)} async-done(((f32[3,3,3,32,256]{4,3,2,1,0:T(8,128)}), f32[3,3,3,32,256]{4,3,2,1,0:T(8,128)}) %all-reduce.4.cloned.1.call-update) | async-done | bytes 884752 | tf_op jit(solution)/shard_map/psum | solution.py:91
  644.3 2.2 broadcast_multiply_fusion
  (62 shorter events, 4.3 us)
Async XLA Ops:
  7.2 6.1 copy-start
  7.2 69.7 %reduce-scatter.2.cloned.1.call-start = ((), (), s32[]{:S(2)}) async-start(), calls=%async_computation.1 | async-start | bytes 1179648 | tf_op jit(solution)/shard_map/reduce_scatter | solution.py:65
  7.2 6.3 collective-permute-start
  11.9 6.5 collective-permute-start.1
  13.2 8.3 %copy-start.11 = (bf16[32,1,8,128]{3,2,1,0:T(8,128)(2,1)S(1)}, bf16[32,1,8,128]{3,2,1,0:T(8,128)(2,1)}, u32[]{:S(2)}) copy-start(bf16[32,1,8,128]{3,2,1,0:T(8,128)(2,1)} %param.3) | copy-start | bytes 196612
  13.3 9.3 %copy-start.2 = (bf16[3,3,3,32,256]{4,3,2,1,0:T(8,128)(2,1)}, bf16[3,3,3,32,256]{4,3,2,1,0:T(8,128)(2,1)S(1)}, u32[]{:S(2)}) copy-start(bf16[3,3,3,32,256]{4,3,2,1,0:T(8,128)(2,1)S(1)} %constant_dynamic-slice_fusion) | copy-start | bytes 1327108
  22.6 1.2 copy-start.1
  25.6 100.1 %all-gather.2.cloned.1.call-start = ((), (), s32[]{:S(2)}) async-start(), calls=%async_computation.2 | async-start | bytes 1769472 | tf_op jit(solution)/shard_map/all_gather | solution.py:75
  25.6 5.4 collective-permute-start.2
  28.9 7.4 %collective-permute-start.3 = (bf16[32,1,8,128]{3,2,1,0:T(8,128)(2,1)}, bf16[32,1,8,128]{3,2,1,0:T(8,128)(2,1)S(1)}, u32[]{:S(2)}, u32[]{:S(2)}) collective-permute-start(bf16[32,1,8,128]{3,2,1,0:T(8,128)(2,1)} %param.5), channel_id=1, source_target_pairs={{8,0},{16,8},{24,16},{32,24},{40,32},{48,40},{56,48},{64,56},{72,6... | collective-permute-start | bytes 196616 | tf_op jit(solution)/shard_map/ppermute | solution.py:17
  37.8 606.5 %all-reduce.4.cloned.1.call-start = ((), (), s32[]{:S(2)}) async-start(), calls=%async_computation.3 | async-start | bytes 1769472 | tf_op jit(solution)/shard_map/psum | solution.py:91
  136.8 9.3 %copy-start.10 = (bf16[256,1,8,128]{3,2,1,0:T(8,128)(2,1)S(1)}, bf16[256,1,8,128]{3,2,1,0:T(8,128)(2,1)}, u32[]{:S(2)}) copy-start(bf16[256,1,8,128]{3,2,1,0:T(8,128)(2,1)} %get-tuple-element.34) | copy-start | bytes 1572868
  143.4 10.5 %copy-start.4 = (bf16[256,1,8,128]{3,2,1,0:T(8,128)(2,1)S(1)}, bf16[256,1,8,128]{3,2,1,0:T(8,128)(2,1)}, u32[]{:S(2)}) copy-start(bf16[256,1,8,128]{3,2,1,0:T(8,128)(2,1)} %get-tuple-element.33) | copy-start | bytes 1572868
  150.4 10.7 %copy-start.9 = (bf16[256,1,8,128]{3,2,1,0:T(8,128)(2,1)S(1)}, bf16[256,1,8,128]{3,2,1,0:T(8,128)(2,1)}, u32[]{:S(2)}) copy-start(bf16[256,1,8,128]{3,2,1,0:T(8,128)(2,1)} %get-tuple-element.29) | copy-start | bytes 1572868
  151.3 10.7 %copy-start.8 = (bf16[256,1,8,128]{3,2,1,0:T(8,128)(2,1)S(1)}, bf16[256,1,8,128]{3,2,1,0:T(8,128)(2,1)}, u32[]{:S(2)}) copy-start(bf16[256,1,8,128]{3,2,1,0:T(8,128)(2,1)} %get-tuple-element.32) | copy-start | bytes 1572868
  152.2 10.7 %copy-start.7 = (bf16[256,1,8,128]{3,2,1,0:T(8,128)(2,1)S(1)}, bf16[256,1,8,128]{3,2,1,0:T(8,128)(2,1)}, u32[]{:S(2)}) copy-start(bf16[256,1,8,128]{3,2,1,0:T(8,128)(2,1)} %get-tuple-element.30) | copy-start | bytes 1572868
  153.1 10.6 %copy-start.6 = (bf16[256,1,8,128]{3,2,1,0:T(8,128)(2,1)S(1)}, bf16[256,1,8,128]{3,2,1,0:T(8,128)(2,1)}, u32[]{:S(2)}) copy-start(bf16[256,1,8,128]{3,2,1,0:T(8,128)(2,1)} %get-tuple-element.31) | copy-start | bytes 1572868
  153.9 10.7 %copy-start.5 = (bf16[256,1,8,128]{3,2,1,0:T(8,128)(2,1)S(1)}, bf16[256,1,8,128]{3,2,1,0:T(8,128)(2,1)}, u32[]{:S(2)}) copy-start(bf16[256,1,8,128]{3,2,1,0:T(8,128)(2,1)} %get-tuple-element.28) | copy-start | bytes 1572868
  155.7 10.7 %copy-start.3 = (bf16[3,3,3,32,256]{4,3,2,1,0:T(8,128)(2,1)S(1)}, bf16[3,3,3,32,256]{4,3,2,1,0:T(8,128)(2,1)}, u32[]{:S(2)}) copy-start(bf16[3,3,3,32,256]{4,3,2,1,0:T(8,128)(2,1)} %copy-done.2) | copy-start | bytes 1327108
Sparse Core Ops, SparseCore 0:
  25.7 51.1 reduce-scatter.1
  80.2 45.4 all-gather.1
  136.9 507.3 all-reduce.3
where the time goes:
time: 654 us; the launch traced here: 653 us
  waiting for transfers between devices  567 us (87%)
  local copies, waits for them, and re-layouts  42.6 us (7%)
  between operations  14.1 us (2%)
  matrix products  12.4 us (2%)
  starting transfers between devices  10.6 us (2%)
    psum x1, waiting for transfers between devices, local(): weight_grad = lax.psum(grad_sum, 'space') * factor  470 us
    all_gather x1, waiting for transfers between devices, local(): portion = lax.all_gather(cot_halo, 'chan', axis=0, tiled=True)  47.2 us
    reduce_scatter x1, waiting for transfers between devices, local(): lax.psum_scatter(lax.dot_general(columns, vol_stack, (((0,), (0,)), ((),...  39 us
    unnamed x78, local copies, waits for them, and re-layouts  27.4 us
  transfers between devices with their start and end apart: 7, of which 7 were waited for; matrix products, arithmetic and copies ran while one was open for 6% of the time, Pallas kernels for 0%

commit v1 on v0

v1 whole, which is shorter than its diff:
```python
import math

import jax
import jax.numpy as jnp
from jax import lax
from jax.experimental import pallas as pl
from jax.experimental.pallas import tpu as pltpu
from jax.sharding import PartitionSpec as P

TAPS = 27
Y_CHIPS = 4
NEAR = 4


def groups_of(count):
    length = count // Y_CHIPS
    far = length // NEAR
    along_y = [[y * length + z for y in range(Y_CHIPS)] for z in range(length)]
    near_z = [
        [y * length + hop * NEAR + k for k in range(NEAR)]
        for y in range(Y_CHIPS)
        for hop in range(far)
    ]
    far_z = [
        [y * length + hop * NEAR + k for hop in range(far)]
        for y in range(Y_CHIPS)
        for k in range(NEAR)
    ]
    return along_y, near_z, far_z


def exchange(pieces, axis, groups=None):
    return lax.all_to_all(pieces, axis, 0, 0, tiled=True, axis_index_groups=groups)


def reduce_pieces(total, axis, groups):
    count = len(groups[0])
    pieces = total.reshape(count, total.shape[0] // count, total.shape[1])
    return jnp.sum(exchange(pieces, axis, groups), axis=0)


def gather_pieces(piece, axis, groups, count):
    whole = exchange(jnp.broadcast_to(piece[None], (count,) + piece.shape), axis, groups)
    return whole.reshape((count * piece.shape[0],) + piece.shape[1:])


def shift_lanes(value, offset, lanes):
    if offset == 0:
        return value
    at = lax.broadcasted_iota(jnp.int32, value.shape, 1)
    if offset < 0:
        return jnp.where(at == 0, 0.0, pltpu.roll(value, 1, 1))
    return jnp.where(at == lanes - 1, 0.0, pltpu.roll(value, lanes - 1, 1))


def weight_kernel(factor, height, breadth, low, own, high, cot, out, stack):
    count = own.shape[0]
    edge = jnp.zeros((9 * count, breadth), stack.dtype)
    stack[:, :breadth] = edge
    stack[:, (height + 1) * breadth :] = edge
    for a, plane in enumerate((low, own, high)):
        for q in range(height):
            row = plane[:, q * breadth : (q + 1) * breadth].astype(jnp.float32)
            for c in range(3):
                at = (a * 3 + c) * count
                stack[at : at + count, (q + 1) * breadth : (q + 2) * breadth] = shift_lanes(
                    row, c - 1, breadth
                ).astype(stack.dtype)
    cells = height * breadth
    group = 3 * count
    for b in range(3):
        part = lax.dot_general(
            stack[:, b * breadth : b * breadth + cells],
            cot[...],
            (((1,), (1,)), ((), ())),
            preferred_element_type=jnp.float32,
        )
        for a in range(3):
            out[(a * 3 + b) * group : (a * 3 + b + 1) * group, :] = (
                part[a * group : (a + 1) * group] * factor
            )
    rest = out.shape[0] - 9 * group
    out[9 * group :, :] = jnp.zeros((rest, out.shape[1]), out.dtype)


def weight_terms(low, own, high, cot, factor, height, breadth):
    count = own.shape[0]
    channels = cot.shape[0]
    rows = (TAPS + 1) * count

    def body(*refs):
        weight_kernel(factor, height, breadth, *refs)

    return pl.pallas_call(
        body,
        out_shape=jax.ShapeDtypeStruct((rows, channels), jnp.float32),
        in_specs=[pl.BlockSpec(memory_space=pltpu.VMEM)] * 4,
        out_specs=pl.BlockSpec(memory_space=pltpu.VMEM),
        scratch_shapes=[pltpu.VMEM((9 * count, (height + 2) * breadth), jnp.bfloat16)],
        compiler_params=pltpu.CompilerParams(vmem_limit_bytes=32 * 1024 * 1024),
        cost_estimate=pl.CostEstimate(
            flops=2 * rows * channels * height * breadth,
            bytes_accessed=4 * rows * channels,
            transcendentals=0,
        ),
    )(low, own, high, cot)


def conv_kernel(mirror, height, breadth, weights, field, out):
    count = out.shape[1]
    for a in range(3):
        part = lax.dot_general(
            weights[a],
            field[...],
            (((1,), (0,)), ((), ())),
            preferred_element_type=jnp.float32,
        )
        for q in range(height):
            total = None
            for c in range(3):
                column = None
                for b in range(3):
                    source = q + (1 - b if mirror else b - 1)
                    if 0 <= source < height:
                        at = (b * 3 + c) * count
                        term = part[at : at + count, source * breadth : (source + 1) * breadth]
                        column = term if column is None else column + term
                moved = shift_lanes(column, 1 - c if mirror else c - 1, breadth)
                total = moved if total is None else total + moved
            out[a, :, q * breadth : (q + 1) * breadth] = total


def conv_terms(weights, field, mirror, height, breadth):
    count = weights.shape[1] // 9
    channels, cells = field.shape

    def body(*refs):
        conv_kernel(mirror, height, breadth, *refs)

    return pl.pallas_call(
        body,
        out_shape=jax.ShapeDtypeStruct((3, count, cells), jnp.float32),
        in_specs=[pl.BlockSpec(memory_space=pltpu.VMEM)] * 2,
        out_specs=pl.BlockSpec(memory_space=pltpu.VMEM),
        compiler_params=pltpu.CompilerParams(vmem_limit_bytes=32 * 1024 * 1024),
        cost_estimate=pl.CostEstimate(
            flops=2 * weights.size * cells,
            bytes_accessed=2 * weights.size + 12 * count * cells,
            transcendentals=0,
        ),
    )(weights, field)


def local(volume, kernel, cotangent):
    count, planes, height, breadth = volume.shape
    cells = height * breadth
    channels = kernel.shape[3]
    slabs = lax.axis_size("space")
    parts = lax.axis_size("chan")
    member = lax.axis_index("chan")
    factor = 1.0 / math.sqrt(slabs * planes * cells)
    along_y, near_z, far_z = groups_of(slabs)
    up = [(i, i + 1) for i in range(slabs - 1)]
    down = [(i + 1, i) for i in range(slabs - 1)]

    vol = volume.reshape(count, cells)
    cot = cotangent.reshape(count, cells)
    vol_low = lax.ppermute(vol, "space", up)
    vol_high = lax.ppermute(vol, "space", down)
    cot_all = exchange(jnp.broadcast_to(cot[None], (parts, count, cells)), "chan")
    cot_all = cot_all.reshape(channels, cells)

    terms = weight_terms(vol_low, vol, vol_high, cot_all, factor, height, breadth)
    terms = reduce_pieces(terms, "space", along_y)
    terms = reduce_pieces(terms, "space", near_z)
    terms = reduce_pieces(terms, "space", far_z)
    total = gather_pieces(terms, "space", far_z, len(far_z[0]))
    total = gather_pieces(total, "space", near_z, len(near_z[0]))
    total = gather_pieces(total, "space", along_y, len(along_y[0]))
    weight_grad = total[: TAPS * count].reshape(3, 3, 3, count, channels)

    vol_all = lax.all_gather(vol, "chan", axis=0, tiled=True)
    fore = lax.dynamic_slice_in_dim(kernel, member * count, count, 4)
    fore = jnp.swapaxes(fore, 3, 4).reshape(3, 9 * count, channels)
    back = lax.dynamic_slice_in_dim(kernel, member * count, count, 3)
    back = back.reshape(3, 9 * count, channels)
    back_terms = conv_terms(back, cot_all, True, height, breadth)
    fore_terms = conv_terms(fore, vol_all, False, height, breadth)

    def finish(own, from_low, from_high):
        whole = own + lax.ppermute(from_low, "space", up) + lax.ppermute(from_high, "space", down)
        return whole.astype(volume.dtype).reshape(volume.shape)

    input_grad = finish(back_terms[1], back_terms[2], back_terms[0])
    output = finish(fore_terms[1], fore_terms[0], fore_terms[2])
    return (output, input_grad, weight_grad)


def solution(mesh):
    return jax.shard_map(
        local,
        mesh=mesh,
        in_specs=(P("chan", "space", None, None), P(), P("chan", "space", None, None)),
        out_specs=(
            P("chan", "space", None, None),
            P("chan", "space", None, None),
            P(None, None, None, "chan", None),
        ),
        check_vma=False,
    )
```

time: 654 us -> 198 us (0.30)
  the two profiles are of different devices: /device:TPU:4 before, /device:TPU:1 now
where the time goes in v1:
time: 198 us; the launch traced here: 196 us
  blocking collectives  110 us (56%)
  starting transfers between devices  39.8 us (20%)
  local copies, waits for them, and re-layouts  24.7 us (12%)
  waiting for transfers between devices  10.4 us (5%)
  other arithmetic  6.37 us (3%)
  Pallas kernels  4.17 us (2%)
    all_to_all x4, blocking collectives, exchange(): lax.all_to_all(pieces, axis, 0, 0, tiled=True, axis_index_groups=groups)  89.1 us
    all_to_all x3, starting transfers between devices, exchange(): lax.all_to_all(pieces, axis, 0, 0, tiled=True, axis_index_groups=groups)  26.4 us
    all_gather x1, blocking collectives, local(): vol_all = lax.all_gather(vol, 'chan', axis=0, tiled=True)  20.9 us
    unnamed x24, local copies, waits for them, and re-layouts  9.3 us
    ppermute x2, starting transfers between devices, finish(): lax.ppermute(from_low, 'space', up)  8.23 us
    broadcast_in_dim x4, local copies, waits for them, and re-layouts, gather_pieces(): jnp.broadcast_to(piece[None], (count,) + piece.shape)  4.93 us
    all_to_all x3, waiting for transfers between devices, exchange(): lax.all_to_all(pieces, axis, 0, 0, tiled=True, axis_index_groups=groups)  4.75 us
    reduce_sum x3, other arithmetic, reduce_pieces(): return jnp.sum(exchange(pieces, axis, groups), axis=0)  4.38 us
  transfers between devices with their start and end apart: 9, of which 4 were waited for; matrix products, arithmetic and copies ran while one was open for 6% of the time, Pallas kernels for 1%

profile of v1, /device:TPU:1, one launch (start us, length us, event | category | flops | bytes accessed | tf_op | source)
XLA Modules:
  0.0 196.3 jit_solution(2667650449527991372)
XLA Ops:
  0.6 1.0 copy.21
  1.6 0.9 broadcast_in_dim.28
  2.5 18.2 %all-to-all-start = ((bf16[8,32,1024]{2,1,0:T(8,128)(2,1)}), bf16[8,32,1024]{2,1,0:T(8,128)(2,1)}, u32[]{:S(2)}, u32[]{:S(2)}) async-start(bf16[8,32,1024]{2,1,0:T(8,128)(2,1)} %broadcast_in_dim.28), calls=%async_computation | async-start | bytes 1048576 | tf_op jit(solution)/shard_map/all_to_all | solution.py:33
  20.7 0.8 copy.22
  21.5 1.3 collective-permute-start.4
  22.8 1.3 collective-permute-start.5
  24.1 0.6 copy-done.4
  24.8 0.6 copy-done.6
  25.4 3.0 %collective-permute-done.5.refs_2_ = bf16[32,1024]{1,0:T(8,128)(2,1)S(1)} collective-permute-done((bf16[32,1024]{1,0:T(8,128)(2,1)S(1)}, bf16[32,1024]{1,0:T(8,128)(2,1)S(1)}, u32[]{:S(2)}, u32[]{:S(2)}) %collective-permute-start.5) | collective-permute-done | bytes 65568 | tf_op jit(solution)/shard_map/ppermute | solution.py:169
  28.4 0.6 copy-done.8
  29.0 1.3 all-to-all-done
  30.3 0.8 copy-done.5
  31.1 0.8 copy-done.7
  32.0 0.8 copy-done.9
  32.8 1.7 shard_map.60
  34.5 18.1 %all_to_all.35 = f32[4,224,256]{2,1,0:T(8,128)} all-to-all(f32[4,224,256]{2,1,0:T(8,128)S(1)} %bitcast.62), channel_id=1, replica_groups={{0,256,512,768},{8,264,520,776},{16,272,528,784},{24,280,536,792},{32,2..., dimensions={0} | all-to-all | bytes 1835008 | tf_op jit(solution)/shard_map/all_to_all | solution.py:33
  52.6 1.9 reduce_sum.27
  54.6 9.8 %all_to_all.36 = f32[4,56,256]{2,1,0:T(8,128)} all-to-all(f32[4,56,256]{2,1,0:T(8,128)} %bitcast.69), channel_id=1, replica_groups={{0,8,16,24},{32,40,48,56},{64,72,80,88},{96,104,112,120},{128,136,144,1..., dimensions={0} | all-to-all | bytes 458752 | tf_op jit(solution)/shard_map/all_to_all | solution.py:33
  64.4 1.6 reduce_sum.28
  66.0 1.5 reshape.51
  67.4 35.8 %all_to_all.37 = f32[8,7,256]{2,1,0:T(8,128)} all-to-all(f32[8,7,256]{2,1,0:T(8,128)} %reshape.51), channel_id=1, replica_groups={{0,32,64,96,128,160,192,224},{8,40,72,104,136,168,200,232},{16,48,80,11..., dimensions={0} | all-to-all | bytes 114688 | tf_op jit(solution)/shard_map/all_to_all | solution.py:33
  103.3 0.9 reduce_sum.29
  104.2 25.3 %all_to_all.38 = f32[8,7,256]{2,1,0:T(8,128)} all-to-all(f32[8,7,256]{2,1,0:T(8,128)S(1)} %broadcast_in_dim.29), channel_id=1, replica_groups={{0,32,64,96,128,160,192,224},{8,40,72,104,136,168,200,232},{16,48,80,11..., dimensions={0} | all-to-all | bytes 114688 | tf_op jit(solution)/shard_map/all_to_all | solution.py:33
  129.5 1.5 broadcast_in_dim.30
  130.9 1.5 broadcast_in_dim.31
  132.5 4.0 %all-to-all-start.5 = ((f32[4,56,256]{2,1,0:T(8,128)}), f32[4,56,256]{2,1,0:T(8,128)}, u32[]{:S(2)}, u32[]{:S(2)}) async-start(f32[4,56,256]{2,1,0:T(8,128)} %broadcast_in_dim.31), calls=%async_computation.5 | async-start | bytes 458752 | tf_op jit(solution)/shard_map/all_to_all | solution.py:33
  136.5 1.8 dynamic-slice_bitcast_fusion
  138.3 2.4 %copy.12 = bf16[3,3,3,32,256]{4,3,2,1,0:T(8,128)(2,1)} copy(bf16[3,3,3,32,256]{3,4,2,1,0:T(8,128)(2,1)} %dynamic-slice_bitcast_fusion) | data formatting | bytes 884736 | tf_op jit(solution)/shard_map/transpose | solution.py:184
  140.7 20.9 %all_gather.3.refs_1_ = bf16[256,1024]{1,0:T(8,128)(2,1)S(1)} all-gather(bf16[32,1024]{1,0:T(8,128)(2,1)} %bitcast.67), channel_id=1, replica_groups=mesh['space'=128,'chan'=8] {'chan'}, dimensions={0}, use_global_device_ids=true | all-gather | bytes 589824 | tf_op jit(solution)/shard_map/all_gather | solution.py:182
  161.6 1.0 copy-done.1
  162.6 0.7 shard_map.58
  163.4 0.8 slice_bitcast_fusion.4
  164.2 4.2 %collective-permute-start = (f32[32,1024]{1,0:T(8,128)}, f32[32,1024]{1,0:T(8,128)}, u32[]{:S(2)}, u32[]{:S(2)}) collective-permute-start(f32[32,1024]{1,0:T(8,128)} %get-tuple-element.14), channel_id=1, source_target_pairs={{0,8},{8,16},{16,24},{24,32},{32,40},{40,48},{48,56},{56,64},{64,7... | collective-permute-start | bytes 393224 | tf_op jit(solution)/shard_map/ppermute | solution.py:191
  168.4 1.3 collective-permute-start.1
  169.7 1.7 shard_map.59
  171.5 0.8 copy-done.3
  172.2 1.9 broadcast_in_dim.33
  174.2 4.2 %all-to-all-start.6 = ((f32[4,224,256]{2,1,0:T(8,128)}), f32[4,224,256]{2,1,0:T(8,128)}, u32[]{:S(2)}, u32[]{:S(2)}) async-start(f32[4,224,256]{2,1,0:T(8,128)} %broadcast_in_dim.33), calls=%async_computation.6 | async-start | bytes 1835008 | tf_op jit(solution)/shard_map/all_to_all | solution.py:33
  178.4 1.0 slice_bitcast_fusion.1
  179.4 4.0 %collective-permute-start.2 = (f32[32,1024]{1,0:T(8,128)S(1)}, f32[32,1024]{1,0:T(8,128)S(1)}, u32[]{:S(2)}, u32[]{:S(2)}) collective-permute-start(f32[32,1024]{1,0:T(8,128)S(1)} %get-tuple-element.12), channel_id=1, source_target_pairs={{0,8},{8,16},{16,24},{24,32},{32,40},{40,48},{48,56},{56,64},{64,7... | collective-permute-start | bytes 393224 | tf_op jit(solution)/shard_map/ppermute | solution.py:191
  183.4 1.3 collective-permute-start.3
  184.7 1.1 fusion.6
  185.8 0.6 copy.16
  186.4 2.7 %collective-permute-done.3 = f32[32,1024]{1,0:T(8,128)S(1)} collective-permute-done((f32[32,1024]{1,0:T(8,128)S(1)}, f32[32,1024]{1,0:T(8,128)S(1)}, u32[]{:S(2)}, u32[]{:S(2)}) %collective-permute-start.3) | collective-permute-done | bytes 131104 | tf_op jit(solution)/shard_map/ppermute | solution.py:191
  189.1 0.9 fusion.7
  190.0 0.6 copy.18
  190.7 3.5 %all-to-all-done.6 = f32[4,224,256]{2,1,0:T(8,128)} async-done(((f32[4,224,256]{2,1,0:T(8,128)}), f32[4,224,256]{2,1,0:T(8,128)}, u32[]{:S(2)}, u32[]{:S(2)}) %all-to-all-start.6) | async-done | bytes 917536 | tf_op jit(solution)/shard_map/all_to_all | solution.py:33
  194.1 2.1 %slice.34 = f32[864,256]{1,0:T(8,128)} slice(f32[896,256]{1,0:T(8,128)} %bitcast.15), slice={[0:864], [0:256]} | slice | bytes 1769472 | tf_op jit(solution)/shard_map/slice | solution.py:180
  (19 shorter events, 0.1 us)
Async XLA Ops:
  0.6 135.9 %copy-start = (bf16[3,3,3,256,256]{4,3,2,1,0:T(8,128)(2,1)S(1)}, bf16[3,3,3,256,256]{4,3,2,1,0:T(8,128)(2,1)}, u32[]{:S(2)}) copy-start(bf16[3,3,3,256,256]{4,3,2,1,0:T(8,128)(2,1)} %param.4) | copy-start | bytes 10616836
  2.5 27.8 %all-to-all-start = ((bf16[8,32,1024]{2,1,0:T(8,128)(2,1)}), bf16[8,32,1024]{2,1,0:T(8,128)(2,1)}, u32[]{:S(2)}, u32[]{:S(2)}) async-start(bf16[8,32,1024]{2,1,0:T(8,128)(2,1)} %broadcast_in_dim.28), calls=%async_computation | async-start | bytes 1048576 | tf_op jit(solution)/shard_map/all_to_all | solution.py:33
  21.5 3.2 %collective-permute-start.4 = (bf16[32,1024]{1,0:T(8,128)(2,1)S(1)}, bf16[32,1024]{1,0:T(8,128)(2,1)S(1)}, u32[]{:S(2)}, u32[]{:S(2)}) collective-permute-start(bf16[32,1024]{1,0:T(8,128)(2,1)S(1)} %bitcast.65), channel_id=1, source_target_pairs={{0,8},{8,16},{16,24},{24,32},{32,40},{40,48},{48,56},{56,64},{64,7... | collective-permute-start | bytes 196616 | tf_op jit(solution)/shard_map/ppermute | solution.py:168
  22.8 5.5 %collective-permute-start.5 = (bf16[32,1024]{1,0:T(8,128)(2,1)S(1)}, bf16[32,1024]{1,0:T(8,128)(2,1)S(1)}, u32[]{:S(2)}, u32[]{:S(2)}) collective-permute-start(bf16[32,1024]{1,0:T(8,128)(2,1)S(1)} %bitcast.66), channel_id=1, source_target_pairs={{8,0},{16,8},{24,16},{32,24},{40,32},{48,40},{56,48},{64,56},{72,6... | collective-permute-start | bytes 196616 | tf_op jit(solution)/shard_map/ppermute | solution.py:169
  24.1 0.6 copy-start.4
  24.8 0.6 copy-start.6
  28.4 0.6 copy-start.8
  30.3 0.8 copy-start.5
  31.1 0.8 copy-start.7
  32.0 0.8 copy-start.9
  132.5 39.8 %all-to-all-start.5 = ((f32[4,56,256]{2,1,0:T(8,128)}), f32[4,56,256]{2,1,0:T(8,128)}, u32[]{:S(2)}, u32[]{:S(2)}) async-start(f32[4,56,256]{2,1,0:T(8,128)} %broadcast_in_dim.31), calls=%async_computation.5 | async-start | bytes 458752 | tf_op jit(solution)/shard_map/all_to_all | solution.py:33
  161.6 1.0 copy-start.1
  163.4 5.0 %copy-start.2 = (f32[3,32,1024]{2,1,0:T(8,128)}, f32[3,32,1024]{2,1,0:T(8,128)S(1)}, u32[]{:S(2)}) copy-start(f32[3,32,1024]{2,1,0:T(8,128)S(1)} %shard_map.58) | copy-start | bytes 1179652
  164.2 20.5 %collective-permute-start = (f32[32,1024]{1,0:T(8,128)}, f32[32,1024]{1,0:T(8,128)}, u32[]{:S(2)}, u32[]{:S(2)}) collective-permute-start(f32[32,1024]{1,0:T(8,128)} %get-tuple-element.14), channel_id=1, source_target_pairs={{0,8},{8,16},{16,24},{24,32},{32,40},{40,48},{48,56},{56,64},{64,7... | collective-permute-start | bytes 393224 | tf_op jit(solution)/shard_map/ppermute | solution.py:191
  168.4 16.3 %collective-permute-start.1 = (f32[32,1024]{1,0:T(8,128)}, f32[32,1024]{1,0:T(8,128)}, u32[]{:S(2)}, u32[]{:S(2)}) collective-permute-start(f32[32,1024]{1,0:T(8,128)} %get-tuple-element.15), channel_id=1, source_target_pairs={{8,0},{16,8},{24,16},{32,24},{40,32},{48,40},{56,48},{64,56},{72,6... | collective-permute-start | bytes 393224 | tf_op jit(solution)/shard_map/ppermute | solution.py:191
  171.5 0.8 copy-start.3
  174.2 20.0 %all-to-all-start.6 = ((f32[4,224,256]{2,1,0:T(8,128)}), f32[4,224,256]{2,1,0:T(8,128)}, u32[]{:S(2)}, u32[]{:S(2)}) async-start(f32[4,224,256]{2,1,0:T(8,128)} %broadcast_in_dim.33), calls=%async_computation.6 | async-start | bytes 1835008 | tf_op jit(solution)/shard_map/all_to_all | solution.py:33
  179.4 7.0 %collective-permute-start.2 = (f32[32,1024]{1,0:T(8,128)S(1)}, f32[32,1024]{1,0:T(8,128)S(1)}, u32[]{:S(2)}, u32[]{:S(2)}) collective-permute-start(f32[32,1024]{1,0:T(8,128)S(1)} %get-tuple-element.12), channel_id=1, source_target_pairs={{0,8},{8,16},{16,24},{24,32},{32,40},{40,48},{48,56},{56,64},{64,7... | collective-permute-start | bytes 393224 | tf_op jit(solution)/shard_map/ppermute | solution.py:191
  183.4 5.7 %collective-permute-start.3 = (f32[32,1024]{1,0:T(8,128)S(1)}, f32[32,1024]{1,0:T(8,128)S(1)}, u32[]{:S(2)}, u32[]{:S(2)}) collective-permute-start(f32[32,1024]{1,0:T(8,128)S(1)} %get-tuple-element.13), channel_id=1, source_target_pairs={{8,0},{16,8},{24,16},{32,24},{40,32},{48,40},{56,48},{64,56},{72,6... | collective-permute-start | bytes 393224 | tf_op jit(solution)/shard_map/ppermute | solution.py:191

commit v2 on v1

--- a/solution.py
+++ b/solution.py
@@ -21,27 +21,25 @@
         for y in range(Y_CHIPS)
         for hop in range(far)
     ]
+    block = [
+        [y * length + hop * NEAR + k for y in range(Y_CHIPS) for k in range(NEAR)]
+        for hop in range(far)
+    ]
     far_z = [
         [y * length + hop * NEAR + k for hop in range(far)]
         for y in range(Y_CHIPS)
         for k in range(NEAR)
     ]
-    return along_y, near_z, far_z
+    return along_y, near_z, block, far_z
 
 
 def exchange(pieces, axis, groups=None):
     return lax.all_to_all(pieces, axis, 0, 0, tiled=True, axis_index_groups=groups)
 
 
-def reduce_pieces(total, axis, groups):
-    count = len(groups[0])
-    pieces = total.reshape(count, total.shape[0] // count, total.shape[1])
-    return jnp.sum(exchange(pieces, axis, groups), axis=0)
-
-
-def gather_pieces(piece, axis, groups, count):
-    whole = exchange(jnp.broadcast_to(piece[None], (count,) + piece.shape), axis, groups)
-    return whole.reshape((count * piece.shape[0],) + piece.shape[1:])
+def whole_of(block, parts):
+    copies = jnp.broadcast_to(block[None], (parts,) + block.shape)
+    return exchange(copies, "chan").reshape((parts * block.shape[0],) + block.shape[1:])
 
 
 def shift_lanes(value, offset, lanes):
@@ -94,10 +92,10 @@
     return pl.pallas_call(
         body,
         out_shape=jax.ShapeDtypeStruct((rows, channels), jnp.float32),
-        in_specs=[pl.BlockSpec(memory_space=pltpu.VMEM)] * 4,
-        out_specs=pl.BlockSpec(memory_space=pltpu.VMEM),
+        in_specs=[pl.BlockSpec()] * 4,
+        out_specs=pl.BlockSpec(),
         scratch_shapes=[pltpu.VMEM((9 * count, (height + 2) * breadth), jnp.bfloat16)],
-        compiler_params=pltpu.CompilerParams(vmem_limit_bytes=32 * 1024 * 1024),
+        compiler_params=pltpu.CompilerParams(vmem_limit_bytes=10 * 1024 * 1024),
         cost_estimate=pl.CostEstimate(
             flops=2 * rows * channels * height * breadth,
             bytes_accessed=4 * rows * channels,
@@ -106,8 +104,9 @@
     )(low, own, high, cot)
 
 
-def conv_kernel(mirror, height, breadth, weights, field, out):
-    count = out.shape[1]
+def conv_terms(weights, field, mirror, height, breadth, own, up, down):
+    count = weights.shape[1] // 9
+    places = (down, own, up) if mirror else (up, own, down)
     for a in range(3):
         part = lax.dot_general(
             weights[a],
@@ -127,28 +126,35 @@
                         column = term if column is None else column + term
                 moved = shift_lanes(column, 1 - c if mirror else c - 1, breadth)
                 total = moved if total is None else total + moved
-            out[a, :, q * breadth : (q + 1) * breadth] = total
-
-
-def conv_terms(weights, field, mirror, height, breadth):
-    count = weights.shape[1] // 9
-    channels, cells = field.shape
-
-    def body(*refs):
-        conv_kernel(mirror, height, breadth, *refs)
-
+            places[a][:, q * breadth : (q + 1) * breadth] = total
+
+
+def plane_terms(fore, vol, back, cot, height, breadth):
+    count = fore.shape[1] // 9
+    cells = vol.shape[1]
+
+    def body(fore_ref, vol_ref, back_ref, cot_ref, own, up, down):
+        halves = [pl.ds(0, count), pl.ds(count, count)]
+        conv_terms(
+            fore_ref, vol_ref, False, height, breadth, *(r.at[halves[0]] for r in (own, up, down))
+        )
+        conv_terms(
+            back_ref, cot_ref, True, height, breadth, *(r.at[halves[1]] for r in (own, up, down))
+        )
+
+    shape = jax.ShapeDtypeStruct((2 * count, cells), jnp.float32)
     return pl.pallas_call(
         body,
-        out_shape=jax.ShapeDtypeStruct((3, count, cells), jnp.float32),
-        in_specs=[pl.BlockSpec(memory_space=pltpu.VMEM)] * 2,
-        out_specs=pl.BlockSpec(memory_space=pltpu.VMEM),
-        compiler_params=pltpu.CompilerParams(vmem_limit_bytes=32 * 1024 * 1024),
+        out_shape=(shape, shape, shape),
+        in_specs=[pl.BlockSpec()] * 4,
+        out_specs=(pl.BlockSpec(),) * 3,
+        compiler_params=pltpu.CompilerParams(vmem_limit_bytes=10 * 1024 * 1024),
         cost_estimate=pl.CostEstimate(
-            flops=2 * weights.size * cells,
-            bytes_accessed=2 * weights.size + 12 * count * cells,
+            flops=4 * fore.size * cells,
+            bytes_accessed=4 * fore.size + 24 * count * cells,
             transcendentals=0,
         ),
-    )(weights, field)
+    )(fore, vol, back, cot)
 
 
 def local(volume, kernel, cotangent):
@@ -159,41 +165,32 @@
     parts = lax.axis_size("chan")
     member = lax.axis_index("chan")
     factor = 1.0 / math.sqrt(slabs * planes * cells)
-    along_y, near_z, far_z = groups_of(slabs)
+    along_y, near_z, block, far_z = groups_of(slabs)
     up = [(i, i + 1) for i in range(slabs - 1)]
     down = [(i + 1, i) for i in range(slabs - 1)]
 
+    cot = cotangent.reshape(count, cells)
+    cot_all = whole_of(cot, parts)
     vol = volume.reshape(count, cells)
-    cot = cotangent.reshape(count, cells)
     vol_low = lax.ppermute(vol, "space", up)
     vol_high = lax.ppermute(vol, "space", down)
-    cot_all = exchange(jnp.broadcast_to(cot[None], (parts, count, cells)), "chan")
-    cot_all = cot_all.reshape(channels, cells)
+    vol_all = lax.all_gather(vol, "chan", axis=0, tiled=True)
 
     terms = weight_terms(vol_low, vol, vol_high, cot_all, factor, height, breadth)
-    terms = reduce_pieces(terms, "space", along_y)
-    terms = reduce_pieces(terms, "space", near_z)
-    terms = reduce_pieces(terms, "space", far_z)
-    total = gather_pieces(terms, "space", far_z, len(far_z[0]))
-    total = gather_pieces(total, "space", near_z, len(near_z[0]))
-    total = gather_pieces(total, "space", along_y, len(along_y[0]))
+    pieces = exchange(terms.reshape(len(block[0]), -1, channels), "space", block)
+    total = lax.psum(jnp.sum(pieces, axis=0), "space", axis_index_groups=far_z)
+    total = lax.all_gather(total, "space", axis=0, tiled=True, axis_index_groups=near_z)
+    total = lax.all_gather(total, "space", axis=0, tiled=True, axis_index_groups=along_y)
     weight_grad = total[: TAPS * count].reshape(3, 3, 3, count, channels)
 
-    vol_all = lax.all_gather(vol, "chan", axis=0, tiled=True)
     fore = lax.dynamic_slice_in_dim(kernel, member * count, count, 4)
     fore = jnp.swapaxes(fore, 3, 4).reshape(3, 9 * count, channels)
     back = lax.dynamic_slice_in_dim(kernel, member * count, count, 3)
     back = back.reshape(3, 9 * count, channels)
-    back_terms = conv_terms(back, cot_all, True, height, breadth)
-    fore_terms = conv_terms(fore, vol_all, False, height, breadth)
-
-    def finish(own, from_low, from_high):
-        whole = own + lax.ppermute(from_low, "space", up) + lax.ppermute(from_high, "space", down)
-        return whole.astype(volume.dtype).reshape(volume.shape)
-
-    input_grad = finish(back_terms[1], back_terms[2], back_terms[0])
-    output = finish(fore_terms[1], fore_terms[0], fore_terms[2])
-    return (output, input_grad, weight_grad)
+    own, upper, lower = plane_terms(fore, vol_all, back, cot_all, height, breadth)
+    whole = own + lax.ppermute(upper, "space", up) + lax.ppermute(lower, "space", down)
+    whole = whole.astype(volume.dtype).reshape((2,) + volume.shape)
+    return (whole[0], whole[1], weight_grad)
 
 
 def solution(mesh):

time: 198 us -> 158 us (0.80)
  the two profiles are of different devices: /device:TPU:1 before, /device:TPU:2 now
where the time goes in v2:
time: 158 us; the launch traced here: 157 us
  blocking collectives  90.5 us (57%)
  starting transfers between devices  32.1 us (20%)
  local copies, waits for them, and re-layouts  15.6 us (10%)
  waiting for transfers between devices  12.6 us (8%)
  Pallas kernels  3.94 us (2%)
  other arithmetic  1.9 us (1%)
    psum x1, blocking collectives, local(): total = lax.psum(jnp.sum(pieces, axis=0), 'space', axis_index_groups=far_z)  49 us
    all_to_all x2, starting transfers between devices, exchange(): lax.all_to_all(pieces, axis, 0, 0, tiled=True, axis_index_groups=groups)  24.4 us
    all_gather x1, blocking collectives, local(): lax.all_gather(total, 'space', axis=0, tiled=True, axis_index_groups=near_z)  14.3 us
    all_gather x1, blocking collectives, local(): lax.all_gather(total, 'space', axis=0, tiled=True, axis_index_groups=alon...  13.8 us
    all_gather x1, blocking collectives, local(): vol_all = lax.all_gather(vol, 'chan', axis=0, tiled=True)  13.3 us
    unnamed x23, local copies, waits for them, and re-layouts  9.48 us
    ppermute x1, waiting for transfers between devices, local(): lax.ppermute(upper, 'space', up)  4.74 us
    transpose x2, local copies, waits for them, and re-layouts, local(): fore = jnp.swapaxes(fore, 3, 4).reshape(3, 9 * count, channels)  4.23 us
  transfers between devices with their start and end apart: 6, of which 4 were waited for; matrix products, arithmetic and copies ran while one was open for 4% of the time, Pallas kernels for 1%

profile of v2, /device:TPU:2, one launch (start us, length us, event | category | flops | bytes accessed | tf_op | source)
XLA Modules:
  0.0 157.3 jit_solution(2123410900325402020)
XLA Ops:
  0.6 0.0 copy-start
  0.6 1.0 copy.15
  1.6 0.9 broadcast_in_dim.8
  2.5 17.2 %all-to-all-start = ((bf16[8,32,1024]{2,1,0:T(8,128)(2,1)}), bf16[8,32,1024]{2,1,0:T(8,128)(2,1)}, u32[]{:S(2)}, u32[]{:S(2)}) async-start(bf16[8,32,1024]{2,1,0:T(8,128)(2,1)} %broadcast_in_dim.8), calls=%async_computation | async-start | bytes 1048576 | tf_op jit(solution)/shard_map/all_to_all | solution.py:37
  19.7 0.8 copy.16
  20.6 1.3 collective-permute-start.2
  21.9 1.3 collective-permute-start.3
  23.2 0.0 copy-start.3
  23.2 0.6 copy-done.3
  23.8 0.0 collective-permute-done.2.refs_0_
  23.8 0.0 copy-start.5
  23.8 0.6 copy-done.5
  24.4 3.6 %collective-permute-done.3.refs_2_ = bf16[32,1024]{1,0:T(8,128)(2,1)S(1)} collective-permute-done((bf16[32,1024]{1,0:T(8,128)(2,1)S(1)}, bf16[32,1024]{1,0:T(8,128)(2,1)S(1)}, u32[]{:S(2)}, u32[]{:S(2)}) %collective-permute-start.3) | collective-permute-done | bytes 65568 | tf_op jit(solution)/shard_map/ppermute | solution.py:176
  28.0 0.0 copy-start.7
  28.0 0.6 copy-done.7
  28.7 0.1 all-to-all-done
  28.7 0.0 copy-start.4
  28.7 0.8 copy-done.4
  29.6 0.0 copy-start.6
  29.6 0.8 copy-done.6
  30.4 0.0 copy-start.8
  30.4 0.8 copy-done.8
  31.3 1.7 %shard_map.59 = f32[896,256]{1,0:T(8,128)S(1)} custom-call(bf16[32,1024]{1,0:T(8,128)(2,1)S(1)} %copy-done.6, bf16[32,1024]{1,0:T(8,128)(2,1)S(1)} %bitcast.37, bf16[32,1024]{1,0:T(8,128)(2,1)S(1)} %copy-done.8, bf16[256,1024]{1,0:T(8,128)(2,1)} %bitcast.3.cot_ref.refs_3_), custom_call_target="tpu_custom_call" | custom-call | flops 469762048 | bytes 917504 | tf_op jit(solution)/shard_map/pallas_call | solution.py:92
  33.0 0.0 copy-start.1
  33.0 0.9 copy-done.1
  33.9 7.2 %all-to-all-start.1 = ((f32[16,56,256]{2,1,0:T(8,128)}), f32[16,56,256]{2,1,0:T(8,128)}, u32[]{:S(2)}, u32[]{:S(2)}) async-start(f32[16,56,256]{2,1,0:T(8,128)} %bitcast.31), calls=%async_computation.1 | async-start | bytes 1835008 | tf_op jit(solution)/shard_map/all_to_all | solution.py:37
  41.1 0.0 copy-done
  41.1 1.8 %dynamic-slice_bitcast_fusion = bf16[3,3,3,32,256]{3,4,2,1,0:T(8,128)(2,1)} fusion(bf16[3,3,3,256,256]{4,3,2,1,0:T(8,128)(2,1)S(1)} %copy-done, s32[]{:T(128)S(6)} %select_n.4), kind=kLoop, calls=%fused_computation | loop fusion | bytes 884740 | tf_op jit(solution)/shard_map/transpose | solution.py:187
  42.9 2.4 %copy.6 = bf16[3,3,3,32,256]{4,3,2,1,0:T(8,128)(2,1)} copy(bf16[3,3,3,32,256]{3,4,2,1,0:T(8,128)(2,1)} %dynamic-slice_bitcast_fusion) | data formatting | bytes 884736 | tf_op jit(solution)/shard_map/transpose | solution.py:187
  45.4 13.3 %all_gather.9.vol_ref = bf16[256,1024]{1,0:T(8,128)(2,1)S(1)} all-gather(bf16[32,1024]{1,0:T(8,128)(2,1)} %bitcast.36), channel_id=1, replica_groups=mesh['space'=128,'chan'=8] {'chan'}, dimensions={0}, use_global_device_ids=true | all-gather | bytes 589824 | tf_op jit(solution)/shard_map/all_gather | solution.py:177
  58.7 0.0 copy-start.2
  58.7 1.0 copy-done.2
  59.7 2.2 %shard_map.58 = (f32[64,1024]{1,0:T(8,128)S(1)}, f32[64,1024]{1,0:T(8,128)S(1)}, f32[64,1024]{1,0:T(8,128)S(1)}) custom-call(bf16[3,288,256]{2,1,0:T(8,128)(2,1)S(1)} %bitcast.33, bf16[256,1024]{1,0:T(8,128)(2,1)S(1)} %all_gather.9.vol_ref, bf16[3,288,256]{2,1,0:T(8,128)(2,1)S(1)} %bitcast.32, bf16[256,1024]{1,0:T(8,128)(2,1)} %bitcast.3.cot_ref.refs_3_), custom_call_target="tpu_custom_call" | custom-call | flops 905969664 | bytes 1671168 | tf_op jit(solution)/shard_map/pallas_call | solution.py:146
  62.0 3.8 %collective-permute-start = (f32[64,1024]{1,0:T(8,128)S(1)}, f32[64,1024]{1,0:T(8,128)S(1)}, u32[]{:S(2)}, u32[]{:S(2)}) collective-permute-start(f32[64,1024]{1,0:T(8,128)S(1)} %get-tuple-element.7), channel_id=1, source_target_pairs={{0,8},{8,16},{16,24},{24,32},{32,40},{40,48},{48,56},{56,64},{64,7... | collective-permute-start | bytes 786440 | tf_op jit(solution)/shard_map/ppermute | solution.py:191
  65.8 1.3 collective-permute-start.1
  67.1 4.7 %collective-permute-done = f32[64,1024]{1,0:T(8,128)S(1)} collective-permute-done((f32[64,1024]{1,0:T(8,128)S(1)}, f32[64,1024]{1,0:T(8,128)S(1)}, u32[]{:S(2)}, u32[]{:S(2)}) %collective-permute-start) | collective-permute-done | bytes 262176 | tf_op jit(solution)/shard_map/ppermute | solution.py:191
  71.8 4.1 %collective-permute-done.1 = f32[64,1024]{1,0:T(8,128)S(1)} collective-permute-done((f32[64,1024]{1,0:T(8,128)S(1)}, f32[64,1024]{1,0:T(8,128)S(1)}, u32[]{:S(2)}, u32[]{:S(2)}) %collective-permute-start.1) | collective-permute-done | bytes 262176 | tf_op jit(solution)/shard_map/ppermute | solution.py:191
  76.0 0.6 copy.11
  76.6 0.6 copy.12
  77.3 0.0 all-to-all-done.1
  77.3 1.9 %reduce_sum.9 = f32[56,256]{1,0:T(8,128)} reduce(f32[16,56,256]{2,1,0:T(8,128)} %all-to-all-done.1, f32[]{:T(128)} %constant.4.clone.1), dimensions={0}, to_apply=%region_0.0 | reduce | flops 215040 | bytes 974852 | tf_op jit(solution)/shard_map/reduce_sum | solution.py:181
  79.1 49.0 %psum.7 = f32[56,256]{1,0:T(8,128)} all-reduce(f32[56,256]{1,0:T(8,128)} %reduce_sum.9), channel_id=1, replica_groups={{0,32,64,96,128,160,192,224},{8,40,72,104,136,168,200,232},{16,48,80,11..., use_global_device_ids=true, to_apply=%region_1.0 | all-reduce | flops 14336 | bytes 114688 | tf_op jit(solution)/shard_map/psum | solution.py:181
  128.2 14.3 %all_gather.10 = f32[224,256]{1,0:T(8,128)S(1)} all-gather(f32[56,256]{1,0:T(8,128)} %psum.7), channel_id=1, replica_groups={{0,8,16,24},{32,40,48,56},{64,72,80,88},{96,104,112,120},{128,136,144,1..., dimensions={0}, use_global_device_ids=true | all-gather | bytes 286720 | tf_op jit(solution)/shard_map/all_gather | solution.py:182
  142.5 13.8 %all_gather.11 = f32[896,256]{1,0:T(8,128)S(1)} all-gather(f32[224,256]{1,0:T(8,128)S(1)} %all_gather.10), channel_id=1, replica_groups={{0,256,512,768},{8,264,520,776},{16,272,528,784},{24,280,536,792},{32,2..., dimensions={0}, use_global_device_ids=true | all-gather | bytes 1146880 | tf_op jit(solution)/shard_map/all_gather | solution.py:183
  156.3 1.0 slice.16
  (3 shorter events, 0.1 us)
Async XLA Ops:
  0.6 40.5 %copy-start = (bf16[3,3,3,256,256]{4,3,2,1,0:T(8,128)(2,1)S(1)}, bf16[3,3,3,256,256]{4,3,2,1,0:T(8,128)(2,1)}, u32[]{:S(2)}) copy-start(bf16[3,3,3,256,256]{4,3,2,1,0:T(8,128)(2,1)} %param.4) | copy-start | bytes 10616836
  2.5 26.2 %all-to-all-start = ((bf16[8,32,1024]{2,1,0:T(8,128)(2,1)}), bf16[8,32,1024]{2,1,0:T(8,128)(2,1)}, u32[]{:S(2)}, u32[]{:S(2)}) async-start(bf16[8,32,1024]{2,1,0:T(8,128)(2,1)} %broadcast_in_dim.8), calls=%async_computation | async-start | bytes 1048576 | tf_op jit(solution)/shard_map/all_to_all | solution.py:37
  20.6 3.2 %collective-permute-start.2 = (bf16[32,1024]{1,0:T(8,128)(2,1)S(1)}, bf16[32,1024]{1,0:T(8,128)(2,1)S(1)}, u32[]{:S(2)}, u32[]{:S(2)}) collective-permute-start(bf16[32,1024]{1,0:T(8,128)(2,1)S(1)} %bitcast.34), channel_id=1, source_target_pairs={{0,8},{8,16},{16,24},{24,32},{32,40},{40,48},{48,56},{56,64},{64,7... | collective-permute-start | bytes 196616 | tf_op jit(solution)/shard_map/ppermute | solution.py:175
  21.9 6.2 %collective-permute-start.3 = (bf16[32,1024]{1,0:T(8,128)(2,1)S(1)}, bf16[32,1024]{1,0:T(8,128)(2,1)S(1)}, u32[]{:S(2)}, u32[]{:S(2)}) collective-permute-start(bf16[32,1024]{1,0:T(8,128)(2,1)S(1)} %bitcast.35), channel_id=1, source_target_pairs={{8,0},{16,8},{24,16},{32,24},{40,32},{48,40},{56,48},{64,56},{72,6... | collective-permute-start | bytes 196616 | tf_op jit(solution)/shard_map/ppermute | solution.py:176
  23.2 0.6 copy-start.3
  23.8 0.6 copy-start.5
  28.0 0.6 copy-start.7
  28.7 0.8 copy-start.4
  29.6 0.8 copy-start.6
  30.4 0.8 copy-start.8
  33.0 0.9 copy-start.1
  33.9 43.4 %all-to-all-start.1 = ((f32[16,56,256]{2,1,0:T(8,128)}), f32[16,56,256]{2,1,0:T(8,128)}, u32[]{:S(2)}, u32[]{:S(2)}) async-start(f32[16,56,256]{2,1,0:T(8,128)} %bitcast.31), calls=%async_computation.1 | async-start | bytes 1835008 | tf_op jit(solution)/shard_map/all_to_all | solution.py:37
  58.7 1.0 copy-start.2
  62.0 9.8 %collective-permute-start = (f32[64,1024]{1,0:T(8,128)S(1)}, f32[64,1024]{1,0:T(8,128)S(1)}, u32[]{:S(2)}, u32[]{:S(2)}) collective-permute-start(f32[64,1024]{1,0:T(8,128)S(1)} %get-tuple-element.7), channel_id=1, source_target_pairs={{0,8},{8,16},{16,24},{24,32},{32,40},{40,48},{48,56},{56,64},{64,7... | collective-permute-start | bytes 786440 | tf_op jit(solution)/shard_map/ppermute | solution.py:191
  65.8 10.2 %collective-permute-start.1 = (f32[64,1024]{1,0:T(8,128)S(1)}, f32[64,1024]{1,0:T(8,128)S(1)}, u32[]{:S(2)}, u32[]{:S(2)}) collective-permute-start(f32[64,1024]{1,0:T(8,128)S(1)} %get-tuple-element.8), channel_id=1, source_target_pairs={{8,0},{16,8},{24,16},{32,24},{40,32},{48,40},{56,48},{64,56},{72,6... | collective-permute-start | bytes 786440 | tf_op jit(solution)/shard_map/ppermute | solution.py:191

commit v3 on v2

v3 whole, which is shorter than its diff:
```python
import math

import jax
import jax.numpy as jnp
from jax import lax
from jax.experimental import pallas as pl
from jax.experimental.pallas import tpu as pltpu
from jax.sharding import PartitionSpec as P

TAPS = 27
Y_CHIPS = 4
NEAR = 4


def groups_of(count):
    length = count // Y_CHIPS
    far = length // NEAR
    along_y = [[y * length + z for y in range(Y_CHIPS)] for z in range(length)]
    near_z = [
        [y * length + hop * NEAR + k for k in range(NEAR)]
        for y in range(Y_CHIPS)
        for hop in range(far)
    ]
    block = [
        [y * length + hop * NEAR + k for y in range(Y_CHIPS) for k in range(NEAR)]
        for hop in range(far)
    ]
    far_z = [
        [y * length + hop * NEAR + k for hop in range(far)]
        for y in range(Y_CHIPS)
        for k in range(NEAR)
    ]
    return along_y, near_z, block, far_z


def exchange(pieces, axis, groups=None):
    return lax.all_to_all(pieces, axis, 0, 0, tiled=True, axis_index_groups=groups)


VMEM = pl.BlockSpec(memory_space=pltpu.VMEM)
HBM = pl.BlockSpec(memory_space=pl.ANY)


def limits(mib=56):
    return pltpu.CompilerParams(vmem_limit_bytes=mib * 1024 * 1024)


TOKEN = jax.ShapeDtypeStruct((8, 128), jnp.float32)


def own_weights(kernel, count):
    channels = kernel.shape[2]
    width = min(channels, 128)
    per = width // count

    def body(kernel_ref, fore, back, token, block, sems):
        token[...] = jnp.zeros(token.shape, token.dtype)
        member = lax.axis_index("chan")
        lanes = pl.ds(pl.multiple_of((member // per) * width, width), width)
        rows = pl.ds(pl.multiple_of(member * count, count), count)
        moves = [
            pltpu.make_async_copy(kernel_ref.at[:, :, lanes], block, sems.at[0]),
            pltpu.make_async_copy(kernel_ref.at[:, rows, :], back, sems.at[1]),
        ]
        for move in moves:
            move.start()
        at = lax.broadcasted_iota(jnp.int32, (count, width), 1)
        row = lax.broadcasted_iota(jnp.int32, (count, width), 0)
        pick = jnp.where(at == row + (member % per) * count, 1.0, 0.0).astype(fore.dtype)
        moves[0].wait()
        for tap in range(TAPS):
            fore[tap] = lax.dot_general(
                pick, block[tap], (((1,), (1,)), ((), ())), preferred_element_type=jnp.float32
            ).astype(fore.dtype)
        moves[1].wait()

    shape = jax.ShapeDtypeStruct((TAPS, count, channels), kernel.dtype)
    return pl.pallas_call(
        body,
        out_shape=(shape, shape, TOKEN),
        in_specs=[HBM],
        out_specs=(VMEM, VMEM, VMEM),
        scratch_shapes=[
            pltpu.VMEM((TAPS, channels, width), kernel.dtype),
            pltpu.SemaphoreType.DMA((2,)),
        ],
        compiler_params=limits(),
    )(kernel)


def spread(block, copies):
    count, height, breadth = block.shape
    cells = height * breadth

    def body(block_ref, out, wide, flat, sems):
        wide[...] = block_ref[...].astype(jnp.float32)
        for q in range(height):
            flat[:, q * breadth : (q + 1) * breadth] = wide[:, q, :].astype(flat.dtype)
        moves = [pltpu.make_async_copy(flat, out.at[k], sems.at[k]) for k in range(copies)]
        for move in moves:
            move.start()
        for move in moves:
            move.wait()

    return pl.pallas_call(
        body,
        out_shape=jax.ShapeDtypeStruct((copies, count, cells), block.dtype),
        in_specs=[VMEM],
        out_specs=HBM,
        scratch_shapes=[
            pltpu.VMEM(block.shape, jnp.float32),
            pltpu.VMEM((count, cells), block.dtype),
            pltpu.SemaphoreType.DMA((copies,)),
        ],
        compiler_params=limits(),
    )(block)


def sum_pieces(pieces, after):
    count, rows, columns = pieces.shape

    def body(pieces_ref, after_ref, out):
        total = pieces_ref[0]
        for k in range(1, count):
            total = total + pieces_ref[k]
        out[...] = total

    return pl.pallas_call(
        body,
        out_shape=jax.ShapeDtypeStruct((rows, columns), pieces.dtype),
        in_specs=[VMEM, VMEM],
        out_specs=VMEM,
        compiler_params=limits(8),
        cost_estimate=pl.CostEstimate(
            flops=pieces.size, bytes_accessed=4 * pieces.size, transcendentals=0
        ),
    )(pieces, after)


def repeated(piece, copies):
    def body(piece_ref, out, sems):
        moves = [pltpu.make_async_copy(piece_ref, out.at[k], sems.at[k]) for k in range(copies)]
        for move in moves:
            move.start()
        for move in moves:
            move.wait()

    return pl.pallas_call(
        body,
        out_shape=jax.ShapeDtypeStruct((copies,) + piece.shape, piece.dtype),
        in_specs=[HBM],
        out_specs=HBM,
        scratch_shapes=[pltpu.SemaphoreType.DMA((copies,))],
        compiler_params=limits(),
    )(piece)


def finish(own, low, high, height, breadth, dtype, after):
    rows = own.shape[0]
    count = rows // 2

    def body(own_ref, low_ref, high_ref, after_ref, first, second, wide):
        for q in range(height):
            lanes = pl.ds(q * breadth, breadth)
            wide[:, q, :] = own_ref[:, lanes] + low_ref[:, lanes] + high_ref[:, lanes]
        first[...] = wide[:count].astype(dtype)
        second[...] = wide[count:].astype(dtype)

    shape = jax.ShapeDtypeStruct((count, height, breadth), dtype)
    return pl.pallas_call(
        body,
        out_shape=(shape, shape),
        in_specs=[VMEM] * 3 + [HBM],
        out_specs=(VMEM, VMEM),
        scratch_shapes=[pltpu.VMEM((rows, height, breadth), jnp.float32)],
        compiler_params=limits(8),
    )(own, low, high, after)


def shift_lanes(value, offset, lanes):
    if offset == 0:
        return value
    at = lax.broadcasted_iota(jnp.int32, value.shape, 1)
    if offset < 0:
        return jnp.where(at == 0, 0.0, pltpu.roll(value, 1, 1))
    return jnp.where(at == lanes - 1, 0.0, pltpu.roll(value, lanes - 1, 1))


def weight_terms(low, own, high, cot, after, factor, height, breadth):
    count, cells = own.shape
    channels = cot.shape[0]
    group = 3 * count
    rows = 9 * group + count

    def body(low_ref, own_ref, high_ref, cot_ref, after_ref, *rest):
        out, planes, field, stack, held, in_sems, out_sems = rest
        sources = (low_ref, own_ref, high_ref)
        moves = [
            pltpu.make_async_copy(source, planes.at[k], in_sems.at[k])
            for k, source in enumerate(sources)
        ]
        moves.append(pltpu.make_async_copy(cot_ref, field, in_sems.at[3]))
        for move in moves:
            move.start()
        sent = []

        def send(start, size):
            move = pltpu.make_async_copy(
                held.at[pl.ds(start, size)], out.at[pl.ds(start, size)], out_sems.at[len(sent)]
            )
            move.start()
            sent.append(move)

        held[9 * group :, :] = jnp.zeros((count, channels), held.dtype)
        send(9 * group, count)
        edge = jnp.zeros((9 * count, breadth), stack.dtype)
        stack[:, :breadth] = edge
        stack[:, (height + 1) * breadth :] = edge
        for a in range(3):
            moves[a].wait()
            for q in range(height):
                row = planes[a, :, q * breadth : (q + 1) * breadth].astype(jnp.float32)
                for c in range(3):
                    at = (a * 3 + c) * count
                    stack[at : at + count, (q + 1) * breadth : (q + 2) * breadth] = shift_lanes(
                        row, c - 1, breadth
                    ).astype(stack.dtype)
        moves[3].wait()
        for b in range(3):
            part = lax.dot_general(
                stack[:, b * breadth : b * breadth + cells],
                field[...],
                (((1,), (1,)), ((), ())),
                preferred_element_type=jnp.float32,
            )
            for a in range(3):
                at = (a * 3 + b) * group
                held[at : at + group, :] = part[a * group : (a + 1) * group] * factor
                send(at, group)
        for move in sent:
            move.wait()

    return pl.pallas_call(
        body,
        out_shape=jax.ShapeDtypeStruct((rows, channels), jnp.float32),
        in_specs=[HBM] * 5,
        out_specs=HBM,
        scratch_shapes=[
            pltpu.VMEM((3, count, cells), own.dtype),
            pltpu.VMEM((channels, cells), cot.dtype),
            pltpu.VMEM((9 * count, cells + 2 * breadth), own.dtype),
            pltpu.VMEM((rows, channels), jnp.float32),
            pltpu.SemaphoreType.DMA((4,)),
            pltpu.SemaphoreType.DMA((10,)),
        ],
        compiler_params=limits(),
        cost_estimate=pl.CostEstimate(
            flops=2 * rows * channels * cells,
            bytes_accessed=4 * rows * channels,
            transcendentals=0,
        ),
    )(low, own, high, cot, after)


def conv_terms(weights, field, mirror, height, breadth, own, up, down):
    count = weights.shape[1] // 9
    places = (down, own, up) if mirror else (up, own, down)
    for a in range(3):
        part = lax.dot_general(
            weights[a],
            field[...],
            (((1,), (0,)), ((), ())),
            preferred_element_type=jnp.float32,
        )
        for q in range(height):
            total = None
            for c in range(3):
                column = None
                for b in range(3):
                    source = q + (1 - b if mirror else b - 1)
                    if 0 <= source < height:
                        at = (b * 3 + c) * count
                        term = part[at : at + count, source * breadth : (source + 1) * breadth]
                        column = term if column is None else column + term
                moved = shift_lanes(column, 1 - c if mirror else c - 1, breadth)
                total = moved if total is None else total + moved
            places[a][:, q * breadth : (q + 1) * breadth] = total


def plane_terms(fore, vol, back, cot, height, breadth):
    count = fore.shape[1] // 9
    cells = vol.shape[1]

    def body(fore_ref, vol_ref, back_ref, cot_ref, own, up, down, token):
        token[...] = jnp.zeros(token.shape, token.dtype)
        halves = [pl.ds(0, count), pl.ds(count, count)]
        conv_terms(
            fore_ref, vol_ref, False, height, breadth, *(r.at[halves[0]] for r in (own, up, down))
        )
        conv_terms(
            back_ref, cot_ref, True, height, breadth, *(r.at[halves[1]] for r in (own, up, down))
        )

    shape = jax.ShapeDtypeStruct((2 * count, cells), jnp.float32)
    return pl.pallas_call(
        body,
        out_shape=(shape, shape, shape, TOKEN),
        in_specs=[VMEM] * 4,
        out_specs=(VMEM,) * 4,
        compiler_params=limits(12),
        cost_estimate=pl.CostEstimate(
            flops=4 * fore.size * cells,
            bytes_accessed=4 * fore.size + 24 * count * cells,
            transcendentals=0,
        ),
    )(fore, vol, back, cot)


def local(volume, kernel, cotangent):
    count, planes, height, breadth = volume.shape
    cells = height * breadth
    channels = kernel.shape[3]
    slabs = lax.axis_size("space")
    parts = lax.axis_size("chan")
    member = lax.axis_index("chan")
    factor = 1.0 / math.sqrt(slabs * planes * cells)
    along_y, near_z, block, far_z = groups_of(slabs)
    up = [(i, i + 1) for i in range(slabs - 1)]
    down = [(i + 1, i) for i in range(slabs - 1)]

    cot_copies = spread(cotangent.reshape(count, height, breadth), parts)
    cot_all = exchange(cot_copies, "chan").reshape(channels, cells)
    vol = volume.reshape(count, cells)
    vol_low = lax.ppermute(vol, "space", up)
    vol_high = lax.ppermute(vol, "space", down)
    fore, back, ready = own_weights(kernel.reshape(TAPS, channels, channels), count)
    fore = fore.reshape(3, 9 * count, channels)
    back = back.reshape(3, 9 * count, channels)

    terms = weight_terms(vol_low, vol, vol_high, cot_all, ready, factor, height, breadth)
    pieces = exchange(terms.reshape(len(block[0]), -1, channels), "space", block)
    vol_all = lax.all_gather(vol, "chan", axis=0, tiled=True)
    own, upper, lower, done = plane_terms(fore, vol_all, back, cot_all, height, breadth)
    total = lax.psum(sum_pieces(pieces, done), "space", axis_index_groups=far_z)
    near = exchange(repeated(total, len(near_z[0])), "space", near_z).reshape(-1, channels)
    whole = exchange(repeated(near, len(along_y[0])), "space", along_y).reshape(-1, channels)
    weight_grad = whole[: TAPS * count].reshape(3, 3, 3, count, channels)

    from_low = lax.ppermute(upper, "space", up)
    from_high = lax.ppermute(lower, "space", down)
    output, input_grad = finish(own, from_low, from_high, height, breadth, volume.dtype, near)
    return (output.reshape(volume.shape), input_grad.reshape(volume.shape), weight_grad)


def solution(mesh):
    return jax.shard_map(
        local,
        mesh=mesh,
        in_specs=(P("chan", "space", None, None), P(), P("chan", "space", None, None)),
        out_specs=(
            P("chan", "space", None, None),
            P("chan", "space", None, None),
            P(None, None, None, "chan", None),
        ),
        check_vma=False,
    )
```

time: 158 us -> 179 us (1.13)
  the two profiles are of different devices: /device:TPU:2 before, /device:TPU:10 now
where the time goes in v3:
time: 179 us; the launch traced here: 178 us
  blocking collectives  70.4 us (39%)
  Pallas kernels  46.9 us (26%)
  starting transfers between devices  44.4 us (25%)
  waiting for transfers between devices  10.8 us (6%)
  local copies, waits for them, and re-layouts  4.6 us (3%)
    psum x1, blocking collectives, local(): total = lax.psum(sum_pieces(pieces, done), 'space', axis_index_groups=far_z)  46.1 us
    pallas_call x2, Pallas kernels, repeated(): pl.pallas_call(body, out_shape=jax.ShapeDtypeStruct((copies,) + piece.sha...  37 us
    ppermute x1, starting transfers between devices, local(): vol_high = lax.ppermute(vol, 'space', down)  16.7 us
    all_to_all x3, starting transfers between devices, exchange(): lax.all_to_all(pieces, axis, 0, 0, tiled=True, axis_index_groups=groups)  16 us
    all_gather x1, blocking collectives, local(): vol_all = lax.all_gather(vol, 'chan', axis=0, tiled=True)  13.3 us
    all_to_all x1, blocking collectives, exchange(): lax.all_to_all(pieces, axis, 0, 0, tiled=True, axis_index_groups=groups)  11 us
    all_to_all x3, waiting for transfers between devices, exchange(): lax.all_to_all(pieces, axis, 0, 0, tiled=True, axis_index_groups=groups)  6.91 us
    ppermute x1, starting transfers between devices, local(): from_high = lax.ppermute(lower, 'space', down)  4.95 us
  transfers between devices with their start and end apart: 7, of which 3 were waited for; matrix products, arithmetic and copies ran while one was open for 0% of the time, Pallas kernels for 3%

profile of v3, /device:TPU:10, one launch (start us, length us, event | category | flops | bytes accessed | tf_op | source)
XLA Modules:
  0.0 177.9 jit_solution(7409428733384607112)
XLA Ops:
  0.6 1.8 %shard_map.59 = bf16[8,32,1024]{2,1,0:T(8,128)(2,1)} custom-call(bf16[32,8,128]{2,1,0:T(8,128)(2,1)} %bitcast.34), custom_call_target="tpu_custom_call" | custom-call | tf_op jit(solution)/shard_map/pallas_call | solution.py:105
  2.5 4.8 %all-to-all-start = ((bf16[8,32,1024]{2,1,0:T(8,128)(2,1)}), bf16[8,32,1024]{2,1,0:T(8,128)(2,1)S(1)}, u32[]{:S(2)}, u32[]{:S(2)}) async-start(bf16[8,32,1024]{2,1,0:T(8,128)(2,1)} %shard_map.59), calls=%async_computation | async-start | bytes 1048576 | tf_op jit(solution)/shard_map/all_to_all | solution.py:37
  7.3 0.8 copy.10
  8.2 0.0 copy-start.5
  8.2 3.8 %collective-permute-start.2 = (bf16[32,1024]{1,0:T(8,128)(2,1)S(1)}, bf16[32,1024]{1,0:T(8,128)(2,1)S(1)}, u32[]{:S(2)}, u32[]{:S(2)}) collective-permute-start(bf16[32,1024]{1,0:T(8,128)(2,1)S(1)} %bitcast.30), channel_id=1, source_target_pairs={{0,8},{8,16},{16,24},{24,32},{32,40},{40,48},{48,56},{56,64},{64,7... | collective-permute-start | bytes 196616 | tf_op jit(solution)/shard_map/ppermute | solution.py:334
  12.0 16.7 %collective-permute-start.3 = (bf16[32,1024]{1,0:T(8,128)(2,1)S(1)}, bf16[32,1024]{1,0:T(8,128)(2,1)S(1)}, u32[]{:S(2)}, u32[]{:S(2)}) collective-permute-start(bf16[32,1024]{1,0:T(8,128)(2,1)S(1)} %bitcast.31), channel_id=1, source_target_pairs={{8,0},{16,8},{24,16},{32,24},{40,32},{48,40},{56,48},{64,56},{72,6... | collective-permute-start | bytes 196616 | tf_op jit(solution)/shard_map/ppermute | solution.py:335
  28.7 3.2 %shard_map.58 = (bf16[27,32,256]{2,1,0:T(8,128)(2,1)}, bf16[27,32,256]{2,1,0:T(8,128)(2,1)}, f32[8,128]{1,0:T(8,128)}) custom-call(bf16[27,256,256]{2,1,0:T(8,128)(2,1)} %bitcast.27), custom_call_target="tpu_custom_call" | custom-call | tf_op jit(solution)/shard_map/pallas_call | solution.py:78
  31.9 0.0 copy-start.3
  31.9 0.0 copy-start.4
  31.9 0.0 collective-permute-done.2.low_ref
  31.9 0.0 copy-start.6
  31.9 0.0 collective-permute-done.3.high_ref
  31.9 0.0 copy-start.7
  32.0 0.0 all-to-all-done
  32.0 0.0 copy-start.1
  32.0 0.0 copy-done.5
  32.0 0.6 copy-done.6
  32.6 0.0 copy-done.7
  32.6 0.2 copy-done.1
  32.8 2.7 %shard_map.61 = f32[896,256]{1,0:T(8,128)} custom-call(bf16[32,1024]{1,0:T(8,128)(2,1)} %copy-done.6, bf16[32,1024]{1,0:T(8,128)(2,1)} %bitcast.32, bf16[32,1024]{1,0:T(8,128)(2,1)} %copy-done.7, bf16[256,1024]{1,0:T(8,128)(2,1)} %bitcast.22, f32[8,128]{1,0:T(8,128)} %get-tuple-element.17.after_ref), custom_call_target="tpu_custom_call" | custom-call | flops 469762048 | bytes 917504 | tf_op jit(solution)/shard_map/pallas_call | solution.py:243
  35.5 5.1 %all-to-all-start.1 = ((f32[16,56,256]{2,1,0:T(8,128)}), f32[16,56,256]{2,1,0:T(8,128)S(1)}, u32[]{:S(2)}, u32[]{:S(2)}) async-start(f32[16,56,256]{2,1,0:T(8,128)} %bitcast.28), calls=%async_computation.1 | async-start | bytes 1835008 | tf_op jit(solution)/shard_map/all_to_all | solution.py:37
  40.6 13.3 %all_gather.3.vol_ref = bf16[256,1024]{1,0:T(8,128)(2,1)S(1)} all-gather(bf16[32,1024]{1,0:T(8,128)(2,1)} %bitcast.33), channel_id=1, replica_groups=mesh['space'=128,'chan'=8] {'chan'}, dimensions={0}, use_global_device_ids=true | all-gather | bytes 589824 | tf_op jit(solution)/shard_map/all_gather | solution.py:342
  53.9 0.0 copy-done.3
  53.9 0.0 copy-done.4
  53.9 0.0 copy-start.2
  53.9 1.0 copy-done.2
  54.9 1.2 shard_map.60
  56.1 6.9 %all-to-all-done.1.pieces_ref = f32[16,56,256]{2,1,0:T(8,128)S(1)} async-done(((f32[16,56,256]{2,1,0:T(8,128)}), f32[16,56,256]{2,1,0:T(8,128)S(1)}, u32[]{:S(2)}, u32[]{:S(2)}) %all-to-all-start.1) | async-done | bytes 917536 | tf_op jit(solution)/shard_map/all_to_all | solution.py:37
  63.0 46.1 %psum.7.piece_ref = f32[56,256]{1,0:T(8,128)} all-reduce(f32[56,256]{1,0:T(8,128)S(1)} %shard_map.62), channel_id=1, replica_groups={{0,32,64,96,128,160,192,224},{8,40,72,104,136,168,200,232},{16,48,80,11..., use_global_device_ids=true, to_apply=%region_0.0 | all-reduce | flops 14336 | bytes 114688 | tf_op jit(solution)/shard_map/psum | solution.py:344
  109.2 8.1 %shard_map.63 = f32[4,56,256]{2,1,0:T(8,128)} custom-call(f32[56,256]{1,0:T(8,128)} %psum.7.piece_ref), custom_call_target="tpu_custom_call" | custom-call | tf_op jit(solution)/shard_map/pallas_call | solution.py:148
  117.3 11.0 %all_to_all.20 = f32[4,56,256]{2,1,0:T(8,128)} all-to-all(f32[4,56,256]{2,1,0:T(8,128)} %shard_map.63), channel_id=1, replica_groups={{0,8,16,24},{32,40,48,56},{64,72,80,88},{96,104,112,120},{128,136,144,1..., dimensions={0} | all-to-all | bytes 458752 | tf_op jit(solution)/shard_map/all_to_all | solution.py:37
  128.3 28.9 %shard_map.65 = f32[4,224,256]{2,1,0:T(8,128)} custom-call(f32[224,256]{1,0:T(8,128)} %bitcast.20), custom_call_target="tpu_custom_call" | custom-call | tf_op jit(solution)/shard_map/pallas_call | solution.py:148
  157.2 6.1 %all-to-all-start.3 = ((f32[4,224,256]{2,1,0:T(8,128)}), f32[4,224,256]{2,1,0:T(8,128)S(1)}, u32[]{:S(2)}, u32[]{:S(2)}) async-start(f32[4,224,256]{2,1,0:T(8,128)} %shard_map.65), calls=%async_computation.3 | async-start | bytes 1835008 | tf_op jit(solution)/shard_map/all_to_all | solution.py:37
  163.3 3.0 %collective-permute-start = (f32[64,1024]{1,0:T(8,128)S(1)}, f32[64,1024]{1,0:T(8,128)S(1)}, u32[]{:S(2)}, u32[]{:S(2)}) collective-permute-start(f32[64,1024]{1,0:T(8,128)S(1)} %get-tuple-element.15), channel_id=1, source_target_pairs={{0,8},{8,16},{16,24},{24,32},{32,40},{40,48},{48,56},{56,64},{64,7... | collective-permute-start | bytes 786440 | tf_op jit(solution)/shard_map/ppermute | solution.py:349
  166.3 5.0 %collective-permute-start.1 = (f32[64,1024]{1,0:T(8,128)S(1)}, f32[64,1024]{1,0:T(8,128)S(1)}, u32[]{:S(2)}, u32[]{:S(2)}) collective-permute-start(f32[64,1024]{1,0:T(8,128)S(1)} %get-tuple-element.16), channel_id=1, source_target_pairs={{8,0},{16,8},{24,16},{32,24},{40,32},{48,40},{56,48},{64,56},{72,6... | collective-permute-start | bytes 786440 | tf_op jit(solution)/shard_map/ppermute | solution.py:350
  171.2 2.4 %collective-permute-done.low_ref = f32[64,1024]{1,0:T(8,128)S(1)} collective-permute-done((f32[64,1024]{1,0:T(8,128)S(1)}, f32[64,1024]{1,0:T(8,128)S(1)}, u32[]{:S(2)}, u32[]{:S(2)}) %collective-permute-start) | collective-permute-done | bytes 262176 | tf_op jit(solution)/shard_map/ppermute | solution.py:349
  173.6 1.5 collective-permute-done.1.high_ref
  175.1 0.0 copy-start
  175.1 0.9 copy-done
  176.0 0.9 shard_map.64
  176.9 0.0 all-to-all-done.3
  176.9 1.0 slice.4
  (1 shorter events, 0.0 us)
Async XLA Ops:
  2.5 29.5 %all-to-all-start = ((bf16[8,32,1024]{2,1,0:T(8,128)(2,1)}), bf16[8,32,1024]{2,1,0:T(8,128)(2,1)S(1)}, u32[]{:S(2)}, u32[]{:S(2)}) async-start(bf16[8,32,1024]{2,1,0:T(8,128)(2,1)} %shard_map.59), calls=%async_computation | async-start | bytes 1048576 | tf_op jit(solution)/shard_map/all_to_all | solution.py:37
  8.2 23.8 %copy-start.5 = (bf16[4,8,8,128]{3,1,2,0:T(8,128)(2,1)}, bf16[4,8,8,128]{3,1,2,0:T(8,128)(2,1)S(1)}, u32[]{:S(2)}) copy-start(bf16[4,8,8,128]{3,1,2,0:T(8,128)(2,1)S(1)} %copy.10) | copy-start | bytes 196612
  8.2 23.7 %collective-permute-start.2 = (bf16[32,1024]{1,0:T(8,128)(2,1)S(1)}, bf16[32,1024]{1,0:T(8,128)(2,1)S(1)}, u32[]{:S(2)}, u32[]{:S(2)}) collective-permute-start(bf16[32,1024]{1,0:T(8,128)(2,1)S(1)} %bitcast.30), channel_id=1, source_target_pairs={{0,8},{8,16},{16,24},{24,32},{32,40},{40,48},{48,56},{56,64},{64,7... | collective-permute-start | bytes 196616 | tf_op jit(solution)/shard_map/ppermute | solution.py:334
  12.0 19.9 %collective-permute-start.3 = (bf16[32,1024]{1,0:T(8,128)(2,1)S(1)}, bf16[32,1024]{1,0:T(8,128)(2,1)S(1)}, u32[]{:S(2)}, u32[]{:S(2)}) collective-permute-start(bf16[32,1024]{1,0:T(8,128)(2,1)S(1)} %bitcast.31), channel_id=1, source_target_pairs={{8,0},{16,8},{24,16},{32,24},{40,32},{48,40},{56,48},{64,56},{72,6... | collective-permute-start | bytes 196616 | tf_op jit(solution)/shard_map/ppermute | solution.py:335
  31.9 22.0 %copy-start.3 = (bf16[27,32,256]{2,1,0:T(8,128)(2,1)S(1)}, bf16[27,32,256]{2,1,0:T(8,128)(2,1)}, u32[]{:S(2)}) copy-start(bf16[27,32,256]{2,1,0:T(8,128)(2,1)} %get-tuple-element.12) | copy-start | bytes 1327108
  31.9 22.0 %copy-start.4 = (bf16[27,32,256]{2,1,0:T(8,128)(2,1)S(1)}, bf16[27,32,256]{2,1,0:T(8,128)(2,1)}, u32[]{:S(2)}) copy-start(bf16[27,32,256]{2,1,0:T(8,128)(2,1)} %get-tuple-element.13) | copy-start | bytes 1327108
  31.9 0.6 copy-start.6
  31.9 0.6 copy-start.7
  32.0 0.8 copy-start.1
  35.5 27.5 %all-to-all-start.1 = ((f32[16,56,256]{2,1,0:T(8,128)}), f32[16,56,256]{2,1,0:T(8,128)S(1)}, u32[]{:S(2)}, u32[]{:S(2)}) async-start(f32[16,56,256]{2,1,0:T(8,128)} %bitcast.28), calls=%async_computation.1 | async-start | bytes 1835008 | tf_op jit(solution)/shard_map/all_to_all | solution.py:37
  53.9 1.0 copy-start.2
  157.2 19.7 %all-to-all-start.3 = ((f32[4,224,256]{2,1,0:T(8,128)}), f32[4,224,256]{2,1,0:T(8,128)S(1)}, u32[]{:S(2)}, u32[]{:S(2)}) async-start(f32[4,224,256]{2,1,0:T(8,128)} %shard_map.65), calls=%async_computation.3 | async-start | bytes 1835008 | tf_op jit(solution)/shard_map/all_to_all | solution.py:37
  163.3 10.4 %collective-permute-start = (f32[64,1024]{1,0:T(8,128)S(1)}, f32[64,1024]{1,0:T(8,128)S(1)}, u32[]{:S(2)}, u32[]{:S(2)}) collective-permute-start(f32[64,1024]{1,0:T(8,128)S(1)} %get-tuple-element.15), channel_id=1, source_target_pairs={{0,8},{8,16},{16,24},{24,32},{32,40},{40,48},{48,56},{56,64},{64,7... | collective-permute-start | bytes 786440 | tf_op jit(solution)/shard_map/ppermute | solution.py:349
  166.3 8.8 %collective-permute-start.1 = (f32[64,1024]{1,0:T(8,128)S(1)}, f32[64,1024]{1,0:T(8,128)S(1)}, u32[]{:S(2)}, u32[]{:S(2)}) collective-permute-start(f32[64,1024]{1,0:T(8,128)S(1)} %get-tuple-element.16), channel_id=1, source_target_pairs={{8,0},{16,8},{24,16},{32,24},{40,32},{48,40},{56,48},{64,56},{72,6... | collective-permute-start | bytes 786440 | tf_op jit(solution)/shard_map/ppermute | solution.py:350
  175.1 0.9 copy-start

commit v4 on v3

--- a/solution.py
+++ b/solution.py
@@ -15,12 +15,6 @@
 def groups_of(count):
     length = count // Y_CHIPS
     far = length // NEAR
-    along_y = [[y * length + z for y in range(Y_CHIPS)] for z in range(length)]
-    near_z = [
-        [y * length + hop * NEAR + k for k in range(NEAR)]
-        for y in range(Y_CHIPS)
-        for hop in range(far)
-    ]
     block = [
         [y * length + hop * NEAR + k for y in range(Y_CHIPS) for k in range(NEAR)]
         for hop in range(far)
@@ -30,7 +24,7 @@
         for y in range(Y_CHIPS)
         for k in range(NEAR)
     ]
-    return along_y, near_z, block, far_z
+    return block, far_z
 
 
 def exchange(pieces, axis, groups=None):
@@ -148,7 +142,7 @@
     return pl.pallas_call(
         body,
         out_shape=jax.ShapeDtypeStruct((copies,) + piece.shape, piece.dtype),
-        in_specs=[HBM],
+        in_specs=[VMEM],
         out_specs=HBM,
         scratch_shapes=[pltpu.SemaphoreType.DMA((copies,))],
         compiler_params=limits(),
@@ -324,7 +318,7 @@
     parts = lax.axis_size("chan")
     member = lax.axis_index("chan")
     factor = 1.0 / math.sqrt(slabs * planes * cells)
-    along_y, near_z, block, far_z = groups_of(slabs)
+    block, far_z = groups_of(slabs)
     up = [(i, i + 1) for i in range(slabs - 1)]
     down = [(i + 1, i) for i in range(slabs - 1)]
 
@@ -342,13 +336,12 @@
     vol_all = lax.all_gather(vol, "chan", axis=0, tiled=True)
     own, upper, lower, done = plane_terms(fore, vol_all, back, cot_all, height, breadth)
     total = lax.psum(sum_pieces(pieces, done), "space", axis_index_groups=far_z)
-    near = exchange(repeated(total, len(near_z[0])), "space", near_z).reshape(-1, channels)
-    whole = exchange(repeated(near, len(along_y[0])), "space", along_y).reshape(-1, channels)
+    whole = exchange(repeated(total, len(block[0])), "space", block).reshape(-1, channels)
     weight_grad = whole[: TAPS * count].reshape(3, 3, 3, count, channels)
 
     from_low = lax.ppermute(upper, "space", up)
     from_high = lax.ppermute(lower, "space", down)
-    output, input_grad = finish(own, from_low, from_high, height, breadth, volume.dtype, near)
+    output, input_grad = finish(own, from_low, from_high, height, breadth, volume.dtype, total)
     return (output.reshape(volume.shape), input_grad.reshape(volume.shape), weight_grad)
 
 

time: 179 us -> 139 us (0.78)
  the two profiles are of different devices: /device:TPU:10 before, /device:TPU:38 now
where the time goes in v4:
time: 139 us
  blocking collectives  59.2 us (43%)
  starting transfers between devices  43.2 us (31%)
  waiting for transfers between devices  19.2 us (14%)
  Pallas kernels  11.7 us (8%)
  local copies, waits for them, and re-layouts  4.48 us (3%)
    psum x1, blocking collectives, local(): total = lax.psum(sum_pieces(pieces, done), 'space', axis_index_groups=far_z)  45.9 us
    all_to_all x3, starting transfers between devices, exchange(): lax.all_to_all(pieces, axis, 0, 0, tiled=True, axis_index_groups=groups)  22.3 us
    all_gather x1, blocking collectives, local(): vol_all = lax.all_gather(vol, 'chan', axis=0, tiled=True)  13.3 us
    ppermute x1, waiting for transfers between devices, local(): from_low = lax.ppermute(upper, 'space', up)  11.3 us
    ppermute x1, starting transfers between devices, local(): vol_high = lax.ppermute(vol, 'space', down)  11.3 us
    all_to_all x3, waiting for transfers between devices, exchange(): lax.all_to_all(pieces, axis, 0, 0, tiled=True, axis_index_groups=groups)  5.78 us
    ppermute x1, starting transfers between devices, local(): vol_low = lax.ppermute(vol, 'space', up)  3.83 us
    unnamed x17, local copies, waits for them, and re-layouts  3.51 us
  transfers between devices with their start and end apart: 7, of which 3 were waited for; matrix products, arithmetic and copies ran while one was open for 1% of the time, Pallas kernels for 4%

profile of v4, /device:TPU:38, one launch (start us, length us, event | category | flops | bytes accessed | tf_op | source)
XLA Modules:
  0.0 138.6 jit_solution(4009261420587653781)
XLA Ops:
  0.6 1.8 %shard_map.59 = bf16[8,32,1024]{2,1,0:T(8,128)(2,1)} custom-call(bf16[32,8,128]{2,1,0:T(8,128)(2,1)} %bitcast.31), custom_call_target="tpu_custom_call" | custom-call | tf_op jit(solution)/shard_map/pallas_call | solution.py:99
  2.5 4.8 %all-to-all-start = ((bf16[8,32,1024]{2,1,0:T(8,128)(2,1)}), bf16[8,32,1024]{2,1,0:T(8,128)(2,1)S(1)}, u32[]{:S(2)}, u32[]{:S(2)}) async-start(bf16[8,32,1024]{2,1,0:T(8,128)(2,1)} %shard_map.59), calls=%async_computation | async-start | bytes 1048576 | tf_op jit(solution)/shard_map/all_to_all | solution.py:31
  7.3 0.8 copy.10
  8.1 0.0 copy-start.5
  8.1 3.8 %collective-permute-start.2 = (bf16[32,1024]{1,0:T(8,128)(2,1)S(1)}, bf16[32,1024]{1,0:T(8,128)(2,1)S(1)}, u32[]{:S(2)}, u32[]{:S(2)}) collective-permute-start(bf16[32,1024]{1,0:T(8,128)(2,1)S(1)} %bitcast.27), channel_id=1, source_target_pairs={{0,8},{8,16},{16,24},{24,32},{32,40},{40,48},{48,56},{56,64},{64,7... | collective-permute-start | bytes 196616 | tf_op jit(solution)/shard_map/ppermute | solution.py:328
  12.0 11.3 %collective-permute-start.3 = (bf16[32,1024]{1,0:T(8,128)(2,1)S(1)}, bf16[32,1024]{1,0:T(8,128)(2,1)S(1)}, u32[]{:S(2)}, u32[]{:S(2)}) collective-permute-start(bf16[32,1024]{1,0:T(8,128)(2,1)S(1)} %bitcast.28), channel_id=1, source_target_pairs={{8,0},{16,8},{24,16},{32,24},{40,32},{48,40},{56,48},{64,56},{72,6... | collective-permute-start | bytes 196616 | tf_op jit(solution)/shard_map/ppermute | solution.py:329
  23.2 3.2 %shard_map.58 = (bf16[27,32,256]{2,1,0:T(8,128)(2,1)}, bf16[27,32,256]{2,1,0:T(8,128)(2,1)}, f32[8,128]{1,0:T(8,128)}) custom-call(bf16[27,256,256]{2,1,0:T(8,128)(2,1)} %bitcast.24), custom_call_target="tpu_custom_call" | custom-call | tf_op jit(solution)/shard_map/pallas_call | solution.py:72
  26.4 0.0 copy-start.3
  26.5 0.0 copy-start.4
  26.5 0.0 collective-permute-done.2.low_ref
  26.5 0.0 copy-start.6
  26.5 0.0 collective-permute-done.3.high_ref
  26.5 0.0 copy-start.7
  26.5 0.0 all-to-all-done
  26.5 0.0 copy-start
  26.5 0.0 copy-done.5
  26.5 0.6 copy-done.6
  27.1 0.0 copy-done.7
  27.1 0.2 copy-done
  27.3 2.7 %shard_map.61 = f32[896,256]{1,0:T(8,128)} custom-call(bf16[32,1024]{1,0:T(8,128)(2,1)} %copy-done.6, bf16[32,1024]{1,0:T(8,128)(2,1)} %bitcast.29, bf16[32,1024]{1,0:T(8,128)(2,1)} %copy-done.7, bf16[256,1024]{1,0:T(8,128)(2,1)} %bitcast.19, f32[8,128]{1,0:T(8,128)} %get-tuple-element.17.after_ref), custom_call_target="tpu_custom_call" | custom-call | flops 469762048 | bytes 917504 | tf_op jit(solution)/shard_map/pallas_call | solution.py:237
  30.1 10.1 %all-to-all-start.1 = ((f32[16,56,256]{2,1,0:T(8,128)}), f32[16,56,256]{2,1,0:T(8,128)S(1)}, u32[]{:S(2)}, u32[]{:S(2)}) async-start(f32[16,56,256]{2,1,0:T(8,128)} %bitcast.25), calls=%async_computation.1 | async-start | bytes 1835008 | tf_op jit(solution)/shard_map/all_to_all | solution.py:31
  40.2 13.3 %all_gather.3.vol_ref = bf16[256,1024]{1,0:T(8,128)(2,1)S(1)} all-gather(bf16[32,1024]{1,0:T(8,128)(2,1)} %bitcast.30), channel_id=1, replica_groups=mesh['space'=128,'chan'=8] {'chan'}, dimensions={0}, use_global_device_ids=true | all-gather | bytes 589824 | tf_op jit(solution)/shard_map/all_gather | solution.py:336
  53.5 0.0 copy-done.3
  53.5 0.0 copy-done.4
  53.5 0.0 copy-start.1
  53.5 1.0 copy-done.1
  54.5 1.2 shard_map.60
  55.7 5.8 %all-to-all-done.1.pieces_ref = f32[16,56,256]{2,1,0:T(8,128)S(1)} async-done(((f32[16,56,256]{2,1,0:T(8,128)}), f32[16,56,256]{2,1,0:T(8,128)S(1)}, u32[]{:S(2)}, u32[]{:S(2)}) %all-to-all-start.1) | async-done | bytes 917536 | tf_op jit(solution)/shard_map/all_to_all | solution.py:31
  61.5 45.9 %psum.7.after_ref.piece_ref = f32[56,256]{1,0:T(8,128)} all-reduce(f32[56,256]{1,0:T(8,128)S(1)} %shard_map.62), channel_id=1, replica_groups={{0,32,64,96,128,160,192,224},{8,40,72,104,136,168,200,232},{16,48,80,11..., use_global_device_ids=true, to_apply=%region_0.0 | all-reduce | flops 14336 | bytes 114688 | tf_op jit(solution)/shard_map/psum | solution.py:338
  107.4 1.9 %shard_map.64 = f32[16,56,256]{2,1,0:T(8,128)} custom-call(f32[56,256]{1,0:T(8,128)} %psum.7.after_ref.piece_ref), custom_call_target="tpu_custom_call" | custom-call | tf_op jit(solution)/shard_map/pallas_call | solution.py:142
  109.3 7.4 %all-to-all-start.2 = ((f32[16,56,256]{2,1,0:T(8,128)}), f32[16,56,256]{2,1,0:T(8,128)S(1)}, u32[]{:S(2)}, u32[]{:S(2)}) async-start(f32[16,56,256]{2,1,0:T(8,128)} %shard_map.64), calls=%async_computation.2 | async-start | bytes 1835008 | tf_op jit(solution)/shard_map/all_to_all | solution.py:31
  116.7 3.4 %collective-permute-start = (f32[64,1024]{1,0:T(8,128)S(1)}, f32[64,1024]{1,0:T(8,128)S(1)}, u32[]{:S(2)}, u32[]{:S(2)}) collective-permute-start(f32[64,1024]{1,0:T(8,128)S(1)} %get-tuple-element.15), channel_id=1, source_target_pairs={{0,8},{8,16},{16,24},{24,32},{32,40},{40,48},{48,56},{56,64},{64,7... | collective-permute-start | bytes 786440 | tf_op jit(solution)/shard_map/ppermute | solution.py:342
  120.1 2.5 %collective-permute-start.1 = (f32[64,1024]{1,0:T(8,128)S(1)}, f32[64,1024]{1,0:T(8,128)S(1)}, u32[]{:S(2)}, u32[]{:S(2)}) collective-permute-start(f32[64,1024]{1,0:T(8,128)S(1)} %get-tuple-element.16), channel_id=1, source_target_pairs={{8,0},{16,8},{24,16},{32,24},{40,32},{48,40},{56,48},{64,56},{72,6... | collective-permute-start | bytes 786440 | tf_op jit(solution)/shard_map/ppermute | solution.py:343
  122.6 11.3 %collective-permute-done.low_ref = f32[64,1024]{1,0:T(8,128)S(1)} collective-permute-done((f32[64,1024]{1,0:T(8,128)S(1)}, f32[64,1024]{1,0:T(8,128)S(1)}, u32[]{:S(2)}, u32[]{:S(2)}) %collective-permute-start) | collective-permute-done | bytes 262176 | tf_op jit(solution)/shard_map/ppermute | solution.py:342
  133.9 2.1 %collective-permute-done.1.high_ref = f32[64,1024]{1,0:T(8,128)S(1)} collective-permute-done((f32[64,1024]{1,0:T(8,128)S(1)}, f32[64,1024]{1,0:T(8,128)S(1)}, u32[]{:S(2)}, u32[]{:S(2)}) %collective-permute-start.1) | collective-permute-done | bytes 262176 | tf_op jit(solution)/shard_map/ppermute | solution.py:343
  136.0 0.0 copy-start.2
  136.0 0.8 copy-done.2
  136.8 0.9 shard_map.63
  137.6 0.0 all-to-all-done.2
  137.6 1.0 slice.4
  (1 shorter events, 0.0 us)
Async XLA Ops:
  2.5 24.0 %all-to-all-start = ((bf16[8,32,1024]{2,1,0:T(8,128)(2,1)}), bf16[8,32,1024]{2,1,0:T(8,128)(2,1)S(1)}, u32[]{:S(2)}, u32[]{:S(2)}) async-start(bf16[8,32,1024]{2,1,0:T(8,128)(2,1)} %shard_map.59), calls=%async_computation | async-start | bytes 1048576 | tf_op jit(solution)/shard_map/all_to_all | solution.py:31
  8.1 18.4 %copy-start.5 = (bf16[4,8,8,128]{3,1,2,0:T(8,128)(2,1)}, bf16[4,8,8,128]{3,1,2,0:T(8,128)(2,1)S(1)}, u32[]{:S(2)}) copy-start(bf16[4,8,8,128]{3,1,2,0:T(8,128)(2,1)S(1)} %copy.10) | copy-start | bytes 196612
  8.1 18.3 %collective-permute-start.2 = (bf16[32,1024]{1,0:T(8,128)(2,1)S(1)}, bf16[32,1024]{1,0:T(8,128)(2,1)S(1)}, u32[]{:S(2)}, u32[]{:S(2)}) collective-permute-start(bf16[32,1024]{1,0:T(8,128)(2,1)S(1)} %bitcast.27), channel_id=1, source_target_pairs={{0,8},{8,16},{16,24},{24,32},{32,40},{40,48},{48,56},{56,64},{64,7... | collective-permute-start | bytes 196616 | tf_op jit(solution)/shard_map/ppermute | solution.py:328
  12.0 14.5 %collective-permute-start.3 = (bf16[32,1024]{1,0:T(8,128)(2,1)S(1)}, bf16[32,1024]{1,0:T(8,128)(2,1)S(1)}, u32[]{:S(2)}, u32[]{:S(2)}) collective-permute-start(bf16[32,1024]{1,0:T(8,128)(2,1)S(1)} %bitcast.28), channel_id=1, source_target_pairs={{8,0},{16,8},{24,16},{32,24},{40,32},{48,40},{56,48},{64,56},{72,6... | collective-permute-start | bytes 196616 | tf_op jit(solution)/shard_map/ppermute | solution.py:329
  26.4 27.0 %copy-start.3 = (bf16[27,32,256]{2,1,0:T(8,128)(2,1)S(1)}, bf16[27,32,256]{2,1,0:T(8,128)(2,1)}, u32[]{:S(2)}) copy-start(bf16[27,32,256]{2,1,0:T(8,128)(2,1)} %get-tuple-element.12) | copy-start | bytes 1327108
  26.5 27.0 %copy-start.4 = (bf16[27,32,256]{2,1,0:T(8,128)(2,1)S(1)}, bf16[27,32,256]{2,1,0:T(8,128)(2,1)}, u32[]{:S(2)}) copy-start(bf16[27,32,256]{2,1,0:T(8,128)(2,1)} %get-tuple-element.13) | copy-start | bytes 1327108
  26.5 0.6 copy-start.6
  26.5 0.6 copy-start.7
  26.5 0.8 copy-start
  30.1 31.4 %all-to-all-start.1 = ((f32[16,56,256]{2,1,0:T(8,128)}), f32[16,56,256]{2,1,0:T(8,128)S(1)}, u32[]{:S(2)}, u32[]{:S(2)}) async-start(f32[16,56,256]{2,1,0:T(8,128)} %bitcast.25), calls=%async_computation.1 | async-start | bytes 1835008 | tf_op jit(solution)/shard_map/all_to_all | solution.py:31
  53.5 1.0 copy-start.1
  109.3 28.3 %all-to-all-start.2 = ((f32[16,56,256]{2,1,0:T(8,128)}), f32[16,56,256]{2,1,0:T(8,128)S(1)}, u32[]{:S(2)}, u32[]{:S(2)}) async-start(f32[16,56,256]{2,1,0:T(8,128)} %shard_map.64), calls=%async_computation.2 | async-start | bytes 1835008 | tf_op jit(solution)/shard_map/all_to_all | solution.py:31
  116.7 17.2 %collective-permute-start = (f32[64,1024]{1,0:T(8,128)S(1)}, f32[64,1024]{1,0:T(8,128)S(1)}, u32[]{:S(2)}, u32[]{:S(2)}) collective-permute-start(f32[64,1024]{1,0:T(8,128)S(1)} %get-tuple-element.15), channel_id=1, source_target_pairs={{0,8},{8,16},{16,24},{24,32},{32,40},{40,48},{48,56},{56,64},{64,7... | collective-permute-start | bytes 786440 | tf_op jit(solution)/shard_map/ppermute | solution.py:342
  120.1 15.9 %collective-permute-start.1 = (f32[64,1024]{1,0:T(8,128)S(1)}, f32[64,1024]{1,0:T(8,128)S(1)}, u32[]{:S(2)}, u32[]{:S(2)}) collective-permute-start(f32[64,1024]{1,0:T(8,128)S(1)} %get-tuple-element.16), channel_id=1, source_target_pairs={{8,0},{16,8},{24,16},{32,24},{40,32},{48,40},{56,48},{64,56},{72,6... | collective-permute-start | bytes 786440 | tf_op jit(solution)/shard_map/ppermute | solution.py:343
  136.0 0.8 copy-start.2

commit v5 on v4

v5 whole, which is shorter than its diff:
```python
import math

import jax
import jax.numpy as jnp
from jax import lax
from jax.experimental import pallas as pl
from jax.experimental.pallas import tpu as pltpu
from jax.sharding import PartitionSpec as P

TAPS = 27
Y_CHIPS = 4
NEAR = 4


def groups_of(count):
    length = count // Y_CHIPS
    far = length // NEAR
    along_y = [[y * length + z for y in range(Y_CHIPS)] for z in range(length)]
    near_z = [[hop * NEAR + k for k in range(NEAR)] for hop in range(count // NEAR)]
    block = [
        [y * length + hop * NEAR + k for y in range(Y_CHIPS) for k in range(NEAR)]
        for hop in range(far)
    ]
    far_z = [
        [y * length + hop * NEAR + k for hop in range(far)]
        for y in range(Y_CHIPS)
        for k in range(NEAR)
    ]
    return along_y, near_z, block, far_z


def exchange(pieces, axis, groups=None):
    return lax.all_to_all(pieces, axis, 0, 0, tiled=True, axis_index_groups=groups)


VMEM = pl.BlockSpec(memory_space=pltpu.VMEM)
HBM = pl.BlockSpec(memory_space=pl.ANY)


def limits(mib=56):
    return pltpu.CompilerParams(vmem_limit_bytes=mib * 1024 * 1024)


TOKEN = jax.ShapeDtypeStruct((8, 128), jnp.float32)


def own_weights(kernel, count):
    channels = kernel.shape[2]
    width = min(channels, 128)
    per = width // count

    def body(kernel_ref, fore, back, token, block, sems):
        token[...] = jnp.zeros(token.shape, token.dtype)
        member = lax.axis_index("chan")
        lanes = pl.ds(pl.multiple_of((member // per) * width, width), width)
        rows = pl.ds(pl.multiple_of(member * count, count), count)
        moves = [
            pltpu.make_async_copy(kernel_ref.at[:, :, lanes], block, sems.at[0]),
            pltpu.make_async_copy(kernel_ref.at[:, rows, :], back, sems.at[1]),
        ]
        for move in moves:
            move.start()
        at = lax.broadcasted_iota(jnp.int32, (count, width), 1)
        row = lax.broadcasted_iota(jnp.int32, (count, width), 0)
        pick = jnp.where(at == row + (member % per) * count, 1.0, 0.0).astype(fore.dtype)
        moves[0].wait()
        for tap in range(TAPS):
            fore[tap] = lax.dot_general(
                pick, block[tap], (((1,), (1,)), ((), ())), preferred_element_type=jnp.float32
            ).astype(fore.dtype)
        moves[1].wait()

    shape = jax.ShapeDtypeStruct((TAPS, count, channels), kernel.dtype)
    return pl.pallas_call(
        body,
        out_shape=(shape, shape, TOKEN),
        in_specs=[HBM],
        out_specs=(VMEM, VMEM, VMEM),
        scratch_shapes=[
            pltpu.VMEM((TAPS, channels, width), kernel.dtype),
            pltpu.SemaphoreType.DMA((2,)),
        ],
        compiler_params=limits(),
    )(kernel)


def flat(block, after):
    count, height, breadth = block.shape

    def body(block_ref, after_ref, out, wide, narrow, sem):
        wide[...] = block_ref[...].astype(jnp.float32)
        for q in range(height):
            narrow[:, q * breadth : (q + 1) * breadth] = wide[:, q, :].astype(narrow.dtype)
        move = pltpu.make_async_copy(narrow, out, sem)
        move.start()
        move.wait()

    shape = (count, height * breadth)
    return pl.pallas_call(
        body,
        out_shape=jax.ShapeDtypeStruct(shape, block.dtype),
        in_specs=[VMEM, HBM],
        out_specs=HBM,
        scratch_shapes=[
            pltpu.VMEM(block.shape, jnp.float32),
            pltpu.VMEM(shape, block.dtype),
            pltpu.SemaphoreType.DMA,
        ],
        compiler_params=limits(),
    )(block, after)


def stacked(first, second, copies, after):
    count, cells = first.shape

    def body(first_ref, second_ref, after_ref, out, sems):
        moves = []
        for k in range(copies):
            for half, source in enumerate((first_ref, second_ref)):
                rows = pl.ds(half * count, count)
                moves.append(
                    pltpu.make_async_copy(source, out.at[k, rows], sems.at[2 * k + half])
                )
        for move in moves:
            move.start()
        for move in moves:
            move.wait()

    return pl.pallas_call(
        body,
        out_shape=jax.ShapeDtypeStruct((copies, 2 * count, cells), first.dtype),
        in_specs=[VMEM, VMEM, HBM],
        out_specs=HBM,
        scratch_shapes=[pltpu.SemaphoreType.DMA((2 * copies,))],
        compiler_params=limits(),
    )(first, second, after)


def sum_pieces(pieces, after):
    count, rows, columns = pieces.shape

    def body(pieces_ref, after_ref, out):
        total = pieces_ref[0]
        for k in range(1, count):
            total = total + pieces_ref[k]
        out[...] = total

    return pl.pallas_call(
        body,
        out_shape=jax.ShapeDtypeStruct((rows, columns), pieces.dtype),
        in_specs=[VMEM, VMEM],
        out_specs=VMEM,
        compiler_params=limits(8),
        cost_estimate=pl.CostEstimate(
            flops=pieces.size, bytes_accessed=4 * pieces.size, transcendentals=0
        ),
    )(pieces, after)


def repeated(piece, copies, after):
    def body(piece_ref, after_ref, out, sems):
        moves = [pltpu.make_async_copy(piece_ref, out.at[k], sems.at[k]) for k in range(copies)]
        for move in moves:
            move.start()
        for move in moves:
            move.wait()

    return pl.pallas_call(
        body,
        out_shape=jax.ShapeDtypeStruct((copies,) + piece.shape, piece.dtype),
        in_specs=[VMEM, HBM],
        out_specs=HBM,
        scratch_shapes=[pltpu.SemaphoreType.DMA((copies,))],
        compiler_params=limits(),
    )(piece, after)


def finish(own, low, high, height, breadth, dtype, after):
    rows = own.shape[0]
    count = rows // 2

    def body(own_ref, low_ref, high_ref, after_ref, first, second, wide):
        for q in range(height):
            lanes = pl.ds(q * breadth, breadth)
            wide[:, q, :] = own_ref[:, lanes] + low_ref[:, lanes] + high_ref[:, lanes]
        first[...] = wide[:count].astype(dtype)
        second[...] = wide[count:].astype(dtype)

    shape = jax.ShapeDtypeStruct((count, height, breadth), dtype)
    return pl.pallas_call(
        body,
        out_shape=(shape, shape),
        in_specs=[VMEM] * 3 + [HBM],
        out_specs=(VMEM, VMEM),
        scratch_shapes=[pltpu.VMEM((rows, height, breadth), jnp.float32)],
        compiler_params=limits(8),
    )(own, low, high, after)


def shift_lanes(value, offset, lanes):
    if offset == 0:
        return value
    at = lax.broadcasted_iota(jnp.int32, value.shape, 1)
    if offset < 0:
        return jnp.where(at == 0, 0.0, pltpu.roll(value, 1, 1))
    return jnp.where(at == lanes - 1, 0.0, pltpu.roll(value, lanes - 1, 1))


def weight_terms(planes, field, vol, cot, factor, height, breadth):
    run, double, cells = planes.shape
    count = double // 2
    share = count // run
    parts = field.shape[0] // count
    outs = parts * share
    group = 9 * count
    wide = -(-group // 128) * 128
    columns = -(-3 * group // 128) * 128

    def body(planes_ref, field_ref, vol_ref, cot_ref, out, both, stack, spots, held, sems):
        moves = [
            pltpu.make_async_copy(vol_ref, both.at[pl.ds(0, count)], sems.at[0]),
            pltpu.make_async_copy(cot_ref, both.at[pl.ds(count, count)], sems.at[1]),
            pltpu.make_async_copy(held, out, sems.at[2]),
        ]
        moves[0].start()
        moves[1].start()
        sources = [(0, count)] + [(k, 0) for k in range(run)] + [(run - 1, count)]
        for m, (k, start) in enumerate(sources):
            for q in range(height):
                lanes = slice(q * breadth, (q + 1) * breadth)
                row = planes_ref[k, start : start + count, lanes].astype(jnp.float32)
                for c in range(3):
                    at = (m * 3 + c) * count
                    stack[at : at + count, lanes] = shift_lanes(row, c - 1, breadth).astype(
                        stack.dtype
                    )
        used = 3 * (run + 2) * count
        stack[used:, :] = jnp.zeros((stack.shape[0] - used, cells), stack.dtype)

        for part in range(parts):
            rows = field_ref[part * count : (part + 1) * count, :].astype(jnp.float32)
            for p in range(run):
                own = rows[p * share : (p + 1) * share, :]
                at = part * share
                spots[p, outs + at : outs + at + share, :] = own
                spots[p, at : at + share, : cells - breadth] = own[:, breadth:]
                spots[p, 2 * outs + at : 2 * outs + at + share, breadth:] = own[:, : cells - breadth]
        for p in range(run):
            edge = jnp.zeros((outs, breadth), spots.dtype)
            spots[p, :outs, cells - breadth :] = edge
            spots[p, 2 * outs :, :breadth] = edge

        total = None
        for p in range(run):
            part = lax.dot_general(
                spots[p].astype(stack.dtype),
                stack[3 * p * count : 3 * p * count + wide, :],
                (((1,), (1,)), ((), ())),
                preferred_element_type=jnp.float32,
            )
            total = part if total is None else total + part
        at = lax.broadcasted_iota(jnp.int32, total.shape, 1)
        total = jnp.where(at < group, total * factor, 0.0)
        held[...] = jnp.zeros(held.shape, held.dtype)
        for b in range(3):
            start = b * group // 128 * 128
            shift = b * group - start
            rows = total[b * outs : (b + 1) * outs, :]
            if shift:
                rows = pltpu.roll(rows, shift, 1)
            held[:, start : start + wide] = held[:, start : start + wide] + rows
        moves[2].start()
        for move in moves:
            move.wait()

    return pl.pallas_call(
        body,
        out_shape=(
            jax.ShapeDtypeStruct((outs, columns), jnp.float32),
            jax.ShapeDtypeStruct((double, cells), planes.dtype),
        ),
        in_specs=[VMEM] * 4,
        out_specs=(HBM, HBM),
        scratch_shapes=[
            pltpu.VMEM((3 * (run - 1) * count + wide, cells), planes.dtype),
            pltpu.VMEM((run, 3 * outs, cells), jnp.float32),
            pltpu.VMEM((outs, columns), jnp.float32),
            pltpu.SemaphoreType.DMA((3,)),
        ],
        compiler_params=limits(32),
        cost_estimate=pl.CostEstimate(
            flops=2 * run * 3 * outs * wide * cells,
            bytes_accessed=4 * outs * columns,
            transcendentals=0,
        ),
    )(planes, field, vol, cot)


def in_order(pieces, count, parts):
    amount, rows, columns = pieces.shape
    run = amount // Y_CHIPS
    share = count // run
    holders = rows // share
    channels = count * parts
    group = 3 * count

    def body(pieces_ref, out, tall, turned, sems):
        for holder in range(parts):
            for k in range(run):
                at = holder * count + k * share
                start = holder % holders * share
                tall[at : at + share, :] = pieces_ref[
                    holder // holders * run + k, start : start + share, :
                ]
        for tile in range(columns // 128):
            lanes = slice(tile * 128, (tile + 1) * 128)
            turned[lanes, :] = tall[:, lanes].T
        moves = []
        for a in range(3):
            for b in range(3):
                moves.append(
                    pltpu.make_async_copy(
                        turned.at[pl.ds((b * 3 + a) * group, group)],
                        out.at[pl.ds((a * 3 + b) * group, group)],
                        sems.at[a * 3 + b],
                    )
                )
        for move in moves:
            move.start()
        for move in moves:
            move.wait()

    return pl.pallas_call(
        body,
        out_shape=jax.ShapeDtypeStruct((9 * group, channels), pieces.dtype),
        in_specs=[VMEM],
        out_specs=HBM,
        scratch_shapes=[
            pltpu.VMEM((channels, columns), pieces.dtype),
            pltpu.VMEM((columns, channels), pieces.dtype),
            pltpu.SemaphoreType.DMA((9,)),
        ],
        compiler_params=limits(32),
    )(pieces)


def conv_terms(weights, field, mirror, height, breadth, own, up, down):
    count = weights.shape[1] // 9
    places = (down, own, up) if mirror else (up, own, down)
    for a in range(3):
        part = lax.dot_general(
            weights[a],
            field[...],
            (((1,), (0,)), ((), ())),
            preferred_element_type=jnp.float32,
        )
        for q in range(height):
            total = None
            for c in range(3):
                column = None
                for b in range(3):
                    source = q + (1 - b if mirror else b - 1)
                    if 0 <= source < height:
                        at = (b * 3 + c) * count
                        term = part[at : at + count, source * breadth : (source + 1) * breadth]
                        column = term if column is None else column + term
                moved = shift_lanes(column, 1 - c if mirror else c - 1, breadth)
                total = moved if total is None else total + moved
            places[a][:, q * breadth : (q + 1) * breadth] = total


def plane_terms(fore, back, fields, after, height, breadth):
    count = fore.shape[1] // 9
    parts, _, cells = fields.shape

    def body(fore_ref, back_ref, fields_ref, after_ref, own, up, down, vol, cot):
        for part in range(parts):
            rows = pl.ds(part * count, count)
            vol[rows, :] = fields_ref[part, :count, :]
            cot[rows, :] = fields_ref[part, count:, :]
        halves = [pl.ds(0, count), pl.ds(count, count)]
        conv_terms(
            fore_ref, vol, False, height, breadth, *(r.at[halves[0]] for r in (own, up, down))
        )
        conv_terms(
            back_ref, cot, True, height, breadth, *(r.at[halves[1]] for r in (own, up, down))
        )

    shape = jax.ShapeDtypeStruct((2 * count, cells), jnp.float32)
    return pl.pallas_call(
        body,
        out_shape=(shape, shape, shape),
        in_specs=[VMEM, VMEM, VMEM, HBM],
        out_specs=(VMEM, VMEM, VMEM),
        scratch_shapes=[pltpu.VMEM((parts * count, cells), fields.dtype)] * 2,
        compiler_params=limits(12),
        cost_estimate=pl.CostEstimate(
            flops=4 * fore.size * cells,
            bytes_accessed=4 * fore.size + 24 * count * cells,
            transcendentals=0,
        ),
    )(fore, back, fields, after)


def local(volume, kernel, cotangent):
    count, planes, height, breadth = volume.shape
    cells = height * breadth
    channels = kernel.shape[3]
    slabs = lax.axis_size("space")
    parts = lax.axis_size("chan")
    factor = 1.0 / math.sqrt(slabs * planes * cells)
    along_y, near_z, block, far_z = groups_of(slabs)
    up = [(i, i + 1) for i in range(slabs - 1)]
    down = [(i + 1, i) for i in range(slabs - 1)]
    ends = [pair for pair in up if pair[1] % NEAR == 0]
    ends = ends + [(high, low) for low, high in ends]

    cot = flat(cotangent.reshape(count, height, breadth), volume)
    traded = exchange(cot.reshape(NEAR, count // NEAR, cells), "space", near_z)
    vol = flat(volume.reshape(count, height, breadth), cot)
    beyond = lax.ppermute(vol, "space", ends)
    field = lax.all_gather(traded.reshape(count, cells), "chan", axis=0, tiled=True)
    run = exchange(stacked(vol, beyond, NEAR, traded), "space", near_z)

    terms, both = weight_terms(run, field, vol, cot, factor, height, breadth)
    pieces = exchange(terms.reshape(Y_CHIPS, -1, terms.shape[1]), "space", along_y)
    fore, back, ready = own_weights(kernel.reshape(TAPS, channels, channels), count)
    fore = fore.reshape(3, 9 * count, channels)
    back = back.reshape(3, 9 * count, channels)
    fields = lax.all_gather(both, "chan", axis=0)
    total = lax.psum(sum_pieces(pieces, ready), "space", axis_index_groups=far_z)
    whole = exchange(repeated(total, len(block[0]), fields), "space", block)
    weight_grad = in_order(whole, count, parts).reshape(3, 3, 3, count, channels)

    own, upper, lower = plane_terms(fore, back, fields, total, height, breadth)
    from_low = lax.ppermute(upper, "space", up)
    from_high = lax.ppermute(lower, "space", down)
    output, input_grad = finish(own, from_low, from_high, height, breadth, volume.dtype, total)
    return (output.reshape(volume.shape), input_grad.reshape(volume.shape), weight_grad)


def solution(mesh):
    return jax.shard_map(
        local,
        mesh=mesh,
        in_specs=(P("chan", "space", None, None), P(), P("chan", "space", None, None)),
        out_specs=(
            P("chan", "space", None, None),
            P("chan", "space", None, None),
            P(None, None, None, "chan", None),
        ),
        check_vma=False,
    )
```

time: 139 us -> 154 us (1.11)
  the two profiles are of different devices: /device:TPU:38 before, /device:TPU:32 now
where the time goes in v5:
time: 154 us; the launch traced here: 153 us
  blocking collectives  58.1 us (38%)
  starting transfers between devices  44.6 us (29%)
  waiting for transfers between devices  17.8 us (12%)
  Pallas kernels  15.5 us (10%)
  between operations  14.2 us (9%)
  local copies, waits for them, and re-layouts  3.01 us (2%)
    psum x1, blocking collectives, local(): lax.psum(sum_pieces(pieces, ready), 'space', axis_index_groups=far_z)  44.8 us
    all_to_all x4, starting transfers between devices, exchange(): lax.all_to_all(pieces, axis, 0, 0, tiled=True, axis_index_groups=groups)  38.1 us
    all_gather x1, blocking collectives, local(): lax.all_gather(traded.reshape(count, cells), 'chan', axis=0, tiled=True)  13.3 us
    ppermute x1, waiting for transfers between devices, local(): from_low = lax.ppermute(upper, 'space', up)  9.7 us
    all_to_all x4, waiting for transfers between devices, exchange(): lax.all_to_all(pieces, axis, 0, 0, tiled=True, axis_index_groups=groups)  6.01 us
    ppermute x1, starting transfers between devices, local(): from_low = lax.ppermute(upper, 'space', up)  3.37 us
    pallas_call x2, Pallas kernels, flat(): pl.pallas_call(body, out_shape=jax.ShapeDtypeStruct(shape, block.dtype),...  3.24 us
    pallas_call x1, Pallas kernels, own_weights(): pl.pallas_call(body, out_shape=(shape, shape, TOKEN), in_specs=[HBM], out...  3.14 us
  transfers between devices with their start and end apart: 8, of which 4 were waited for; matrix products, arithmetic and copies ran while one was open for 0% of the time, Pallas kernels for 4%

profile of v5, /device:TPU:32, one launch (start us, length us, event | category | flops | bytes accessed | tf_op | source)
XLA Modules:
  0.0 153.2 jit_solution(16262575813667030662)
XLA Ops:
  7.2 1.6 %shard_map.59.after_ref.cot_ref = bf16[32,1024]{1,0:T(8,128)(2,1)} custom-call(bf16[32,8,128]{2,1,0:T(8,128)(2,1)} %bitcast.25, bf16[32,1,8,128]{3,2,1,0:T(8,128)(2,1)} %after_ref.1), custom_call_target="tpu_custom_call" | custom-call | tf_op jit(solution)/shard_map/pallas_call | solution.py:99
  8.8 16.0 %all-to-all-start = ((bf16[4,8,1024]{2,1,0:T(8,128)(2,1)}), bf16[4,8,1024]{2,1,0:T(8,128)(2,1)S(1)}, u32[]{:S(2)}, u32[]{:S(2)}) async-start(bf16[4,8,1024]{2,1,0:T(8,128)(2,1)} %bitcast.18), calls=%async_computation | async-start | bytes 131072 | tf_op jit(solution)/shard_map/all_to_all | solution.py:33
  24.8 1.6 %shard_map.60.first_ref.vol_ref = bf16[32,1024]{1,0:T(8,128)(2,1)} custom-call(bf16[32,8,128]{2,1,0:T(8,128)(2,1)} %bitcast.24, bf16[32,1024]{1,0:T(8,128)(2,1)} %shard_map.59.after_ref.cot_ref), custom_call_target="tpu_custom_call" | custom-call | tf_op jit(solution)/shard_map/pallas_call | solution.py:99
  26.4 0.7 collective-permute-start
  27.1 0.0 collective-permute-done.second_ref
  27.1 0.0 copy-start.8
  27.1 2.3 %all-to-all-done.after_ref = bf16[4,8,1024]{2,1,0:T(8,128)(2,1)S(1)} async-done(((bf16[4,8,1024]{2,1,0:T(8,128)(2,1)}), bf16[4,8,1024]{2,1,0:T(8,128)(2,1)S(1)}, u32[]{:S(2)}, u32[]{:S(2)}) %all-to-all-start) | async-done | bytes 65568 | tf_op jit(solution)/shard_map/all_to_all | solution.py:33
  29.5 0.0 copy-done.8
  29.5 0.0 copy-start.7
  29.5 0.6 copy-done.7
  30.1 1.7 %shard_map.61 = bf16[4,64,1024]{2,1,0:T(8,128)(2,1)} custom-call(bf16[32,1024]{1,0:T(8,128)(2,1)} %shard_map.60.first_ref.vol_ref, bf16[32,1024]{1,0:T(8,128)(2,1)} %copy-done.8, bf16[4,8,1024]{2,1,0:T(8,128)(2,1)} %copy-done.7), custom_call_target="tpu_custom_call" | custom-call | tf_op jit(solution)/shard_map/pallas_call | solution.py:129
  31.8 10.3 %all-to-all-start.1 = ((bf16[4,64,1024]{2,1,0:T(8,128)(2,1)}), bf16[4,64,1024]{2,1,0:T(8,128)(2,1)S(1)}, u32[]{:S(2)}, u32[]{:S(2)}) async-start(bf16[4,64,1024]{2,1,0:T(8,128)(2,1)} %shard_map.61), calls=%async_computation.1 | async-start | bytes 1048576 | tf_op jit(solution)/shard_map/all_to_all | solution.py:33
  42.1 0.0 all-gather.3.cloned.1.call-start
  42.1 13.3 %all_gather.9.field_ref = bf16[256,1024]{1,0:T(8,128)(2,1)S(1)} all-gather(bf16[32,1024]{1,0:T(8,128)(2,1)} %bitcast.23), channel_id=1, replica_groups=mesh['space'=128,'chan'=8] {'chan'}, dimensions={0}, use_global_device_ids=true | all-gather | bytes 589824 | tf_op jit(solution)/shard_map/all_gather | solution.py:422
  55.4 0.0 all-to-all-done.1.planes_ref
  55.4 0.0 copy-start.1
  55.4 0.8 copy-done.1
  56.3 0.0 copy-start.3
  56.3 0.8 copy-done.3
  57.1 2.1 %shard_map.62 = (f32[64,896]{1,0:T(8,128)}, bf16[64,1024]{1,0:T(8,128)(2,1)}) custom-call(bf16[4,64,1024]{2,1,0:T(8,128)(2,1)S(1)} %all-to-all-done.1.planes_ref, bf16[256,1024]{1,0:T(8,128)(2,1)S(1)} %all_gather.9.field_ref, bf16[32,1024]{1,0:T(8,128)(2,1)S(1)} %copy-done.3, bf16[32,1024]{1,0:T(8,128)(2,1)S(1)} %copy-done.1), custom_call_target="tpu_custom_call" | custom-call | flops 603979776 | bytes 229376 | tf_op jit(solution)/shard_map/pallas_call | solution.py:276
  59.2 0.0 all-gather.3.cloned.1.call-update
  59.2 6.0 %all-to-all-start.2 = ((f32[4,16,896]{2,1,0:T(8,128)}), f32[4,16,896]{2,1,0:T(8,128)S(1)}, u32[]{:S(2)}, u32[]{:S(2)}) async-start(f32[4,16,896]{2,1,0:T(8,128)} %bitcast.8), calls=%async_computation.2 | async-start | bytes 458752 | tf_op jit(solution)/shard_map/all_to_all | solution.py:33
  65.2 3.1 %shard_map.58 = (bf16[27,32,256]{2,1,0:T(8,128)(2,1)}, bf16[27,32,256]{2,1,0:T(8,128)(2,1)}, f32[8,128]{1,0:T(8,128)}) custom-call(bf16[27,256,256]{2,1,0:T(8,128)(2,1)} %bitcast.21), custom_call_target="tpu_custom_call" | custom-call | tf_op jit(solution)/shard_map/pallas_call | solution.py:74
  68.3 3.7 %all-to-all-done.2.pieces_ref = f32[4,16,896]{2,1,0:T(8,128)S(1)} async-done(((f32[4,16,896]{2,1,0:T(8,128)}), f32[4,16,896]{2,1,0:T(8,128)S(1)}, u32[]{:S(2)}, u32[]{:S(2)}) %all-to-all-start.2) | async-done | bytes 229408 | tf_op jit(solution)/shard_map/all_to_all | solution.py:33
  72.0 0.0 copy-start.4
  72.0 0.7 copy-done.4
  72.7 0.0 copy-start.5
  72.7 0.0 copy-start.6
  72.7 44.8 %psum.7.after_ref.piece_ref = f32[16,896]{1,0:T(8,128)} all-reduce(f32[16,896]{1,0:T(8,128)S(1)} %shard_map.63), channel_id=1, replica_groups={{0,32,64,96,128,160,192,224},{8,40,72,104,136,168,200,232},{16,48,80,11..., use_global_device_ids=true, to_apply=%region_0.0 | all-reduce | flops 14336 | bytes 114688 | tf_op jit(solution)/shard_map/psum | solution.py:431
  117.5 0.0 copy-start.2
  117.5 0.0 all-gather.3.cloned.1.call-done
  117.5 0.0 copy-start
  117.5 2.0 %shard_map.66 = f32[16,16,896]{2,1,0:T(8,128)} custom-call(f32[16,896]{1,0:T(8,128)} %psum.7.after_ref.piece_ref, bf16[8,64,1024]{2,1,0:T(8,128)(2,1)} %bitcast.16), custom_call_target="tpu_custom_call" | custom-call | tf_op jit(solution)/shard_map/pallas_call | solution.py:168
  119.5 5.8 %all-to-all-start.3 = ((f32[16,16,896]{2,1,0:T(8,128)}), f32[16,16,896]{2,1,0:T(8,128)S(1)}, u32[]{:S(2)}, u32[]{:S(2)}) async-start(f32[16,16,896]{2,1,0:T(8,128)} %shard_map.66), calls=%async_computation.3 | async-start | bytes 1835008 | tf_op jit(solution)/shard_map/all_to_all | solution.py:33
  125.2 0.0 copy-done.5
  125.3 0.0 copy-done.6
  125.3 0.0 copy-done.2
  125.3 0.0 copy-done
  125.3 1.2 shard_map.64
  126.5 3.4 %collective-permute-start.1 = (f32[64,1024]{1,0:T(8,128)S(1)}, f32[64,1024]{1,0:T(8,128)S(1)}, u32[]{:S(2)}, u32[]{:S(2)}) collective-permute-start(f32[64,1024]{1,0:T(8,128)S(1)} %get-tuple-element.19), channel_id=1, source_target_pairs={{0,8},{8,16},{16,24},{24,32},{32,40},{40,48},{48,56},{56,64},{64,7... | collective-permute-start | bytes 786440 | tf_op jit(solution)/shard_map/ppermute | solution.py:436
  129.9 2.5 %collective-permute-start.2 = (f32[64,1024]{1,0:T(8,128)S(1)}, f32[64,1024]{1,0:T(8,128)S(1)}, u32[]{:S(2)}, u32[]{:S(2)}) collective-permute-start(f32[64,1024]{1,0:T(8,128)S(1)} %get-tuple-element.20), channel_id=1, source_target_pairs={{8,0},{16,8},{24,16},{32,24},{40,32},{48,40},{56,48},{64,56},{72,6... | collective-permute-start | bytes 786440 | tf_op jit(solution)/shard_map/ppermute | solution.py:437
  132.3 9.7 %collective-permute-done.1.low_ref = f32[64,1024]{1,0:T(8,128)S(1)} collective-permute-done((f32[64,1024]{1,0:T(8,128)S(1)}, f32[64,1024]{1,0:T(8,128)S(1)}, u32[]{:S(2)}, u32[]{:S(2)}) %collective-permute-start.1) | collective-permute-done | bytes 262176 | tf_op jit(solution)/shard_map/ppermute | solution.py:436
  142.0 2.1 %collective-permute-done.2.high_ref = f32[64,1024]{1,0:T(8,128)S(1)} collective-permute-done((f32[64,1024]{1,0:T(8,128)S(1)}, f32[64,1024]{1,0:T(8,128)S(1)}, u32[]{:S(2)}, u32[]{:S(2)}) %collective-permute-start.2) | collective-permute-done | bytes 262176 | tf_op jit(solution)/shard_map/ppermute | solution.py:437
  144.2 0.9 shard_map.65
  145.0 0.0 all-to-all-done.3.pieces_ref
  145.0 1.3 shard_map.67
  (1 shorter events, 0.0 us)
Async XLA Ops:
  8.8 20.7 %all-to-all-start = ((bf16[4,8,1024]{2,1,0:T(8,128)(2,1)}), bf16[4,8,1024]{2,1,0:T(8,128)(2,1)S(1)}, u32[]{:S(2)}, u32[]{:S(2)}) async-start(bf16[4,8,1024]{2,1,0:T(8,128)(2,1)} %bitcast.18), calls=%async_computation | async-start | bytes 131072 | tf_op jit(solution)/shard_map/all_to_all | solution.py:33
  26.4 0.7 collective-permute-start
  27.1 2.3 %copy-start.8 = (bf16[32,1024]{1,0:T(8,128)(2,1)}, bf16[32,1024]{1,0:T(8,128)(2,1)S(1)}, u32[]{:S(2)}) copy-start(bf16[32,1024]{1,0:T(8,128)(2,1)S(1)} %collective-permute-done.second_ref) | copy-start | bytes 196612
  29.5 0.6 copy-start.7
  31.8 23.6 %all-to-all-start.1 = ((bf16[4,64,1024]{2,1,0:T(8,128)(2,1)}), bf16[4,64,1024]{2,1,0:T(8,128)(2,1)S(1)}, u32[]{:S(2)}, u32[]{:S(2)}) async-start(bf16[4,64,1024]{2,1,0:T(8,128)(2,1)} %shard_map.61), calls=%async_computation.1 | async-start | bytes 1048576 | tf_op jit(solution)/shard_map/all_to_all | solution.py:33
  42.1 75.4 %all-gather.3.cloned.1.call-start = ((), (), s32[]{:S(2)}) async-start(), calls=%async_computation.4 | async-start | bytes 1179648 | tf_op jit(solution)/shard_map/all_gather | solution.py:430
  55.4 0.8 copy-start.1
  56.3 0.8 copy-start.3
  59.2 12.8 %all-to-all-start.2 = ((f32[4,16,896]{2,1,0:T(8,128)}), f32[4,16,896]{2,1,0:T(8,128)S(1)}, u32[]{:S(2)}, u32[]{:S(2)}) async-start(f32[4,16,896]{2,1,0:T(8,128)} %bitcast.8), calls=%async_computation.2 | async-start | bytes 458752 | tf_op jit(solution)/shard_map/all_to_all | solution.py:33
  72.0 0.7 copy-start.4
  72.7 52.6 %copy-start.5 = (bf16[27,32,256]{2,1,0:T(8,128)(2,1)S(1)}, bf16[27,32,256]{2,1,0:T(8,128)(2,1)}, u32[]{:S(2)}) copy-start(bf16[27,32,256]{2,1,0:T(8,128)(2,1)} %get-tuple-element.13) | copy-start | bytes 1327108
  72.7 52.6 %copy-start.6 = (bf16[27,32,256]{2,1,0:T(8,128)(2,1)S(1)}, bf16[27,32,256]{2,1,0:T(8,128)(2,1)}, u32[]{:S(2)}) copy-start(bf16[27,32,256]{2,1,0:T(8,128)(2,1)} %get-tuple-element.14) | copy-start | bytes 1327108
  117.5 7.8 %copy-start.2 = (f32[16,896]{1,0:T(8,128)S(1)}, f32[16,896]{1,0:T(8,128)}, u32[]{:S(2)}) copy-start(f32[16,896]{1,0:T(8,128)} %psum.7.after_ref.piece_ref) | copy-start | bytes 172036
  117.5 7.8 %copy-start = (bf16[512,1024]{1,0:T(8,128)(2,1)S(1)}, bf16[512,1024]{1,0:T(8,128)(2,1)}, u32[]{:S(2)}) copy-start(bf16[512,1024]{1,0:T(8,128)(2,1)} %all-gather.3.cloned.1.call-done) | copy-start | bytes 3145732
  119.5 25.6 %all-to-all-start.3 = ((f32[16,16,896]{2,1,0:T(8,128)}), f32[16,16,896]{2,1,0:T(8,128)S(1)}, u32[]{:S(2)}, u32[]{:S(2)}) async-start(f32[16,16,896]{2,1,0:T(8,128)} %shard_map.66), calls=%async_computation.3 | async-start | bytes 1835008 | tf_op jit(solution)/shard_map/all_to_all | solution.py:33
  126.5 15.6 %collective-permute-start.1 = (f32[64,1024]{1,0:T(8,128)S(1)}, f32[64,1024]{1,0:T(8,128)S(1)}, u32[]{:S(2)}, u32[]{:S(2)}) collective-permute-start(f32[64,1024]{1,0:T(8,128)S(1)} %get-tuple-element.19), channel_id=1, source_target_pairs={{0,8},{8,16},{16,24},{24,32},{32,40},{40,48},{48,56},{56,64},{64,7... | collective-permute-start | bytes 786440 | tf_op jit(solution)/shard_map/ppermute | solution.py:436
  129.9 14.3 %collective-permute-start.2 = (f32[64,1024]{1,0:T(8,128)S(1)}, f32[64,1024]{1,0:T(8,128)S(1)}, u32[]{:S(2)}, u32[]{:S(2)}) collective-permute-start(f32[64,1024]{1,0:T(8,128)S(1)} %get-tuple-element.20), channel_id=1, source_target_pairs={{8,0},{16,8},{24,16},{32,24},{40,32},{48,40},{56,48},{64,56},{72,6... | collective-permute-start | bytes 786440 | tf_op jit(solution)/shard_map/ppermute | solution.py:437
Sparse Core Ops, SparseCore 0:
  59.3 35.9 all-gather.2

commit v6 on v4

--- a/solution.py
+++ b/solution.py
@@ -131,8 +131,8 @@
     )(pieces, after)
 
 
-def repeated(piece, copies):
-    def body(piece_ref, out, sems):
+def repeated(piece, copies, first, second):
+    def body(piece_ref, first_ref, second_ref, out, sems):
         moves = [pltpu.make_async_copy(piece_ref, out.at[k], sems.at[k]) for k in range(copies)]
         for move in moves:
             move.start()
@@ -142,11 +142,11 @@
     return pl.pallas_call(
         body,
         out_shape=jax.ShapeDtypeStruct((copies,) + piece.shape, piece.dtype),
-        in_specs=[VMEM],
+        in_specs=[VMEM, HBM, HBM],
         out_specs=HBM,
         scratch_shapes=[pltpu.SemaphoreType.DMA((copies,))],
-        compiler_params=limits(),
-    )(piece)
+        compiler_params=limits(32),
+    )(piece, first, second)
 
 
 def finish(own, low, high, height, breadth, dtype, after):
@@ -186,16 +186,7 @@
     group = 3 * count
     rows = 9 * group + count
 
-    def body(low_ref, own_ref, high_ref, cot_ref, after_ref, *rest):
-        out, planes, field, stack, held, in_sems, out_sems = rest
-        sources = (low_ref, own_ref, high_ref)
-        moves = [
-            pltpu.make_async_copy(source, planes.at[k], in_sems.at[k])
-            for k, source in enumerate(sources)
-        ]
-        moves.append(pltpu.make_async_copy(cot_ref, field, in_sems.at[3]))
-        for move in moves:
-            move.start()
+    def body(low_ref, own_ref, high_ref, cot_ref, after_ref, out, stack, held, out_sems):
         sent = []
 
         def send(start, size):
@@ -210,20 +201,18 @@
         edge = jnp.zeros((9 * count, breadth), stack.dtype)
         stack[:, :breadth] = edge
         stack[:, (height + 1) * breadth :] = edge
-        for a in range(3):
-            moves[a].wait()
+        for a, plane in enumerate((low_ref, own_ref, high_ref)):
             for q in range(height):
-                row = planes[a, :, q * breadth : (q + 1) * breadth].astype(jnp.float32)
+                row = plane[:, q * breadth : (q + 1) * breadth].astype(jnp.float32)
                 for c in range(3):
                     at = (a * 3 + c) * count
                     stack[at : at + count, (q + 1) * breadth : (q + 2) * breadth] = shift_lanes(
                         row, c - 1, breadth
                     ).astype(stack.dtype)
-        moves[3].wait()
         for b in range(3):
             part = lax.dot_general(
                 stack[:, b * breadth : b * breadth + cells],
-                field[...],
+                cot_ref[...],
                 (((1,), (1,)), ((), ())),
                 preferred_element_type=jnp.float32,
             )
@@ -237,17 +226,14 @@
     return pl.pallas_call(
         body,
         out_shape=jax.ShapeDtypeStruct((rows, channels), jnp.float32),
-        in_specs=[HBM] * 5,
+        in_specs=[VMEM] * 5,
         out_specs=HBM,
         scratch_shapes=[
-            pltpu.VMEM((3, count, cells), own.dtype),
-            pltpu.VMEM((channels, cells), cot.dtype),
             pltpu.VMEM((9 * count, cells + 2 * breadth), own.dtype),
             pltpu.VMEM((rows, channels), jnp.float32),
-            pltpu.SemaphoreType.DMA((4,)),
             pltpu.SemaphoreType.DMA((10,)),
         ],
-        compiler_params=limits(),
+        compiler_params=limits(32),
         cost_estimate=pl.CostEstimate(
             flops=2 * rows * channels * cells,
             bytes_accessed=4 * rows * channels,
@@ -336,11 +322,12 @@
     vol_all = lax.all_gather(vol, "chan", axis=0, tiled=True)
     own, upper, lower, done = plane_terms(fore, vol_all, back, cot_all, height, breadth)
     total = lax.psum(sum_pieces(pieces, done), "space", axis_index_groups=far_z)
-    whole = exchange(repeated(total, len(block[0])), "space", block).reshape(-1, channels)
-    weight_grad = whole[: TAPS * count].reshape(3, 3, 3, count, channels)
-
     from_low = lax.ppermute(upper, "space", up)
     from_high = lax.ppermute(lower, "space", down)
+    copies = repeated(total, len(block[0]), from_low, from_high)
+    whole = exchange(copies, "space", block).reshape(-1, channels)
+    weight_grad = whole[: TAPS * count].reshape(3, 3, 3, count, channels)
+
     output, input_grad = finish(own, from_low, from_high, height, breadth, volume.dtype, total)
     return (output.reshape(volume.shape), input_grad.reshape(volume.shape), weight_grad)
 

time: 139 us -> 134 us (0.964)
  the two profiles are of different devices: /device:TPU:38 before, /device:TPU:2 now
where the time goes in v6:
time: 134 us
  blocking collectives  58.4 us (44%)
  starting transfers between devices  37.2 us (28%)
  waiting for transfers between devices  25.2 us (19%)
  Pallas kernels  9.71 us (7%)
  local copies, waits for them, and re-layouts  2.51 us (2%)
    psum x1, blocking collectives, local(): total = lax.psum(sum_pieces(pieces, done), 'space', axis_index_groups=far_z)  45.3 us
    all_to_all x3, starting transfers between devices, exchange(): lax.all_to_all(pieces, axis, 0, 0, tiled=True, axis_index_groups=groups)  29.5 us
    all_to_all x3, waiting for transfers between devices, exchange(): lax.all_to_all(pieces, axis, 0, 0, tiled=True, axis_index_groups=groups)  23.6 us
    all_gather x1, blocking collectives, local(): vol_all = lax.all_gather(vol, 'chan', axis=0, tiled=True)  13.1 us
    ppermute x1, starting transfers between devices, local(): from_low = lax.ppermute(upper, 'space', up)  3.83 us
    pallas_call x1, Pallas kernels, own_weights(): pl.pallas_call(body, out_shape=(shape, shape, TOKEN), in_specs=[HBM], out...  3.21 us
  transfers between devices with their start and end apart: 7, of which 4 were waited for; matrix products, arithmetic and copies ran while one was open for 1% of the time, Pallas kernels for 4%

profile of v6, /device:TPU:2, one launch (start us, length us, event | category | flops | bytes accessed | tf_op | source)
XLA Modules:
  0.0 133.8 jit_solution(16874098340231513130)
XLA Ops:
  0.6 1.8 %shard_map.59 = bf16[8,32,1024]{2,1,0:T(8,128)(2,1)} custom-call(bf16[32,8,128]{2,1,0:T(8,128)(2,1)} %bitcast.30), custom_call_target="tpu_custom_call" | custom-call | tf_op jit(solution)/shard_map/pallas_call | solution.py:99
  2.5 16.6 %all-to-all-start = ((bf16[8,32,1024]{2,1,0:T(8,128)(2,1)}), bf16[8,32,1024]{2,1,0:T(8,128)(2,1)S(1)}, u32[]{:S(2)}, u32[]{:S(2)}) async-start(bf16[8,32,1024]{2,1,0:T(8,128)(2,1)} %shard_map.59), calls=%async_computation | async-start | bytes 1048576 | tf_op jit(solution)/shard_map/all_to_all | solution.py:31
  19.1 0.8 copy.10
  19.9 1.3 collective-permute-start.2
  21.2 1.3 collective-permute-start.3
  22.5 3.2 %shard_map.58 = (bf16[27,32,256]{2,1,0:T(8,128)(2,1)}, bf16[27,32,256]{2,1,0:T(8,128)(2,1)}, f32[8,128]{1,0:T(8,128)}) custom-call(bf16[27,256,256]{2,1,0:T(8,128)(2,1)} %bitcast.28), custom_call_target="tpu_custom_call" | custom-call | tf_op jit(solution)/shard_map/pallas_call | solution.py:72
  25.7 0.0 copy-start
  25.8 0.0 copy-start.1
  25.8 0.0 collective-permute-done.2.low_ref
  25.8 1.6 %collective-permute-done.3.high_ref = bf16[32,1024]{1,0:T(8,128)(2,1)S(1)} collective-permute-done((bf16[32,1024]{1,0:T(8,128)(2,1)S(1)}, bf16[32,1024]{1,0:T(8,128)(2,1)S(1)}, u32[]{:S(2)}, u32[]{:S(2)}) %collective-permute-start.3) | collective-permute-done | bytes 65568 | tf_op jit(solution)/shard_map/ppermute | solution.py:315
  27.4 0.6 all-to-all-done
  28.0 0.0 copy-start.2
  28.0 0.7 copy-done.2
  28.7 1.5 %shard_map.61 = f32[896,256]{1,0:T(8,128)} custom-call(bf16[32,1024]{1,0:T(8,128)(2,1)S(1)} %collective-permute-done.2.low_ref, bf16[32,1024]{1,0:T(8,128)(2,1)S(1)} %bitcast.23, bf16[32,1024]{1,0:T(8,128)(2,1)S(1)} %collective-permute-done.3.high_ref, bf16[256,1024]{1,0:T(8,128)(2,1)S(1)} %bitcast.19, f32[8,128]{1,0:T(8,128)S(1)} %copy-done.2), custom_call_target="tpu_custom_call" | custom-call | flops 469762048 | bytes 917504 | tf_op jit(solution)/shard_map/pallas_call | solution.py:226
  30.2 8.7 %all-to-all-start.1 = ((f32[16,56,256]{2,1,0:T(8,128)}), f32[16,56,256]{2,1,0:T(8,128)S(1)}, u32[]{:S(2)}, u32[]{:S(2)}) async-start(f32[16,56,256]{2,1,0:T(8,128)} %bitcast.5), calls=%async_computation.1 | async-start | bytes 1835008 | tf_op jit(solution)/shard_map/all_to_all | solution.py:31
  38.9 13.1 %all_gather.3.vol_ref = bf16[256,1024]{1,0:T(8,128)(2,1)S(1)} all-gather(bf16[32,1024]{1,0:T(8,128)(2,1)S(1)} %bitcast.24), channel_id=1, replica_groups=mesh['space'=128,'chan'=8] {'chan'}, dimensions={0}, use_global_device_ids=true | all-gather | bytes 589824 | tf_op jit(solution)/shard_map/all_gather | solution.py:322
  52.1 0.0 copy-done
  52.1 0.0 copy-done.1
  52.1 1.2 shard_map.60
  53.2 3.8 %collective-permute-start = (f32[64,1024]{1,0:T(8,128)S(1)}, f32[64,1024]{1,0:T(8,128)S(1)}, u32[]{:S(2)}, u32[]{:S(2)}) collective-permute-start(f32[64,1024]{1,0:T(8,128)S(1)} %get-tuple-element.15), channel_id=1, source_target_pairs={{0,8},{8,16},{16,24},{24,32},{32,40},{40,48},{48,56},{56,64},{64,7... | collective-permute-start | bytes 786440 | tf_op jit(solution)/shard_map/ppermute | solution.py:325
  57.1 1.3 collective-permute-start.1
  58.4 5.6 %all-to-all-done.1.pieces_ref = f32[16,56,256]{2,1,0:T(8,128)S(1)} async-done(((f32[16,56,256]{2,1,0:T(8,128)}), f32[16,56,256]{2,1,0:T(8,128)S(1)}, u32[]{:S(2)}, u32[]{:S(2)}) %all-to-all-start.1) | async-done | bytes 917536 | tf_op jit(solution)/shard_map/all_to_all | solution.py:31
  64.0 45.3 %psum.7.after_ref.piece_ref = f32[56,256]{1,0:T(8,128)S(1)} all-reduce(f32[56,256]{1,0:T(8,128)S(1)} %shard_map.62), channel_id=1, replica_groups={{0,32,64,96,128,160,192,224},{8,40,72,104,136,168,200,232},{16,48,80,11..., use_global_device_ids=true, to_apply=%region_0.0 | all-reduce | flops 14336 | bytes 114688 | tf_op jit(solution)/shard_map/psum | solution.py:324
  109.3 0.0 collective-permute-done.low_ref.first_ref
  109.3 0.0 collective-permute-done.1.high_ref.second_ref
  109.3 1.1 shard_map.64
  110.4 4.2 %all-to-all-start.2 = ((f32[16,56,256]{2,1,0:T(8,128)}), f32[16,56,256]{2,1,0:T(8,128)S(1)}, u32[]{:S(2)}, u32[]{:S(2)}) async-start(f32[16,56,256]{2,1,0:T(8,128)} %shard_map.64), calls=%async_computation.2 | async-start | bytes 1835008 | tf_op jit(solution)/shard_map/all_to_all | solution.py:31
  114.6 0.9 shard_map.63
  115.4 17.4 %all-to-all-done.2 = f32[16,56,256]{2,1,0:T(8,128)S(1)} async-done(((f32[16,56,256]{2,1,0:T(8,128)}), f32[16,56,256]{2,1,0:T(8,128)S(1)}, u32[]{:S(2)}, u32[]{:S(2)}) %all-to-all-start.2) | async-done | bytes 917536 | tf_op jit(solution)/shard_map/all_to_all | solution.py:31
  132.8 1.0 slice.4
  (1 shorter events, 0.0 us)
Async XLA Ops:
  2.5 25.5 %all-to-all-start = ((bf16[8,32,1024]{2,1,0:T(8,128)(2,1)}), bf16[8,32,1024]{2,1,0:T(8,128)(2,1)S(1)}, u32[]{:S(2)}, u32[]{:S(2)}) async-start(bf16[8,32,1024]{2,1,0:T(8,128)(2,1)} %shard_map.59), calls=%async_computation | async-start | bytes 1048576 | tf_op jit(solution)/shard_map/all_to_all | solution.py:31
  19.9 5.8 %collective-permute-start.2 = (bf16[32,1024]{1,0:T(8,128)(2,1)S(1)}, bf16[32,1024]{1,0:T(8,128)(2,1)S(1)}, u32[]{:S(2)}, u32[]{:S(2)}) collective-permute-start(bf16[32,1024]{1,0:T(8,128)(2,1)S(1)} %bitcast.21), channel_id=1, source_target_pairs={{0,8},{8,16},{16,24},{24,32},{32,40},{40,48},{48,56},{56,64},{64,7... | collective-permute-start | bytes 196616 | tf_op jit(solution)/shard_map/ppermute | solution.py:314
  21.2 6.2 %collective-permute-start.3 = (bf16[32,1024]{1,0:T(8,128)(2,1)S(1)}, bf16[32,1024]{1,0:T(8,128)(2,1)S(1)}, u32[]{:S(2)}, u32[]{:S(2)}) collective-permute-start(bf16[32,1024]{1,0:T(8,128)(2,1)S(1)} %bitcast.22), channel_id=1, source_target_pairs={{8,0},{16,8},{24,16},{32,24},{40,32},{48,40},{56,48},{64,56},{72,6... | collective-permute-start | bytes 196616 | tf_op jit(solution)/shard_map/ppermute | solution.py:315
  25.7 26.3 %copy-start = (bf16[27,32,256]{2,1,0:T(8,128)(2,1)S(1)}, bf16[27,32,256]{2,1,0:T(8,128)(2,1)}, u32[]{:S(2)}) copy-start(bf16[27,32,256]{2,1,0:T(8,128)(2,1)} %get-tuple-element.12) | copy-start | bytes 1327108
  25.8 26.3 %copy-start.1 = (bf16[27,32,256]{2,1,0:T(8,128)(2,1)S(1)}, bf16[27,32,256]{2,1,0:T(8,128)(2,1)}, u32[]{:S(2)}) copy-start(bf16[27,32,256]{2,1,0:T(8,128)(2,1)} %get-tuple-element.13) | copy-start | bytes 1327108
  28.0 0.7 copy-start.2
  30.2 33.8 %all-to-all-start.1 = ((f32[16,56,256]{2,1,0:T(8,128)}), f32[16,56,256]{2,1,0:T(8,128)S(1)}, u32[]{:S(2)}, u32[]{:S(2)}) async-start(f32[16,56,256]{2,1,0:T(8,128)} %bitcast.5), calls=%async_computation.1 | async-start | bytes 1835008 | tf_op jit(solution)/shard_map/all_to_all | solution.py:31
  53.2 56.1 %collective-permute-start = (f32[64,1024]{1,0:T(8,128)S(1)}, f32[64,1024]{1,0:T(8,128)S(1)}, u32[]{:S(2)}, u32[]{:S(2)}) collective-permute-start(f32[64,1024]{1,0:T(8,128)S(1)} %get-tuple-element.15), channel_id=1, source_target_pairs={{0,8},{8,16},{16,24},{24,32},{32,40},{40,48},{48,56},{56,64},{64,7... | collective-permute-start | bytes 786440 | tf_op jit(solution)/shard_map/ppermute | solution.py:325
  57.1 52.2 %collective-permute-start.1 = (f32[64,1024]{1,0:T(8,128)S(1)}, f32[64,1024]{1,0:T(8,128)S(1)}, u32[]{:S(2)}, u32[]{:S(2)}) collective-permute-start(f32[64,1024]{1,0:T(8,128)S(1)} %get-tuple-element.16), channel_id=1, source_target_pairs={{8,0},{16,8},{24,16},{32,24},{40,32},{48,40},{56,48},{64,56},{72,6... | collective-permute-start | bytes 786440 | tf_op jit(solution)/shard_map/ppermute | solution.py:326
  110.4 22.4 %all-to-all-start.2 = ((f32[16,56,256]{2,1,0:T(8,128)}), f32[16,56,256]{2,1,0:T(8,128)S(1)}, u32[]{:S(2)}, u32[]{:S(2)}) async-start(f32[16,56,256]{2,1,0:T(8,128)} %shard_map.64), calls=%async_computation.2 | async-start | bytes 1835008 | tf_op jit(solution)/shard_map/all_to_all | solution.py:31

commit v7 on v6

--- a/solution.py
+++ b/solution.py
@@ -39,7 +39,8 @@
     return pltpu.CompilerParams(vmem_limit_bytes=mib * 1024 * 1024)
 
 
-TOKEN = jax.ShapeDtypeStruct((8, 128), jnp.float32)
+TOKEN = jax.ShapeDtypeStruct((1,), jnp.int32)
+SMEM = pl.BlockSpec(memory_space=pltpu.SMEM)
 
 
 def own_weights(kernel, count):
@@ -48,7 +49,7 @@
     per = width // count
 
     def body(kernel_ref, fore, back, token, block, sems):
-        token[...] = jnp.zeros(token.shape, token.dtype)
+        token[0] = 0
         member = lax.axis_index("chan")
         lanes = pl.ds(pl.multiple_of((member // per) * width, width), width)
         rows = pl.ds(pl.multiple_of(member * count, count), count)
@@ -73,7 +74,7 @@
         body,
         out_shape=(shape, shape, TOKEN),
         in_specs=[HBM],
-        out_specs=(VMEM, VMEM, VMEM),
+        out_specs=(VMEM, VMEM, SMEM),
         scratch_shapes=[
             pltpu.VMEM((TAPS, channels, width), kernel.dtype),
             pltpu.SemaphoreType.DMA((2,)),
@@ -122,7 +123,7 @@
     return pl.pallas_call(
         body,
         out_shape=jax.ShapeDtypeStruct((rows, columns), pieces.dtype),
-        in_specs=[VMEM, VMEM],
+        in_specs=[VMEM, SMEM],
         out_specs=VMEM,
         compiler_params=limits(8),
         cost_estimate=pl.CostEstimate(
@@ -131,22 +132,56 @@
     )(pieces, after)
 
 
-def repeated(piece, copies, first, second):
-    def body(piece_ref, first_ref, second_ref, out, sems):
-        moves = [pltpu.make_async_copy(piece_ref, out.at[k], sems.at[k]) for k in range(copies)]
-        for move in moves:
-            move.start()
+TOP = 13.0
+SPARE = 8
+
+
+def scaled(piece, first, second):
+    rows, columns = piece.shape
+
+    def body(piece_ref, first_ref, second_ref, out):
+        value = piece_ref[...]
+        most = jnp.max(jnp.max(jnp.abs(value), axis=0, keepdims=True), axis=1, keepdims=True)
+        power = jnp.floor(jnp.log2(jnp.maximum(most, 1e-34)))
+        out[:rows, :] = value * jnp.exp2(TOP - power)
+        out[rows:, :] = jnp.broadcast_to(power, (SPARE, columns))
+
+    return pl.pallas_call(
+        body,
+        out_shape=jax.ShapeDtypeStruct((rows + SPARE, columns), piece.dtype),
+        in_specs=[VMEM, HBM, HBM],
+        out_specs=VMEM,
+        compiler_params=limits(32),
+    )(piece, first, second)
+
+
+def unscaled(pieces, amount):
+    count, height, columns = pieces.shape
+    rows = height - SPARE
+    spans = [(k * rows, min(rows, amount - k * rows)) for k in range(count) if k * rows < amount]
+
+    def body(pieces_ref, out, held, sems):
+        moves = []
+        for k, (start, size) in enumerate(spans):
+            power = pieces_ref[k, rows:, :][:1]
+            held[start : start + size, :] = pieces_ref[k, :size, :] * jnp.exp2(power - TOP)
+            span = pl.ds(start, size)
+            moves.append(pltpu.make_async_copy(held.at[span], out.at[span], sems.at[k]))
+            moves[-1].start()
         for move in moves:
             move.wait()
 
     return pl.pallas_call(
         body,
-        out_shape=jax.ShapeDtypeStruct((copies,) + piece.shape, piece.dtype),
-        in_specs=[VMEM, HBM, HBM],
+        out_shape=jax.ShapeDtypeStruct((amount, columns), pieces.dtype),
+        in_specs=[VMEM],
         out_specs=HBM,
-        scratch_shapes=[pltpu.SemaphoreType.DMA((copies,))],
+        scratch_shapes=[
+            pltpu.VMEM((amount, columns), pieces.dtype),
+            pltpu.SemaphoreType.DMA((len(spans),)),
+        ],
         compiler_params=limits(32),
-    )(piece, first, second)
+    )(pieces)
 
 
 def finish(own, low, high, height, breadth, dtype, after):
@@ -226,7 +261,7 @@
     return pl.pallas_call(
         body,
         out_shape=jax.ShapeDtypeStruct((rows, channels), jnp.float32),
-        in_specs=[VMEM] * 5,
+        in_specs=[VMEM] * 4 + [SMEM],
         out_specs=HBM,
         scratch_shapes=[
             pltpu.VMEM((9 * count, cells + 2 * breadth), own.dtype),
@@ -272,7 +307,7 @@
     cells = vol.shape[1]
 
     def body(fore_ref, vol_ref, back_ref, cot_ref, own, up, down, token):
-        token[...] = jnp.zeros(token.shape, token.dtype)
+        token[0] = 0
         halves = [pl.ds(0, count), pl.ds(count, count)]
         conv_terms(
             fore_ref, vol_ref, False, height, breadth, *(r.at[halves[0]] for r in (own, up, down))
@@ -286,7 +321,7 @@
         body,
         out_shape=(shape, shape, shape, TOKEN),
         in_specs=[VMEM] * 4,
-        out_specs=(VMEM,) * 4,
+        out_specs=(VMEM, VMEM, VMEM, SMEM),
         compiler_params=limits(12),
         cost_estimate=pl.CostEstimate(
             flops=4 * fore.size * cells,
@@ -324,9 +359,10 @@
     total = lax.psum(sum_pieces(pieces, done), "space", axis_index_groups=far_z)
     from_low = lax.ppermute(upper, "space", up)
     from_high = lax.ppermute(lower, "space", down)
-    copies = repeated(total, len(block[0]), from_low, from_high)
-    whole = exchange(copies, "space", block).reshape(-1, channels)
-    weight_grad = whole[: TAPS * count].reshape(3, 3, 3, count, channels)
+    packed = scaled(total, from_low, from_high).astype(jnp.float16)
+    copies = jnp.broadcast_to(packed[None], (len(block[0]),) + packed.shape)
+    whole = exchange(copies, "space", block).astype(jnp.float32)
+    weight_grad = unscaled(whole, TAPS * count).reshape(3, 3, 3, count, channels)
 
     output, input_grad = finish(own, from_low, from_high, height, breadth, volume.dtype, total)
     return (output.reshape(volume.shape), input_grad.reshape(volume.shape), weight_grad)

time: 134 us -> 129 us (0.963)
  waiting for transfers between devices: 25.2 us -> 19 us
  Pallas kernels: 9.71 us -> 11.3 us
    all_to_all x3, waiting for transfers between devices: 23.6 us -> 17.4 us  [exchange(): lax.all_to_all(pieces, axis, 0, 0, tiled=True, axis_index_groups=groups)]
  transfers between devices with their start and end apart: 7 -> 7, of which waited for: 4 -> 4; matrix products, arithmetic and copies ran while one was open for 1% -> 1% of each run, Pallas kernels for 4% -> 5%
where the time goes in v7:
time: 129 us
  blocking collectives  58.5 us (45%)
  starting transfers between devices  37.2 us (29%)
  waiting for transfers between devices  19 us (15%)
  Pallas kernels  11.3 us (9%)
  local copies, waits for them, and re-layouts  1.71 us (1%)
    psum x1, blocking collectives, local(): total = lax.psum(sum_pieces(pieces, done), 'space', axis_index_groups=far_z)  45.4 us
    all_to_all x3, starting transfers between devices, exchange(): lax.all_to_all(pieces, axis, 0, 0, tiled=True, axis_index_groups=groups)  29.5 us
    all_to_all x3, waiting for transfers between devices, exchange(): lax.all_to_all(pieces, axis, 0, 0, tiled=True, axis_index_groups=groups)  17.4 us
    all_gather x1, blocking collectives, local(): vol_all = lax.all_gather(vol, 'chan', axis=0, tiled=True)  13.1 us
    ppermute x1, starting transfers between devices, local(): from_low = lax.ppermute(upper, 'space', up)  3.83 us
    pallas_call x1, Pallas kernels, own_weights(): pl.pallas_call(body, out_shape=(shape, shape, TOKEN), in_specs=[HBM], out...  3.22 us
  transfers between devices with their start and end apart: 7, of which 4 were waited for; matrix products, arithmetic and copies ran while one was open for 1% of the time, Pallas kernels for 5%

profile of v7, /device:TPU:2, one launch (start us, length us, event | category | flops | bytes accessed | tf_op | source)
XLA Modules:
  0.0 128.6 jit_solution(13846857869146560449)
XLA Ops:
  0.6 1.8 %shard_map.59 = bf16[8,32,1024]{2,1,0:T(8,128)(2,1)} custom-call(bf16[32,8,128]{2,1,0:T(8,128)(2,1)} %bitcast.28), custom_call_target="tpu_custom_call" | custom-call | tf_op jit(solution)/shard_map/pallas_call | solution.py:100
  2.5 16.6 %all-to-all-start = ((bf16[8,32,1024]{2,1,0:T(8,128)(2,1)}), bf16[8,32,1024]{2,1,0:T(8,128)(2,1)S(1)}, u32[]{:S(2)}, u32[]{:S(2)}) async-start(bf16[8,32,1024]{2,1,0:T(8,128)(2,1)} %shard_map.59), calls=%async_computation | async-start | bytes 1048576 | tf_op jit(solution)/shard_map/all_to_all | solution.py:31
  19.1 0.8 copy.10
  19.9 1.3 %collective-permute-start.2 = (bf16[32,1024]{1,0:T(8,128)(2,1)S(1)}, bf16[32,1024]{1,0:T(8,128)(2,1)S(1)}, u32[]{:S(2)}, u32[]{:S(2)}) collective-permute-start(bf16[32,1024]{1,0:T(8,128)(2,1)S(1)} %bitcast.20), channel_id=1, source_target_pairs={{0,8},{8,16},{16,24},{24,32},{32,40},{40,48},{48,56},{56,64},{64,7... | collective-permute-start | bytes 196616 | tf_op jit(solution)/shard_map/ppermute | solution.py:349
  21.2 1.3 %collective-permute-start.3 = (bf16[32,1024]{1,0:T(8,128)(2,1)S(1)}, bf16[32,1024]{1,0:T(8,128)(2,1)S(1)}, u32[]{:S(2)}, u32[]{:S(2)}) collective-permute-start(bf16[32,1024]{1,0:T(8,128)(2,1)S(1)} %bitcast.21), channel_id=1, source_target_pairs={{8,0},{16,8},{24,16},{32,24},{40,32},{48,40},{56,48},{64,56},{72,6... | collective-permute-start | bytes 196616 | tf_op jit(solution)/shard_map/ppermute | solution.py:350
  22.5 3.2 %shard_map.58 = (bf16[27,32,256]{2,1,0:T(8,128)(2,1)}, bf16[27,32,256]{2,1,0:T(8,128)(2,1)}, s32[1]{0:T(128)}) custom-call(bf16[27,256,256]{2,1,0:T(8,128)(2,1)} %bitcast.26), custom_call_target="tpu_custom_call" | custom-call | tf_op jit(solution)/shard_map/pallas_call | solution.py:73
  25.7 0.0 copy-start
  25.8 0.0 copy-start.1
  25.8 0.0 collective-permute-done.2.low_ref
  25.8 1.6 %collective-permute-done.3.high_ref = bf16[32,1024]{1,0:T(8,128)(2,1)S(1)} collective-permute-done((bf16[32,1024]{1,0:T(8,128)(2,1)S(1)}, bf16[32,1024]{1,0:T(8,128)(2,1)S(1)}, u32[]{:S(2)}, u32[]{:S(2)}) %collective-permute-start.3) | collective-permute-done | bytes 65568 | tf_op jit(solution)/shard_map/ppermute | solution.py:350
  27.4 0.6 all-to-all-done
  28.0 2.2 %shard_map.61 = f32[896,256]{1,0:T(8,128)} custom-call(bf16[32,1024]{1,0:T(8,128)(2,1)S(1)} %collective-permute-done.2.low_ref, bf16[32,1024]{1,0:T(8,128)(2,1)S(1)} %bitcast.22, bf16[32,1024]{1,0:T(8,128)(2,1)S(1)} %collective-permute-done.3.high_ref, bf16[256,1024]{1,0:T(8,128)(2,1)S(1)} %bitcast.18, s32[1]{0:T(128)} %get-tuple-element.17.after_ref), custom_call_target="tpu_custom_call" | custom-call | flops 469762048 | bytes 917504 | tf_op jit(solution)/shard_map/pallas_call | solution.py:261
  30.2 8.7 %all-to-all-start.1 = ((f32[16,56,256]{2,1,0:T(8,128)}), f32[16,56,256]{2,1,0:T(8,128)S(1)}, u32[]{:S(2)}, u32[]{:S(2)}) async-start(f32[16,56,256]{2,1,0:T(8,128)} %bitcast.5), calls=%async_computation.1 | async-start | bytes 1835008 | tf_op jit(solution)/shard_map/all_to_all | solution.py:31
  38.9 13.1 %all_gather.3.vol_ref = bf16[256,1024]{1,0:T(8,128)(2,1)S(1)} all-gather(bf16[32,1024]{1,0:T(8,128)(2,1)S(1)} %bitcast.23), channel_id=1, replica_groups=mesh['space'=128,'chan'=8] {'chan'}, dimensions={0}, use_global_device_ids=true | all-gather | bytes 589824 | tf_op jit(solution)/shard_map/all_gather | solution.py:357
  52.0 0.0 copy-done
  52.0 0.0 copy-done.1
  52.0 1.4 %shard_map.60 = (f32[64,1024]{1,0:T(8,128)S(1)}, f32[64,1024]{1,0:T(8,128)S(1)}, f32[64,1024]{1,0:T(8,128)S(1)}, s32[1]{0:T(128)}) custom-call(bf16[3,288,256]{2,1,0:T(8,128)(2,1)S(1)} %bitcast.24, bf16[256,1024]{1,0:T(8,128)(2,1)S(1)} %all_gather.3.vol_ref, bf16[3,288,256]{2,1,0:T(8,128)(2,1)S(1)} %bitcast.25, bf16[256,1024]{1,0:T(8,128)(2,1)S(1)} %bitcast.19), custom_call_target="tpu_custom_call" | custom-call | flops 905969664 | bytes 1671168 | tf_op jit(solution)/shard_map/pallas_call | solution.py:320
  53.4 3.8 %collective-permute-start = (f32[64,1024]{1,0:T(8,128)S(1)}, f32[64,1024]{1,0:T(8,128)S(1)}, u32[]{:S(2)}, u32[]{:S(2)}) collective-permute-start(f32[64,1024]{1,0:T(8,128)S(1)} %get-tuple-element.15), channel_id=1, source_target_pairs={{0,8},{8,16},{16,24},{24,32},{32,40},{40,48},{48,56},{56,64},{64,7... | collective-permute-start | bytes 786440 | tf_op jit(solution)/shard_map/ppermute | solution.py:360
  57.2 1.3 %collective-permute-start.1 = (f32[64,1024]{1,0:T(8,128)S(1)}, f32[64,1024]{1,0:T(8,128)S(1)}, u32[]{:S(2)}, u32[]{:S(2)}) collective-permute-start(f32[64,1024]{1,0:T(8,128)S(1)} %get-tuple-element.16), channel_id=1, source_target_pairs={{8,0},{16,8},{24,16},{32,24},{40,32},{48,40},{56,48},{64,56},{72,6... | collective-permute-start | bytes 786440 | tf_op jit(solution)/shard_map/ppermute | solution.py:361
  58.5 5.4 %all-to-all-done.1.pieces_ref = f32[16,56,256]{2,1,0:T(8,128)S(1)} async-done(((f32[16,56,256]{2,1,0:T(8,128)}), f32[16,56,256]{2,1,0:T(8,128)S(1)}, u32[]{:S(2)}, u32[]{:S(2)}) %all-to-all-start.1) | async-done | bytes 917536 | tf_op jit(solution)/shard_map/all_to_all | solution.py:31
  63.9 0.7 shard_map.62
  64.6 45.4 %psum.7.after_ref.piece_ref = f32[56,256]{1,0:T(8,128)S(1)} all-reduce(f32[56,256]{1,0:T(8,128)S(1)} %shard_map.62), channel_id=1, replica_groups={{0,32,64,96,128,160,192,224},{8,40,72,104,136,168,200,232},{16,48,80,11..., use_global_device_ids=true, to_apply=%region_0.0 | all-reduce | flops 14336 | bytes 114688 | tf_op jit(solution)/shard_map/psum | solution.py:359
  110.0 0.0 collective-permute-done.low_ref.first_ref
  110.0 0.0 collective-permute-done.1.high_ref.second_ref
  110.0 0.1 shard_map.64
  110.1 0.8 broadcast_in_dim.2
  111.0 4.2 %all-to-all-start.2 = ((f16[16,64,256]{2,1,0:T(8,128)(2,1)}), f16[16,64,256]{2,1,0:T(8,128)(2,1)S(1)}, u32[]{:S(2)}, u32[]{:S(2)}) async-start(f16[16,64,256]{2,1,0:T(8,128)(2,1)} %broadcast_in_dim.2), calls=%async_computation.2 | async-start | bytes 1048576 | tf_op jit(solution)/shard_map/all_to_all | solution.py:31
  115.2 0.9 shard_map.63
  116.0 11.4 %all-to-all-done.2 = f16[16,64,256]{2,1,0:T(8,128)(2,1)S(1)} async-done(((f16[16,64,256]{2,1,0:T(8,128)(2,1)}), f16[16,64,256]{2,1,0:T(8,128)(2,1)S(1)}, u32[]{:S(2)}, u32[]{:S(2)}) %all-to-all-start.2) | async-done | bytes 524320 | tf_op jit(solution)/shard_map/all_to_all | solution.py:31
  127.5 0.1 convert_element_type.7.pieces_ref
  127.6 1.0 shard_map.65
  (1 shorter events, 0.0 us)
Async XLA Ops:
  2.5 25.5 %all-to-all-start = ((bf16[8,32,1024]{2,1,0:T(8,128)(2,1)}), bf16[8,32,1024]{2,1,0:T(8,128)(2,1)S(1)}, u32[]{:S(2)}, u32[]{:S(2)}) async-start(bf16[8,32,1024]{2,1,0:T(8,128)(2,1)} %shard_map.59), calls=%async_computation | async-start | bytes 1048576 | tf_op jit(solution)/shard_map/all_to_all | solution.py:31
  19.9 5.9 %collective-permute-start.2 = (bf16[32,1024]{1,0:T(8,128)(2,1)S(1)}, bf16[32,1024]{1,0:T(8,128)(2,1)S(1)}, u32[]{:S(2)}, u32[]{:S(2)}) collective-permute-start(bf16[32,1024]{1,0:T(8,128)(2,1)S(1)} %bitcast.20), channel_id=1, source_target_pairs={{0,8},{8,16},{16,24},{24,32},{32,40},{40,48},{48,56},{56,64},{64,7... | collective-permute-start | bytes 196616 | tf_op jit(solution)/shard_map/ppermute | solution.py:349
  21.2 6.2 %collective-permute-start.3 = (bf16[32,1024]{1,0:T(8,128)(2,1)S(1)}, bf16[32,1024]{1,0:T(8,128)(2,1)S(1)}, u32[]{:S(2)}, u32[]{:S(2)}) collective-permute-start(bf16[32,1024]{1,0:T(8,128)(2,1)S(1)} %bitcast.21), channel_id=1, source_target_pairs={{8,0},{16,8},{24,16},{32,24},{40,32},{48,40},{56,48},{64,56},{72,6... | collective-permute-start | bytes 196616 | tf_op jit(solution)/shard_map/ppermute | solution.py:350
  25.7 26.3 %copy-start = (bf16[27,32,256]{2,1,0:T(8,128)(2,1)S(1)}, bf16[27,32,256]{2,1,0:T(8,128)(2,1)}, u32[]{:S(2)}) copy-start(bf16[27,32,256]{2,1,0:T(8,128)(2,1)} %get-tuple-element.12) | copy-start | bytes 1327108
  25.8 26.3 %copy-start.1 = (bf16[27,32,256]{2,1,0:T(8,128)(2,1)S(1)}, bf16[27,32,256]{2,1,0:T(8,128)(2,1)}, u32[]{:S(2)}) copy-start(bf16[27,32,256]{2,1,0:T(8,128)(2,1)} %get-tuple-element.13) | copy-start | bytes 1327108
  30.2 33.7 %all-to-all-start.1 = ((f32[16,56,256]{2,1,0:T(8,128)}), f32[16,56,256]{2,1,0:T(8,128)S(1)}, u32[]{:S(2)}, u32[]{:S(2)}) async-start(f32[16,56,256]{2,1,0:T(8,128)} %bitcast.5), calls=%async_computation.1 | async-start | bytes 1835008 | tf_op jit(solution)/shard_map/all_to_all | solution.py:31
  53.4 56.6 %collective-permute-start = (f32[64,1024]{1,0:T(8,128)S(1)}, f32[64,1024]{1,0:T(8,128)S(1)}, u32[]{:S(2)}, u32[]{:S(2)}) collective-permute-start(f32[64,1024]{1,0:T(8,128)S(1)} %get-tuple-element.15), channel_id=1, source_target_pairs={{0,8},{8,16},{16,24},{24,32},{32,40},{40,48},{48,56},{56,64},{64,7... | collective-permute-start | bytes 786440 | tf_op jit(solution)/shard_map/ppermute | solution.py:360
  57.2 52.8 %collective-permute-start.1 = (f32[64,1024]{1,0:T(8,128)S(1)}, f32[64,1024]{1,0:T(8,128)S(1)}, u32[]{:S(2)}, u32[]{:S(2)}) collective-permute-start(f32[64,1024]{1,0:T(8,128)S(1)} %get-tuple-element.16), channel_id=1, source_target_pairs={{8,0},{16,8},{24,16},{32,24},{40,32},{48,40},{56,48},{64,56},{72,6... | collective-permute-start | bytes 786440 | tf_op jit(solution)/shard_map/ppermute | solution.py:361
  111.0 16.5 %all-to-all-start.2 = ((f16[16,64,256]{2,1,0:T(8,128)(2,1)}), f16[16,64,256]{2,1,0:T(8,128)(2,1)S(1)}, u32[]{:S(2)}, u32[]{:S(2)}) async-start(f16[16,64,256]{2,1,0:T(8,128)(2,1)} %broadcast_in_dim.2), calls=%async_computation.2 | async-start | bytes 1048576 | tf_op jit(solution)/shard_map/all_to_all | solution.py:31

commit v8 on v7

--- a/solution.py
+++ b/solution.py
@@ -136,11 +136,13 @@
 SPARE = 8
 
 
-def scaled(piece, first, second):
-    rows, columns = piece.shape
-
-    def body(piece_ref, first_ref, second_ref, out):
-        value = piece_ref[...]
+def scaled(pieces, first, second):
+    count, rows, columns = pieces.shape
+
+    def body(pieces_ref, first_ref, second_ref, out):
+        value = pieces_ref[0]
+        for k in range(1, count):
+            value = value + pieces_ref[k]
         most = jnp.max(jnp.max(jnp.abs(value), axis=0, keepdims=True), axis=1, keepdims=True)
         power = jnp.floor(jnp.log2(jnp.maximum(most, 1e-34)))
         out[:rows, :] = value * jnp.exp2(TOP - power)
@@ -148,11 +150,11 @@
 
     return pl.pallas_call(
         body,
-        out_shape=jax.ShapeDtypeStruct((rows + SPARE, columns), piece.dtype),
+        out_shape=jax.ShapeDtypeStruct((rows + SPARE, columns), pieces.dtype),
         in_specs=[VMEM, HBM, HBM],
         out_specs=VMEM,
         compiler_params=limits(32),
-    )(piece, first, second)
+    )(pieces, first, second)
 
 
 def unscaled(pieces, amount):
@@ -356,15 +358,16 @@
     pieces = exchange(terms.reshape(len(block[0]), -1, channels), "space", block)
     vol_all = lax.all_gather(vol, "chan", axis=0, tiled=True)
     own, upper, lower, done = plane_terms(fore, vol_all, back, cot_all, height, breadth)
-    total = lax.psum(sum_pieces(pieces, done), "space", axis_index_groups=far_z)
+    near = sum_pieces(pieces, done)
+    far = lax.all_gather(near, "space", axis=0, axis_index_groups=far_z)
     from_low = lax.ppermute(upper, "space", up)
     from_high = lax.ppermute(lower, "space", down)
-    packed = scaled(total, from_low, from_high).astype(jnp.float16)
+    packed = scaled(far, from_low, from_high).astype(jnp.float16)
     copies = jnp.broadcast_to(packed[None], (len(block[0]),) + packed.shape)
     whole = exchange(copies, "space", block).astype(jnp.float32)
     weight_grad = unscaled(whole, TAPS * count).reshape(3, 3, 3, count, channels)
 
-    output, input_grad = finish(own, from_low, from_high, height, breadth, volume.dtype, total)
+    output, input_grad = finish(own, from_low, from_high, height, breadth, volume.dtype, far)
     return (output.reshape(volume.shape), input_grad.reshape(volume.shape), weight_grad)
 
 

time: 129 us -> 128 us (level)
  blocking collectives: 58.5 us -> 56.4 us
    psum x1 -> x0, blocking collectives: 45.4 us -> none  [local(): total = lax.psum(sum_pieces(pieces, done), 'space', axis_index_groups=far_z)]
    all_gather x0 -> x1, blocking collectives: none -> 43.3 us  [local(): far = lax.all_gather(near, 'space', axis=0, axis_index_groups=far_z)]
where the time goes in v8:
time: 128 us; the launch traced here: 127 us
  blocking collectives  56.4 us (44%)
  starting transfers between devices  38 us (30%)
  waiting for transfers between devices  19 us (15%)
  Pallas kernels  11.3 us (9%)
  local copies, waits for them, and re-layouts  1.71 us (1%)
    all_gather x1, blocking collectives, local(): far = lax.all_gather(near, 'space', axis=0, axis_index_groups=far_z)  43.3 us
    all_to_all x3, starting transfers between devices, exchange(): lax.all_to_all(pieces, axis, 0, 0, tiled=True, axis_index_groups=groups)  30.3 us
    all_to_all x3, waiting for transfers between devices, exchange(): lax.all_to_all(pieces, axis, 0, 0, tiled=True, axis_index_groups=groups)  17.4 us
    all_gather x1, blocking collectives, local(): vol_all = lax.all_gather(vol, 'chan', axis=0, tiled=True)  13.1 us
    ppermute x1, starting transfers between devices, local(): from_low = lax.ppermute(upper, 'space', up)  3.83 us
    pallas_call x1, Pallas kernels, own_weights(): pl.pallas_call(body, out_shape=(shape, shape, TOKEN), in_specs=[HBM], out...  3.21 us
  transfers between devices with their start and end apart: 7, of which 4 were waited for; matrix products, arithmetic and copies ran while one was open for 1% of the time, Pallas kernels for 5%

profile of v8, /device:TPU:2, one launch (start us, length us, event | category | flops | bytes accessed | tf_op | source)
XLA Modules:
  0.0 127.4 jit_solution(13687862064241024477)
XLA Ops:
  0.6 1.8 %shard_map.59 = bf16[8,32,1024]{2,1,0:T(8,128)(2,1)} custom-call(bf16[32,8,128]{2,1,0:T(8,128)(2,1)} %bitcast.31), custom_call_target="tpu_custom_call" | custom-call | tf_op jit(solution)/shard_map/pallas_call | solution.py:100
  2.5 16.6 %all-to-all-start = ((bf16[8,32,1024]{2,1,0:T(8,128)(2,1)}), bf16[8,32,1024]{2,1,0:T(8,128)(2,1)S(1)}, u32[]{:S(2)}, u32[]{:S(2)}) async-start(bf16[8,32,1024]{2,1,0:T(8,128)(2,1)} %shard_map.59), calls=%async_computation | async-start | bytes 1048576 | tf_op jit(solution)/shard_map/all_to_all | solution.py:31
  19.1 0.8 copy.10
  19.9 1.3 %collective-permute-start.2 = (bf16[32,1024]{1,0:T(8,128)(2,1)S(1)}, bf16[32,1024]{1,0:T(8,128)(2,1)S(1)}, u32[]{:S(2)}, u32[]{:S(2)}) collective-permute-start(bf16[32,1024]{1,0:T(8,128)(2,1)S(1)} %bitcast.23), channel_id=1, source_target_pairs={{0,8},{8,16},{16,24},{24,32},{32,40},{40,48},{48,56},{56,64},{64,7... | collective-permute-start | bytes 196616 | tf_op jit(solution)/shard_map/ppermute | solution.py:351
  21.2 1.3 %collective-permute-start.3 = (bf16[32,1024]{1,0:T(8,128)(2,1)S(1)}, bf16[32,1024]{1,0:T(8,128)(2,1)S(1)}, u32[]{:S(2)}, u32[]{:S(2)}) collective-permute-start(bf16[32,1024]{1,0:T(8,128)(2,1)S(1)} %bitcast.24), channel_id=1, source_target_pairs={{8,0},{16,8},{24,16},{32,24},{40,32},{48,40},{56,48},{64,56},{72,6... | collective-permute-start | bytes 196616 | tf_op jit(solution)/shard_map/ppermute | solution.py:352
  22.5 3.2 %shard_map.58 = (bf16[27,32,256]{2,1,0:T(8,128)(2,1)}, bf16[27,32,256]{2,1,0:T(8,128)(2,1)}, s32[1]{0:T(128)}) custom-call(bf16[27,256,256]{2,1,0:T(8,128)(2,1)} %bitcast.29), custom_call_target="tpu_custom_call" | custom-call | tf_op jit(solution)/shard_map/pallas_call | solution.py:73
  25.7 0.0 copy-start
  25.8 0.0 copy-start.1
  25.8 0.0 collective-permute-done.2.low_ref
  25.8 1.6 %collective-permute-done.3.high_ref = bf16[32,1024]{1,0:T(8,128)(2,1)S(1)} collective-permute-done((bf16[32,1024]{1,0:T(8,128)(2,1)S(1)}, bf16[32,1024]{1,0:T(8,128)(2,1)S(1)}, u32[]{:S(2)}, u32[]{:S(2)}) %collective-permute-start.3) | collective-permute-done | bytes 65568 | tf_op jit(solution)/shard_map/ppermute | solution.py:352
  27.4 0.6 all-to-all-done
  28.0 2.2 %shard_map.61 = f32[896,256]{1,0:T(8,128)} custom-call(bf16[32,1024]{1,0:T(8,128)(2,1)S(1)} %collective-permute-done.2.low_ref, bf16[32,1024]{1,0:T(8,128)(2,1)S(1)} %bitcast.25, bf16[32,1024]{1,0:T(8,128)(2,1)S(1)} %collective-permute-done.3.high_ref, bf16[256,1024]{1,0:T(8,128)(2,1)S(1)} %bitcast.21, s32[1]{0:T(128)} %get-tuple-element.17.after_ref), custom_call_target="tpu_custom_call" | custom-call | flops 469762048 | bytes 917504 | tf_op jit(solution)/shard_map/pallas_call | solution.py:263
  30.2 8.7 %all-to-all-start.1 = ((f32[16,56,256]{2,1,0:T(8,128)}), f32[16,56,256]{2,1,0:T(8,128)S(1)}, u32[]{:S(2)}, u32[]{:S(2)}) async-start(f32[16,56,256]{2,1,0:T(8,128)} %bitcast.5), calls=%async_computation.1 | async-start | bytes 1835008 | tf_op jit(solution)/shard_map/all_to_all | solution.py:31
  38.9 13.1 %all_gather.9.vol_ref = bf16[256,1024]{1,0:T(8,128)(2,1)S(1)} all-gather(bf16[32,1024]{1,0:T(8,128)(2,1)S(1)} %bitcast.26), channel_id=1, replica_groups=mesh['space'=128,'chan'=8] {'chan'}, dimensions={0}, use_global_device_ids=true | all-gather | bytes 589824 | tf_op jit(solution)/shard_map/all_gather | solution.py:359
  52.0 0.0 copy-done
  52.0 0.0 copy-done.1
  52.0 1.4 %shard_map.60 = (f32[64,1024]{1,0:T(8,128)S(1)}, f32[64,1024]{1,0:T(8,128)S(1)}, f32[64,1024]{1,0:T(8,128)S(1)}, s32[1]{0:T(128)}) custom-call(bf16[3,288,256]{2,1,0:T(8,128)(2,1)S(1)} %bitcast.27, bf16[256,1024]{1,0:T(8,128)(2,1)S(1)} %all_gather.9.vol_ref, bf16[3,288,256]{2,1,0:T(8,128)(2,1)S(1)} %bitcast.28, bf16[256,1024]{1,0:T(8,128)(2,1)S(1)} %bitcast.22), custom_call_target="tpu_custom_call" | custom-call | flops 905969664 | bytes 1671168 | tf_op jit(solution)/shard_map/pallas_call | solution.py:322
  53.4 3.8 %collective-permute-start = (f32[64,1024]{1,0:T(8,128)S(1)}, f32[64,1024]{1,0:T(8,128)S(1)}, u32[]{:S(2)}, u32[]{:S(2)}) collective-permute-start(f32[64,1024]{1,0:T(8,128)S(1)} %get-tuple-element.15), channel_id=1, source_target_pairs={{0,8},{8,16},{16,24},{24,32},{32,40},{40,48},{48,56},{56,64},{64,7... | collective-permute-start | bytes 786440 | tf_op jit(solution)/shard_map/ppermute | solution.py:363
  57.3 1.3 %collective-permute-start.1 = (f32[64,1024]{1,0:T(8,128)S(1)}, f32[64,1024]{1,0:T(8,128)S(1)}, u32[]{:S(2)}, u32[]{:S(2)}) collective-permute-start(f32[64,1024]{1,0:T(8,128)S(1)} %get-tuple-element.16), channel_id=1, source_target_pairs={{8,0},{16,8},{24,16},{32,24},{40,32},{48,40},{56,48},{64,56},{72,6... | collective-permute-start | bytes 786440 | tf_op jit(solution)/shard_map/ppermute | solution.py:364
  58.6 5.4 %all-to-all-done.1.pieces_ref = f32[16,56,256]{2,1,0:T(8,128)S(1)} async-done(((f32[16,56,256]{2,1,0:T(8,128)}), f32[16,56,256]{2,1,0:T(8,128)S(1)}, u32[]{:S(2)}, u32[]{:S(2)}) %all-to-all-start.1) | async-done | bytes 917536 | tf_op jit(solution)/shard_map/all_to_all | solution.py:31
  63.9 0.7 shard_map.62
  64.6 43.3 %all-gather = f32[448,256]{1,0:T(8,128)S(1)} all-gather(f32[56,256]{1,0:T(8,128)S(1)} %shard_map.62), channel_id=2, replica_groups={{0,32,64,96,128,160,192,224},{8,40,72,104,136,168,200,232},{16,48,80,11..., dimensions={0}, use_global_device_ids=true | all-gather | bytes 516096 | tf_op jit(solution)/shard_map/all_gather | solution.py:362
  107.9 0.0 collective-permute-done.low_ref.first_ref
  107.9 0.0 collective-permute-done.1.high_ref.second_ref
  107.9 0.1 shard_map.64
  108.1 0.8 broadcast_in_dim.2
  108.9 5.0 %all-to-all-start.2 = ((f16[16,64,256]{2,1,0:T(8,128)(2,1)}), f16[16,64,256]{2,1,0:T(8,128)(2,1)S(1)}, u32[]{:S(2)}, u32[]{:S(2)}) async-start(f16[16,64,256]{2,1,0:T(8,128)(2,1)} %broadcast_in_dim.2), calls=%async_computation.2 | async-start | bytes 1048576 | tf_op jit(solution)/shard_map/all_to_all | solution.py:31
  113.9 0.9 shard_map.63
  114.8 11.4 %all-to-all-done.2 = f16[16,64,256]{2,1,0:T(8,128)(2,1)S(1)} async-done(((f16[16,64,256]{2,1,0:T(8,128)(2,1)}), f16[16,64,256]{2,1,0:T(8,128)(2,1)S(1)}, u32[]{:S(2)}, u32[]{:S(2)}) %all-to-all-start.2) | async-done | bytes 524320 | tf_op jit(solution)/shard_map/all_to_all | solution.py:31
  126.2 0.1 convert_element_type.7.pieces_ref
  126.3 1.0 shard_map.65
  (1 shorter events, 0.0 us)
Async XLA Ops:
  2.5 25.5 %all-to-all-start = ((bf16[8,32,1024]{2,1,0:T(8,128)(2,1)}), bf16[8,32,1024]{2,1,0:T(8,128)(2,1)S(1)}, u32[]{:S(2)}, u32[]{:S(2)}) async-start(bf16[8,32,1024]{2,1,0:T(8,128)(2,1)} %shard_map.59), calls=%async_computation | async-start | bytes 1048576 | tf_op jit(solution)/shard_map/all_to_all | solution.py:31
  19.9 5.8 %collective-permute-start.2 = (bf16[32,1024]{1,0:T(8,128)(2,1)S(1)}, bf16[32,1024]{1,0:T(8,128)(2,1)S(1)}, u32[]{:S(2)}, u32[]{:S(2)}) collective-permute-start(bf16[32,1024]{1,0:T(8,128)(2,1)S(1)} %bitcast.23), channel_id=1, source_target_pairs={{0,8},{8,16},{16,24},{24,32},{32,40},{40,48},{48,56},{56,64},{64,7... | collective-permute-start | bytes 196616 | tf_op jit(solution)/shard_map/ppermute | solution.py:351
  21.2 6.2 %collective-permute-start.3 = (bf16[32,1024]{1,0:T(8,128)(2,1)S(1)}, bf16[32,1024]{1,0:T(8,128)(2,1)S(1)}, u32[]{:S(2)}, u32[]{:S(2)}) collective-permute-start(bf16[32,1024]{1,0:T(8,128)(2,1)S(1)} %bitcast.24), channel_id=1, source_target_pairs={{8,0},{16,8},{24,16},{32,24},{40,32},{48,40},{56,48},{64,56},{72,6... | collective-permute-start | bytes 196616 | tf_op jit(solution)/shard_map/ppermute | solution.py:352
  25.7 26.3 %copy-start = (bf16[27,32,256]{2,1,0:T(8,128)(2,1)S(1)}, bf16[27,32,256]{2,1,0:T(8,128)(2,1)}, u32[]{:S(2)}) copy-start(bf16[27,32,256]{2,1,0:T(8,128)(2,1)} %get-tuple-element.12) | copy-start | bytes 1327108
  25.8 26.3 %copy-start.1 = (bf16[27,32,256]{2,1,0:T(8,128)(2,1)S(1)}, bf16[27,32,256]{2,1,0:T(8,128)(2,1)}, u32[]{:S(2)}) copy-start(bf16[27,32,256]{2,1,0:T(8,128)(2,1)} %get-tuple-element.13) | copy-start | bytes 1327108
  30.2 33.7 %all-to-all-start.1 = ((f32[16,56,256]{2,1,0:T(8,128)}), f32[16,56,256]{2,1,0:T(8,128)S(1)}, u32[]{:S(2)}, u32[]{:S(2)}) async-start(f32[16,56,256]{2,1,0:T(8,128)} %bitcast.5), calls=%async_computation.1 | async-start | bytes 1835008 | tf_op jit(solution)/shard_map/all_to_all | solution.py:31
  53.4 54.5 %collective-permute-start = (f32[64,1024]{1,0:T(8,128)S(1)}, f32[64,1024]{1,0:T(8,128)S(1)}, u32[]{:S(2)}, u32[]{:S(2)}) collective-permute-start(f32[64,1024]{1,0:T(8,128)S(1)} %get-tuple-element.15), channel_id=1, source_target_pairs={{0,8},{8,16},{16,24},{24,32},{32,40},{40,48},{48,56},{56,64},{64,7... | collective-permute-start | bytes 786440 | tf_op jit(solution)/shard_map/ppermute | solution.py:363
  57.3 50.7 %collective-permute-start.1 = (f32[64,1024]{1,0:T(8,128)S(1)}, f32[64,1024]{1,0:T(8,128)S(1)}, u32[]{:S(2)}, u32[]{:S(2)}) collective-permute-start(f32[64,1024]{1,0:T(8,128)S(1)} %get-tuple-element.16), channel_id=1, source_target_pairs={{8,0},{16,8},{24,16},{32,24},{40,32},{48,40},{56,48},{64,56},{72,6... | collective-permute-start | bytes 786440 | tf_op jit(solution)/shard_map/ppermute | solution.py:364
  108.9 17.3 %all-to-all-start.2 = ((f16[16,64,256]{2,1,0:T(8,128)(2,1)}), f16[16,64,256]{2,1,0:T(8,128)(2,1)S(1)}, u32[]{:S(2)}, u32[]{:S(2)}) async-start(f16[16,64,256]{2,1,0:T(8,128)(2,1)} %broadcast_in_dim.2), calls=%async_computation.2 | async-start | bytes 1048576 | tf_op jit(solution)/shard_map/all_to_all | solution.py:31

commit v9 on v8

--- a/solution.py
+++ b/solution.py
@@ -15,6 +15,8 @@
 def groups_of(count):
     length = count // Y_CHIPS
     far = length // NEAR
+    along_y = [[y * length + z for y in range(Y_CHIPS)] for z in range(length)]
+    near_z = [[hop * NEAR + k for k in range(NEAR)] for hop in range(count // NEAR)]
     block = [
         [y * length + hop * NEAR + k for y in range(Y_CHIPS) for k in range(NEAR)]
         for hop in range(far)
@@ -24,7 +26,7 @@
         for y in range(Y_CHIPS)
         for k in range(NEAR)
     ]
-    return block, far_z
+    return along_y, near_z, block, far_z
 
 
 def exchange(pieces, axis, groups=None):
@@ -123,7 +125,7 @@
     return pl.pallas_call(
         body,
         out_shape=jax.ShapeDtypeStruct((rows, columns), pieces.dtype),
-        in_specs=[VMEM, SMEM],
+        in_specs=[VMEM, pl.BlockSpec(memory_space=pl.ANY)],
         out_specs=VMEM,
         compiler_params=limits(8),
         cost_estimate=pl.CostEstimate(
@@ -341,7 +343,7 @@
     parts = lax.axis_size("chan")
     member = lax.axis_index("chan")
     factor = 1.0 / math.sqrt(slabs * planes * cells)
-    block, far_z = groups_of(slabs)
+    along_y, near_z, block, far_z = groups_of(slabs)
     up = [(i, i + 1) for i in range(slabs - 1)]
     down = [(i + 1, i) for i in range(slabs - 1)]
 
@@ -355,10 +357,11 @@
     back = back.reshape(3, 9 * count, channels)
 
     terms = weight_terms(vol_low, vol, vol_high, cot_all, ready, factor, height, breadth)
-    pieces = exchange(terms.reshape(len(block[0]), -1, channels), "space", block)
+    pieces = exchange(terms.reshape(len(along_y[0]), -1, channels), "space", along_y)
     vol_all = lax.all_gather(vol, "chan", axis=0, tiled=True)
     own, upper, lower, done = plane_terms(fore, vol_all, back, cot_all, height, breadth)
-    near = sum_pieces(pieces, done)
+    pieces = sum_pieces(pieces, vol_all).reshape(len(near_z[0]), -1, channels)
+    near = sum_pieces(exchange(pieces, "space", near_z), done)
     far = lax.all_gather(near, "space", axis=0, axis_index_groups=far_z)
     from_low = lax.ppermute(upper, "space", up)
     from_high = lax.ppermute(lower, "space", down)

time: 128 us -> 131 us (1.023)
  starting transfers between devices: 38 us -> 46.6 us
  waiting for transfers between devices: 19 us -> 13.3 us
    all_to_all x3 -> x4, starting transfers between devices: 30.3 us -> 35.6 us  [exchange(): lax.all_to_all(pieces, axis, 0, 0, tiled=True, axis_index_groups=groups)]
    all_to_all x3 -> x4, waiting for transfers between devices: 17.4 us -> 13.3 us  [exchange(): lax.all_to_all(pieces, axis, 0, 0, tiled=True, axis_index_groups=groups)]
    ppermute x1, starting transfers between devices: 1.29 us -> 4.55 us  [local(): vol_low = lax.ppermute(vol, 'space', up)]
    ppermute x1, waiting for transfers between devices: 1.61 us -> 0.01 us  [local(): vol_high = lax.ppermute(vol, 'space', down)]
  transfers between devices with their start and end apart: 7 -> 8, of which waited for: 4 -> 2; matrix products, arithmetic and copies ran while one was open for 1% -> 1% of each run, Pallas kernels for 5% -> 5%
where the time goes in v9:
time: 131 us
  blocking collectives  55.5 us (42%)
  starting transfers between devices  46.6 us (36%)
  waiting for transfers between devices  13.3 us (10%)
  Pallas kernels  12.6 us (10%)
  local copies, waits for them, and re-layouts  1.71 us (1%)
    all_gather x1, blocking collectives, local(): far = lax.all_gather(near, 'space', axis=0, axis_index_groups=far_z)  42.4 us
    all_to_all x4, starting transfers between devices, exchange(): lax.all_to_all(pieces, axis, 0, 0, tiled=True, axis_index_groups=groups)  35.6 us
    all_to_all x4, waiting for transfers between devices, exchange(): lax.all_to_all(pieces, axis, 0, 0, tiled=True, axis_index_groups=groups)  13.3 us
    all_gather x1, blocking collectives, local(): vol_all = lax.all_gather(vol, 'chan', axis=0, tiled=True)  13.1 us
    ppermute x1, starting transfers between devices, local(): vol_low = lax.ppermute(vol, 'space', up)  4.55 us
    ppermute x1, starting transfers between devices, local(): from_low = lax.ppermute(upper, 'space', up)  3.89 us
    pallas_call x1, Pallas kernels, own_weights(): pl.pallas_call(body, out_shape=(shape, shape, TOKEN), in_specs=[HBM], out...  3.24 us
  transfers between devices with their start and end apart: 8, of which 2 were waited for; matrix products, arithmetic and copies ran while one was open for 1% of the time, Pallas kernels for 5%

profile of v9, /device:TPU:2, one launch (start us, length us, event | category | flops | bytes accessed | tf_op | source)
XLA Modules:
  0.0 130.7 jit_solution(16673042049173028988)
XLA Ops:
  0.6 1.8 %shard_map.59 = bf16[8,32,1024]{2,1,0:T(8,128)(2,1)} custom-call(bf16[32,8,128]{2,1,0:T(8,128)(2,1)} %bitcast.32), custom_call_target="tpu_custom_call" | custom-call | tf_op jit(solution)/shard_map/pallas_call | solution.py:102
  2.5 16.6 %all-to-all-start = ((bf16[8,32,1024]{2,1,0:T(8,128)(2,1)}), bf16[8,32,1024]{2,1,0:T(8,128)(2,1)S(1)}, u32[]{:S(2)}, u32[]{:S(2)}) async-start(bf16[8,32,1024]{2,1,0:T(8,128)(2,1)} %shard_map.59), calls=%async_computation | async-start | bytes 1048576 | tf_op jit(solution)/shard_map/all_to_all | solution.py:33
  19.1 0.8 copy.10
  19.9 1.3 collective-permute-start.3
  21.2 4.5 %collective-permute-start.2 = (bf16[32,1024]{1,0:T(8,128)(2,1)S(1)}, bf16[32,1024]{1,0:T(8,128)(2,1)S(1)}, u32[]{:S(2)}, u32[]{:S(2)}) collective-permute-start(bf16[32,1024]{1,0:T(8,128)(2,1)S(1)} %bitcast.25), channel_id=1, source_target_pairs={{0,8},{8,16},{16,24},{24,32},{32,40},{40,48},{48,56},{56,64},{64,7... | collective-permute-start | bytes 196616 | tf_op jit(solution)/shard_map/ppermute | solution.py:353
  25.8 3.2 %shard_map.58 = (bf16[27,32,256]{2,1,0:T(8,128)(2,1)}, bf16[27,32,256]{2,1,0:T(8,128)(2,1)}, s32[1]{0:T(128)}) custom-call(bf16[27,256,256]{2,1,0:T(8,128)(2,1)} %bitcast.30), custom_call_target="tpu_custom_call" | custom-call | tf_op jit(solution)/shard_map/pallas_call | solution.py:75
  29.0 0.0 copy-start
  29.0 0.0 copy-start.1
  29.0 0.0 collective-permute-done.3.high_ref
  29.1 0.0 collective-permute-done.2.low_ref
  29.1 0.0 all-to-all-done
  29.1 2.3 %shard_map.61 = f32[896,256]{1,0:T(8,128)} custom-call(bf16[32,1024]{1,0:T(8,128)(2,1)S(1)} %collective-permute-done.2.low_ref, bf16[32,1024]{1,0:T(8,128)(2,1)S(1)} %bitcast.26, bf16[32,1024]{1,0:T(8,128)(2,1)S(1)} %collective-permute-done.3.high_ref, bf16[256,1024]{1,0:T(8,128)(2,1)S(1)} %bitcast.22, s32[1]{0:T(128)} %get-tuple-element.17.after_ref), custom_call_target="tpu_custom_call" | custom-call | flops 469762048 | bytes 917504 | tf_op jit(solution)/shard_map/pallas_call | solution.py:265
  31.4 10.5 %all-to-all-start.1 = ((f32[4,224,256]{2,1,0:T(8,128)}), f32[4,224,256]{2,1,0:T(8,128)S(1)}, u32[]{:S(2)}, u32[]{:S(2)}) async-start(f32[4,224,256]{2,1,0:T(8,128)} %bitcast.5), calls=%async_computation.1 | async-start | bytes 1835008 | tf_op jit(solution)/shard_map/all_to_all | solution.py:33
  41.8 13.1 %all_gather.9.vol_ref.after_ref = bf16[256,1024]{1,0:T(8,128)(2,1)S(1)} all-gather(bf16[32,1024]{1,0:T(8,128)(2,1)S(1)} %bitcast.27), channel_id=1, replica_groups=mesh['space'=128,'chan'=8] {'chan'}, dimensions={0}, use_global_device_ids=true | all-gather | bytes 589824 | tf_op jit(solution)/shard_map/all_gather | solution.py:361
  54.9 0.0 all-to-all-done.1.pieces_ref
  54.9 0.7 shard_map.62
  55.6 3.4 %all-to-all-start.2 = ((f32[4,56,256]{2,1,0:T(8,128)}), f32[4,56,256]{2,1,0:T(8,128)S(1)}, u32[]{:S(2)}, u32[]{:S(2)}) async-start(f32[4,56,256]{2,1,0:T(8,128)} %bitcast.6), calls=%async_computation.2 | async-start | bytes 458752 | tf_op jit(solution)/shard_map/all_to_all | solution.py:33
  59.0 0.0 copy-done
  59.1 0.0 copy-done.1
  59.1 1.9 %shard_map.60 = (f32[64,1024]{1,0:T(8,128)S(1)}, f32[64,1024]{1,0:T(8,128)}, f32[64,1024]{1,0:T(8,128)S(1)}, s32[1]{0:T(128)}) custom-call(bf16[3,288,256]{2,1,0:T(8,128)(2,1)S(1)} %bitcast.28, bf16[256,1024]{1,0:T(8,128)(2,1)S(1)} %all_gather.9.vol_ref.after_ref, bf16[3,288,256]{2,1,0:T(8,128)(2,1)S(1)} %bitcast.29, bf16[256,1024]{1,0:T(8,128)(2,1)S(1)} %bitcast.23), custom_call_target="tpu_custom_call" | custom-call | flops 905969664 | bytes 1671168 | tf_op jit(solution)/shard_map/pallas_call | solution.py:324
  61.0 3.9 %collective-permute-start = (f32[64,1024]{1,0:T(8,128)}, f32[64,1024]{1,0:T(8,128)S(1)}, u32[]{:S(2)}, u32[]{:S(2)}) collective-permute-start(f32[64,1024]{1,0:T(8,128)} %get-tuple-element.15), channel_id=1, source_target_pairs={{0,8},{8,16},{16,24},{24,32},{32,40},{40,48},{48,56},{56,64},{64,7... | collective-permute-start | bytes 786440 | tf_op jit(solution)/shard_map/ppermute | solution.py:366
  64.8 1.3 collective-permute-start.1
  66.1 1.8 %all-to-all-done.2.pieces_ref = f32[4,56,256]{2,1,0:T(8,128)S(1)} async-done(((f32[4,56,256]{2,1,0:T(8,128)}), f32[4,56,256]{2,1,0:T(8,128)S(1)}, u32[]{:S(2)}, u32[]{:S(2)}) %all-to-all-start.2) | async-done | bytes 229408 | tf_op jit(solution)/shard_map/all_to_all | solution.py:33
  68.0 0.7 shard_map.63
  68.6 42.4 %all-gather = f32[448,256]{1,0:T(8,128)S(1)} all-gather(f32[56,256]{1,0:T(8,128)S(1)} %shard_map.63), channel_id=2, replica_groups={{0,32,64,96,128,160,192,224},{8,40,72,104,136,168,200,232},{16,48,80,11..., dimensions={0}, use_global_device_ids=true | all-gather | bytes 516096 | tf_op jit(solution)/shard_map/all_gather | solution.py:365
  111.1 0.0 collective-permute-done.low_ref.first_ref
  111.1 0.0 collective-permute-done.1.high_ref.second_ref
  111.1 0.1 shard_map.65
  111.2 0.8 broadcast_in_dim.2
  112.1 5.2 %all-to-all-start.3 = ((f16[16,64,256]{2,1,0:T(8,128)(2,1)}), f16[16,64,256]{2,1,0:T(8,128)(2,1)S(1)}, u32[]{:S(2)}, u32[]{:S(2)}) async-start(f16[16,64,256]{2,1,0:T(8,128)(2,1)} %broadcast_in_dim.2), calls=%async_computation.3 | async-start | bytes 1048576 | tf_op jit(solution)/shard_map/all_to_all | solution.py:33
  117.2 0.9 shard_map.64
  118.1 11.4 %all-to-all-done.3 = f16[16,64,256]{2,1,0:T(8,128)(2,1)S(1)} async-done(((f16[16,64,256]{2,1,0:T(8,128)(2,1)}), f16[16,64,256]{2,1,0:T(8,128)(2,1)S(1)}, u32[]{:S(2)}, u32[]{:S(2)}) %all-to-all-start.3) | async-done | bytes 524320 | tf_op jit(solution)/shard_map/all_to_all | solution.py:33
  129.5 0.1 convert_element_type.7.pieces_ref
  129.6 1.0 shard_map.66
  (1 shorter events, 0.0 us)
Async XLA Ops:
  2.5 26.6 %all-to-all-start = ((bf16[8,32,1024]{2,1,0:T(8,128)(2,1)}), bf16[8,32,1024]{2,1,0:T(8,128)(2,1)S(1)}, u32[]{:S(2)}, u32[]{:S(2)}) async-start(bf16[8,32,1024]{2,1,0:T(8,128)(2,1)} %shard_map.59), calls=%async_computation | async-start | bytes 1048576 | tf_op jit(solution)/shard_map/all_to_all | solution.py:33
  19.9 9.1 %collective-permute-start.3 = (bf16[32,1024]{1,0:T(8,128)(2,1)S(1)}, bf16[32,1024]{1,0:T(8,128)(2,1)S(1)}, u32[]{:S(2)}, u32[]{:S(2)}) collective-permute-start(bf16[32,1024]{1,0:T(8,128)(2,1)S(1)} %bitcast.24), channel_id=1, source_target_pairs={{8,0},{16,8},{24,16},{32,24},{40,32},{48,40},{56,48},{64,56},{72,6... | collective-permute-start | bytes 196616 | tf_op jit(solution)/shard_map/ppermute | solution.py:354
  21.2 7.8 %collective-permute-start.2 = (bf16[32,1024]{1,0:T(8,128)(2,1)S(1)}, bf16[32,1024]{1,0:T(8,128)(2,1)S(1)}, u32[]{:S(2)}, u32[]{:S(2)}) collective-permute-start(bf16[32,1024]{1,0:T(8,128)(2,1)S(1)} %bitcast.25), channel_id=1, source_target_pairs={{0,8},{8,16},{16,24},{24,32},{32,40},{40,48},{48,56},{56,64},{64,7... | collective-permute-start | bytes 196616 | tf_op jit(solution)/shard_map/ppermute | solution.py:353
  29.0 30.0 %copy-start = (bf16[27,32,256]{2,1,0:T(8,128)(2,1)S(1)}, bf16[27,32,256]{2,1,0:T(8,128)(2,1)}, u32[]{:S(2)}) copy-start(bf16[27,32,256]{2,1,0:T(8,128)(2,1)} %get-tuple-element.12) | copy-start | bytes 1327108
  29.0 30.0 %copy-start.1 = (bf16[27,32,256]{2,1,0:T(8,128)(2,1)S(1)}, bf16[27,32,256]{2,1,0:T(8,128)(2,1)}, u32[]{:S(2)}) copy-start(bf16[27,32,256]{2,1,0:T(8,128)(2,1)} %get-tuple-element.13) | copy-start | bytes 1327108
  31.4 23.5 %all-to-all-start.1 = ((f32[4,224,256]{2,1,0:T(8,128)}), f32[4,224,256]{2,1,0:T(8,128)S(1)}, u32[]{:S(2)}, u32[]{:S(2)}) async-start(f32[4,224,256]{2,1,0:T(8,128)} %bitcast.5), calls=%async_computation.1 | async-start | bytes 1835008 | tf_op jit(solution)/shard_map/all_to_all | solution.py:33
  55.6 12.3 %all-to-all-start.2 = ((f32[4,56,256]{2,1,0:T(8,128)}), f32[4,56,256]{2,1,0:T(8,128)S(1)}, u32[]{:S(2)}, u32[]{:S(2)}) async-start(f32[4,56,256]{2,1,0:T(8,128)} %bitcast.6), calls=%async_computation.2 | async-start | bytes 458752 | tf_op jit(solution)/shard_map/all_to_all | solution.py:33
  61.0 50.1 %collective-permute-start = (f32[64,1024]{1,0:T(8,128)}, f32[64,1024]{1,0:T(8,128)S(1)}, u32[]{:S(2)}, u32[]{:S(2)}) collective-permute-start(f32[64,1024]{1,0:T(8,128)} %get-tuple-element.15), channel_id=1, source_target_pairs={{0,8},{8,16},{16,24},{24,32},{32,40},{40,48},{48,56},{56,64},{64,7... | collective-permute-start | bytes 786440 | tf_op jit(solution)/shard_map/ppermute | solution.py:366
  64.8 46.2 %collective-permute-start.1 = (f32[64,1024]{1,0:T(8,128)S(1)}, f32[64,1024]{1,0:T(8,128)S(1)}, u32[]{:S(2)}, u32[]{:S(2)}) collective-permute-start(f32[64,1024]{1,0:T(8,128)S(1)} %get-tuple-element.16), channel_id=1, source_target_pairs={{8,0},{16,8},{24,16},{32,24},{40,32},{48,40},{56,48},{64,56},{72,6... | collective-permute-start | bytes 786440 | tf_op jit(solution)/shard_map/ppermute | solution.py:367
  112.1 17.5 %all-to-all-start.3 = ((f16[16,64,256]{2,1,0:T(8,128)(2,1)}), f16[16,64,256]{2,1,0:T(8,128)(2,1)S(1)}, u32[]{:S(2)}, u32[]{:S(2)}) async-start(f16[16,64,256]{2,1,0:T(8,128)(2,1)} %broadcast_in_dim.2), calls=%async_computation.3 | async-start | bytes 1048576 | tf_op jit(solution)/shard_map/all_to_all | solution.py:33

commit v10 on v8

--- a/solution.py
+++ b/solution.py
@@ -136,10 +136,10 @@
 SPARE = 8
 
 
-def scaled(pieces, first, second):
+def scaled(pieces):
     count, rows, columns = pieces.shape
 
-    def body(pieces_ref, first_ref, second_ref, out):
+    def body(pieces_ref, out):
         value = pieces_ref[0]
         for k in range(1, count):
             value = value + pieces_ref[k]
@@ -151,10 +151,10 @@
     return pl.pallas_call(
         body,
         out_shape=jax.ShapeDtypeStruct((rows + SPARE, columns), pieces.dtype),
-        in_specs=[VMEM, HBM, HBM],
+        in_specs=[VMEM],
         out_specs=VMEM,
         compiler_params=limits(32),
-    )(pieces, first, second)
+    )(pieces)
 
 
 def unscaled(pieces, amount):
@@ -362,7 +362,7 @@
     far = lax.all_gather(near, "space", axis=0, axis_index_groups=far_z)
     from_low = lax.ppermute(upper, "space", up)
     from_high = lax.ppermute(lower, "space", down)
-    packed = scaled(far, from_low, from_high).astype(jnp.float16)
+    packed = scaled(far).astype(jnp.float16)
     copies = jnp.broadcast_to(packed[None], (len(block[0]),) + packed.shape)
     whole = exchange(copies, "space", block).astype(jnp.float32)
     weight_grad = unscaled(whole, TAPS * count).reshape(3, 3, 3, count, channels)

time: 128 us -> 128 us (level)
  the two profiles are of different devices: /device:TPU:2 before, /device:TPU:32 now
where the time goes in v10:
time: 128 us
  blocking collectives  57.4 us (45%)
  starting transfers between devices  41.6 us (32%)
  waiting for transfers between devices  14.8 us (12%)
  Pallas kernels  11.4 us (9%)
  local copies, waits for them, and re-layouts  1.71 us (1%)
    all_gather x1, blocking collectives, local(): far = lax.all_gather(near, 'space', axis=0, axis_index_groups=far_z)  43.5 us
    all_to_all x3, starting transfers between devices, exchange(): lax.all_to_all(pieces, axis, 0, 0, tiled=True, axis_index_groups=groups)  20.6 us
    all_gather x1, blocking collectives, local(): vol_all = lax.all_gather(vol, 'chan', axis=0, tiled=True)  13.9 us
    ppermute x1, starting transfers between devices, local(): vol_high = lax.ppermute(vol, 'space', down)  11.3 us
    ppermute x1, waiting for transfers between devices, local(): from_low = lax.ppermute(upper, 'space', up)  6.38 us
    all_to_all x3, waiting for transfers between devices, exchange(): lax.all_to_all(pieces, axis, 0, 0, tiled=True, axis_index_groups=groups)  6.24 us
    ppermute x1, starting transfers between devices, local(): vol_low = lax.ppermute(vol, 'space', up)  3.83 us
    ppermute x1, starting transfers between devices, local(): from_low = lax.ppermute(upper, 'space', up)  3.36 us
  transfers between devices with their start and end apart: 7, of which 3 were waited for; matrix products, arithmetic and copies ran while one was open for 1% of the time, Pallas kernels for 4%

profile of v10, /device:TPU:32, one launch (start us, length us, event | category | flops | bytes accessed | tf_op | source)
XLA Modules:
  0.0 127.8 jit_solution(2007445478680178058)
XLA Ops:
  0.6 1.8 %shard_map.59 = bf16[8,32,1024]{2,1,0:T(8,128)(2,1)} custom-call(bf16[32,8,128]{2,1,0:T(8,128)(2,1)} %bitcast.31), custom_call_target="tpu_custom_call" | custom-call | tf_op jit(solution)/shard_map/pallas_call | solution.py:100
  2.5 4.3 %all-to-all-start = ((bf16[8,32,1024]{2,1,0:T(8,128)(2,1)}), bf16[8,32,1024]{2,1,0:T(8,128)(2,1)S(1)}, u32[]{:S(2)}, u32[]{:S(2)}) async-start(bf16[8,32,1024]{2,1,0:T(8,128)(2,1)} %shard_map.59), calls=%async_computation | async-start | bytes 1048576 | tf_op jit(solution)/shard_map/all_to_all | solution.py:31
  6.8 0.8 copy.10
  7.6 3.8 %collective-permute-start.2 = (bf16[32,1024]{1,0:T(8,128)(2,1)S(1)}, bf16[32,1024]{1,0:T(8,128)(2,1)S(1)}, u32[]{:S(2)}, u32[]{:S(2)}) collective-permute-start(bf16[32,1024]{1,0:T(8,128)(2,1)S(1)} %bitcast.23), channel_id=1, source_target_pairs={{0,8},{8,16},{16,24},{24,32},{32,40},{40,48},{48,56},{56,64},{64,7... | collective-permute-start | bytes 196616 | tf_op jit(solution)/shard_map/ppermute | solution.py:351
  11.5 11.3 %collective-permute-start.3 = (bf16[32,1024]{1,0:T(8,128)(2,1)S(1)}, bf16[32,1024]{1,0:T(8,128)(2,1)S(1)}, u32[]{:S(2)}, u32[]{:S(2)}) collective-permute-start(bf16[32,1024]{1,0:T(8,128)(2,1)S(1)} %bitcast.24), channel_id=1, source_target_pairs={{8,0},{16,8},{24,16},{32,24},{40,32},{48,40},{56,48},{64,56},{72,6... | collective-permute-start | bytes 196616 | tf_op jit(solution)/shard_map/ppermute | solution.py:352
  22.8 3.2 %shard_map.58 = (bf16[27,32,256]{2,1,0:T(8,128)(2,1)}, bf16[27,32,256]{2,1,0:T(8,128)(2,1)}, s32[1]{0:T(128)}) custom-call(bf16[27,256,256]{2,1,0:T(8,128)(2,1)} %bitcast.29), custom_call_target="tpu_custom_call" | custom-call | tf_op jit(solution)/shard_map/pallas_call | solution.py:73
  26.0 0.0 copy-start
  26.0 0.0 copy-start.1
  26.1 0.0 collective-permute-done.2.low_ref
  26.1 0.0 collective-permute-done.3.high_ref
  26.1 0.0 all-to-all-done
  26.1 2.3 %shard_map.61 = f32[896,256]{1,0:T(8,128)} custom-call(bf16[32,1024]{1,0:T(8,128)(2,1)S(1)} %collective-permute-done.2.low_ref, bf16[32,1024]{1,0:T(8,128)(2,1)S(1)} %bitcast.25, bf16[32,1024]{1,0:T(8,128)(2,1)S(1)} %collective-permute-done.3.high_ref, bf16[256,1024]{1,0:T(8,128)(2,1)S(1)} %bitcast.21, s32[1]{0:T(128)} %get-tuple-element.17.after_ref), custom_call_target="tpu_custom_call" | custom-call | flops 469762048 | bytes 917504 | tf_op jit(solution)/shard_map/pallas_call | solution.py:263
  28.4 10.0 %all-to-all-start.1 = ((f32[16,56,256]{2,1,0:T(8,128)}), f32[16,56,256]{2,1,0:T(8,128)S(1)}, u32[]{:S(2)}, u32[]{:S(2)}) async-start(f32[16,56,256]{2,1,0:T(8,128)} %bitcast.5), calls=%async_computation.1 | async-start | bytes 1835008 | tf_op jit(solution)/shard_map/all_to_all | solution.py:31
  38.4 13.9 %all_gather.9.vol_ref = bf16[256,1024]{1,0:T(8,128)(2,1)S(1)} all-gather(bf16[32,1024]{1,0:T(8,128)(2,1)S(1)} %bitcast.26), channel_id=1, replica_groups=mesh['space'=128,'chan'=8] {'chan'}, dimensions={0}, use_global_device_ids=true | all-gather | bytes 589824 | tf_op jit(solution)/shard_map/all_gather | solution.py:359
  52.3 0.0 copy-done
  52.3 0.0 copy-done.1
  52.3 1.4 %shard_map.60 = (f32[64,1024]{1,0:T(8,128)S(1)}, f32[64,1024]{1,0:T(8,128)S(1)}, f32[64,1024]{1,0:T(8,128)S(1)}, s32[1]{0:T(128)}) custom-call(bf16[3,288,256]{2,1,0:T(8,128)(2,1)S(1)} %bitcast.27, bf16[256,1024]{1,0:T(8,128)(2,1)S(1)} %all_gather.9.vol_ref, bf16[3,288,256]{2,1,0:T(8,128)(2,1)S(1)} %bitcast.28, bf16[256,1024]{1,0:T(8,128)(2,1)S(1)} %bitcast.22), custom_call_target="tpu_custom_call" | custom-call | flops 905969664 | bytes 1671168 | tf_op jit(solution)/shard_map/pallas_call | solution.py:322
  53.7 6.2 %all-to-all-done.1.pieces_ref = f32[16,56,256]{2,1,0:T(8,128)S(1)} async-done(((f32[16,56,256]{2,1,0:T(8,128)}), f32[16,56,256]{2,1,0:T(8,128)S(1)}, u32[]{:S(2)}, u32[]{:S(2)}) %all-to-all-start.1) | async-done | bytes 917536 | tf_op jit(solution)/shard_map/all_to_all | solution.py:31
  60.0 0.7 shard_map.62
  60.7 43.5 %all-gather = f32[448,256]{1,0:T(8,128)S(1)} all-gather(f32[56,256]{1,0:T(8,128)S(1)} %shard_map.62), channel_id=2, replica_groups={{0,32,64,96,128,160,192,224},{8,40,72,104,136,168,200,232},{16,48,80,11..., dimensions={0}, use_global_device_ids=true | all-gather | bytes 516096 | tf_op jit(solution)/shard_map/all_gather | solution.py:362
  104.1 0.1 shard_map.64
  104.3 0.8 broadcast_in_dim.2
  105.1 6.3 %all-to-all-start.2 = ((f16[16,64,256]{2,1,0:T(8,128)(2,1)}), f16[16,64,256]{2,1,0:T(8,128)(2,1)S(1)}, u32[]{:S(2)}, u32[]{:S(2)}) async-start(f16[16,64,256]{2,1,0:T(8,128)(2,1)} %broadcast_in_dim.2), calls=%async_computation.2 | async-start | bytes 1048576 | tf_op jit(solution)/shard_map/all_to_all | solution.py:31
  111.4 3.4 %collective-permute-start = (f32[64,1024]{1,0:T(8,128)S(1)}, f32[64,1024]{1,0:T(8,128)S(1)}, u32[]{:S(2)}, u32[]{:S(2)}) collective-permute-start(f32[64,1024]{1,0:T(8,128)S(1)} %get-tuple-element.15), channel_id=1, source_target_pairs={{0,8},{8,16},{16,24},{24,32},{32,40},{40,48},{48,56},{56,64},{64,7... | collective-permute-start | bytes 786440 | tf_op jit(solution)/shard_map/ppermute | solution.py:363
  114.8 2.5 %collective-permute-start.1 = (f32[64,1024]{1,0:T(8,128)S(1)}, f32[64,1024]{1,0:T(8,128)S(1)}, u32[]{:S(2)}, u32[]{:S(2)}) collective-permute-start(f32[64,1024]{1,0:T(8,128)S(1)} %get-tuple-element.16), channel_id=1, source_target_pairs={{8,0},{16,8},{24,16},{32,24},{40,32},{48,40},{56,48},{64,56},{72,6... | collective-permute-start | bytes 786440 | tf_op jit(solution)/shard_map/ppermute | solution.py:364
  117.3 6.4 %collective-permute-done.low_ref = f32[64,1024]{1,0:T(8,128)S(1)} collective-permute-done((f32[64,1024]{1,0:T(8,128)S(1)}, f32[64,1024]{1,0:T(8,128)S(1)}, u32[]{:S(2)}, u32[]{:S(2)}) %collective-permute-start) | collective-permute-done | bytes 262176 | tf_op jit(solution)/shard_map/ppermute | solution.py:363
  123.6 2.1 %collective-permute-done.1.high_ref = f32[64,1024]{1,0:T(8,128)S(1)} collective-permute-done((f32[64,1024]{1,0:T(8,128)S(1)}, f32[64,1024]{1,0:T(8,128)S(1)}, u32[]{:S(2)}, u32[]{:S(2)}) %collective-permute-start.1) | collective-permute-done | bytes 262176 | tf_op jit(solution)/shard_map/ppermute | solution.py:364
  125.8 0.9 shard_map.63
  126.6 0.0 all-to-all-done.2
  126.6 0.1 convert_element_type.7.pieces_ref
  126.7 1.0 shard_map.65
  (1 shorter events, 0.0 us)
Async XLA Ops:
  2.5 23.6 %all-to-all-start = ((bf16[8,32,1024]{2,1,0:T(8,128)(2,1)}), bf16[8,32,1024]{2,1,0:T(8,128)(2,1)S(1)}, u32[]{:S(2)}, u32[]{:S(2)}) async-start(bf16[8,32,1024]{2,1,0:T(8,128)(2,1)} %shard_map.59), calls=%async_computation | async-start | bytes 1048576 | tf_op jit(solution)/shard_map/all_to_all | solution.py:31
  7.6 18.4 %collective-permute-start.2 = (bf16[32,1024]{1,0:T(8,128)(2,1)S(1)}, bf16[32,1024]{1,0:T(8,128)(2,1)S(1)}, u32[]{:S(2)}, u32[]{:S(2)}) collective-permute-start(bf16[32,1024]{1,0:T(8,128)(2,1)S(1)} %bitcast.23), channel_id=1, source_target_pairs={{0,8},{8,16},{16,24},{24,32},{32,40},{40,48},{48,56},{56,64},{64,7... | collective-permute-start | bytes 196616 | tf_op jit(solution)/shard_map/ppermute | solution.py:351
  11.5 14.6 %collective-permute-start.3 = (bf16[32,1024]{1,0:T(8,128)(2,1)S(1)}, bf16[32,1024]{1,0:T(8,128)(2,1)S(1)}, u32[]{:S(2)}, u32[]{:S(2)}) collective-permute-start(bf16[32,1024]{1,0:T(8,128)(2,1)S(1)} %bitcast.24), channel_id=1, source_target_pairs={{8,0},{16,8},{24,16},{32,24},{40,32},{48,40},{56,48},{64,56},{72,6... | collective-permute-start | bytes 196616 | tf_op jit(solution)/shard_map/ppermute | solution.py:352
  26.0 26.3 %copy-start = (bf16[27,32,256]{2,1,0:T(8,128)(2,1)S(1)}, bf16[27,32,256]{2,1,0:T(8,128)(2,1)}, u32[]{:S(2)}) copy-start(bf16[27,32,256]{2,1,0:T(8,128)(2,1)} %get-tuple-element.12) | copy-start | bytes 1327108
  26.0 26.3 %copy-start.1 = (bf16[27,32,256]{2,1,0:T(8,128)(2,1)S(1)}, bf16[27,32,256]{2,1,0:T(8,128)(2,1)}, u32[]{:S(2)}) copy-start(bf16[27,32,256]{2,1,0:T(8,128)(2,1)} %get-tuple-element.13) | copy-start | bytes 1327108
  28.4 31.6 %all-to-all-start.1 = ((f32[16,56,256]{2,1,0:T(8,128)}), f32[16,56,256]{2,1,0:T(8,128)S(1)}, u32[]{:S(2)}, u32[]{:S(2)}) async-start(f32[16,56,256]{2,1,0:T(8,128)} %bitcast.5), calls=%async_computation.1 | async-start | bytes 1835008 | tf_op jit(solution)/shard_map/all_to_all | solution.py:31
  105.1 21.5 %all-to-all-start.2 = ((f16[16,64,256]{2,1,0:T(8,128)(2,1)}), f16[16,64,256]{2,1,0:T(8,128)(2,1)S(1)}, u32[]{:S(2)}, u32[]{:S(2)}) async-start(f16[16,64,256]{2,1,0:T(8,128)(2,1)} %broadcast_in_dim.2), calls=%async_computation.2 | async-start | bytes 1048576 | tf_op jit(solution)/shard_map/all_to_all | solution.py:31
  111.4 12.2 %collective-permute-start = (f32[64,1024]{1,0:T(8,128)S(1)}, f32[64,1024]{1,0:T(8,128)S(1)}, u32[]{:S(2)}, u32[]{:S(2)}) collective-permute-start(f32[64,1024]{1,0:T(8,128)S(1)} %get-tuple-element.15), channel_id=1, source_target_pairs={{0,8},{8,16},{16,24},{24,32},{32,40},{40,48},{48,56},{56,64},{64,7... | collective-permute-start | bytes 786440 | tf_op jit(solution)/shard_map/ppermute | solution.py:363
  114.8 11.0 %collective-permute-start.1 = (f32[64,1024]{1,0:T(8,128)S(1)}, f32[64,1024]{1,0:T(8,128)S(1)}, u32[]{:S(2)}, u32[]{:S(2)}) collective-permute-start(f32[64,1024]{1,0:T(8,128)S(1)} %get-tuple-element.16), channel_id=1, source_target_pairs={{8,0},{16,8},{24,16},{32,24},{40,32},{48,40},{56,48},{64,56},{72,6... | collective-permute-start | bytes 786440 | tf_op jit(solution)/shard_map/ppermute | solution.py:364
